TPU v7x, 32 devices: a whole 2x2x4 slice. The times are simulated.
32 devices in a mesh: groups: 2 (over x), dp: 4 (over y, core), tensor: 4 (over z).
Axes of the slice: x: 2, y: 2, z: 4, core: 2. Of those that a mesh axis runs over, the one named last changes fastest.
Arguments:
- hidden: bfloat16 [4096, 8192], P(('groups', 'dp'), 'tensor'), parts along dimension 0, may hold values from -0.59765625 to 0.59765625
- query_gradient: bfloat16 [4096, 4096], P(('groups', 'dp'), 'tensor'), parts along dimension 0, may hold values from -6 to 6
- frozen_query_weight: bfloat16 [8192, 4096], P(None, 'tensor'), may hold values from -0.0625 to 0.0625
- adapter_down_weight: bfloat16 [16, 8192, 64], P(('groups', 'dp'), 'tensor'), parts along dimension 0, may hold values from -0.0625 to 0.0625
- adapter_up_weight: bfloat16 [16, 64, 4096], P(('groups', 'dp'), None, 'tensor'), parts along dimension 0, may hold values from -0.09375 to 0.09375
- block_member_owner: int32 [32], P('groups'), parts along dimension 0, may hold values from 0 to 7, as said below
- member_last_block_count: int32 [16], P('groups'), parts along dimension 0, may hold values from 1 to 128
Outputs:
- hidden_gradient: bfloat16 [4096, 8192], P(('groups', 'dp'), 'tensor'), parts along dimension 0
- grad_down: float32 [16, 8192, 64], P(('groups', 'dp'), 'tensor'), parts along dimension 0
- grad_up: float32 [16, 64, 4096], P(('groups', 'dp'), None, 'tensor'), parts along dimension 0
There are 2 independent parts, one for each index of `groups`. A program takes and returns all parts, laid end to end along the dimension named above; an argument that names none is the same for every part. Nothing has to cross between parts.
Inputs may be any that keep to these rules, and one draw needn't show every extreme that they name: `block_member_owner`: the blocks come in consecutive runs, one run for each member, in an order drawn from the seed; each run is 1 to 3 blocks long, and at least one run is exactly 3 blocks long.
All inputs are finite; a program needn't handle non-finite values.
Results may differ from a plain program's by a relative error of at most 0.015.
Values may be sent and summed in bfloat16 or wider, within the bound.
No kernel may reach another device: no remote copies, remote signals or barrier semaphores. Data moves between devices by JAX's collectives and lax.ppermute only.
A program may use at most 128 MiB of HBM per device.

v0:
```python
import jax
import jax.numpy as jnp
from jax import lax
from jax.sharding import PartitionSpec as P

BLK = 128


def live_mask(block_member_owner, member_last_block_count):
    following = jnp.concatenate([block_member_owner[1:], jnp.full((1,), -1, jnp.int32)])
    closing = block_member_owner != following
    tails = jnp.take(member_last_block_count, block_member_owner)
    places = jnp.arange(BLK, dtype=jnp.int32)
    return jnp.logical_or(jnp.logical_not(closing)[:, None], places[None, :] < tails[:, None])


def body(
    hidden,
    query_gradient,
    frozen_query_weight,
    adapter_down_weight,
    adapter_up_weight,
    block_member_owner,
    member_last_block_count,
):
    blocks_dev = hidden.shape[0] // BLK
    local_width = hidden.shape[1]
    cols_local = query_gradient.shape[1]
    owned_tokens = adapter_down_weight.shape[0]
    first = lax.axis_index("dp") * blocks_dev
    live = live_mask(block_member_owner, member_last_block_count)
    member_list = lax.dynamic_slice_in_dim(block_member_owner, first, blocks_dev)
    keep = lax.dynamic_slice_in_dim(live, first, blocks_dev).reshape(-1)
    cotan = jnp.where(keep[:, None], query_gradient, jnp.zeros_like(query_gradient))
    down_table, up_table = (
        lax.all_gather(adapter_down_weight, "dp", axis=0, tiled=True),
        lax.all_gather(adapter_up_weight, "dp", axis=0, tiled=True),
    )
    selected_down = jnp.take(down_table, member_list, axis=0)
    selected_up = jnp.take(up_table, member_list, axis=0)
    token_rows = hidden.reshape(blocks_dev, BLK, local_width)
    cotan_blocks = cotan.reshape(blocks_dev, BLK, cols_local)
    activation_piece = jnp.einsum(
        "nhx,nxs->nhs", token_rows, selected_down, preferred_element_type=jnp.float32
    )
    grad_part = jnp.einsum(
        "bkq,brq->bkr", cotan_blocks, selected_up, preferred_element_type=jnp.float32
    )
    rank_activation, rank_gradient = (
        lax.psum(activation_piece.astype(jnp.bfloat16), "tensor").astype(jnp.float32),
        lax.psum(grad_part.astype(jnp.bfloat16), "tensor").astype(jnp.float32),
    )
    rank_activation = rank_activation.astype(jnp.bfloat16)
    rank_gradient = rank_gradient.astype(jnp.bfloat16)
    term = lax.dot_general(
        cotan, frozen_query_weight, (((1,), (1,)), ((), ())), preferred_element_type=jnp.float32
    )
    frozen_term = lax.psum_scatter(
        term.astype(jnp.bfloat16), "tensor", scatter_dimension=1, tiled=True
    ).astype(jnp.float32)
    adapter_contribution = jnp.einsum(
        "jym,jim->jyi", rank_gradient, selected_down, preferred_element_type=jnp.float32
    )
    hidden_gradient = (frozen_term + adapter_contribution.reshape(-1, local_width)).astype(
        jnp.bfloat16
    )
    block_down_matrix = jnp.einsum(
        "uza,uzm->uam", token_rows, rank_gradient, preferred_element_type=jnp.float32
    )
    block_up = jnp.einsum(
        "bkr,bkq->brq", rank_activation, cotan_blocks, preferred_element_type=jnp.float32
    )
    member_ids = jnp.arange(down_table.shape[0], dtype=jnp.int32)
    onehot = (member_ids[:, None] == member_list[None, :]).astype(jnp.float32)
    share_down = jnp.einsum("mb,bdr->mdr", onehot, block_down_matrix)
    share_up = jnp.einsum("mb,brq->mrq", onehot, block_up)
    total_down, total_up = (
        lax.psum(share_down.astype(jnp.bfloat16), "dp").astype(jnp.float32),
        lax.psum(share_up.astype(jnp.bfloat16), "dp").astype(jnp.float32),
    )
    own_first = lax.axis_index("dp") * owned_tokens
    grad_down = lax.dynamic_slice_in_dim(total_down, own_first, owned_tokens, 0)
    grad_up = lax.dynamic_slice_in_dim(total_up, own_first, owned_tokens, 0)
    return (hidden_gradient, grad_down, grad_up)


def solution(mesh):
    placed = (
        P(("groups", "dp"), "tensor"),
        P(("groups", "dp"), "tensor"),
        P(None, "tensor"),
        P(("groups", "dp"), "tensor", None),
        P(("groups", "dp"), None, "tensor"),
        P("groups"),
        P("groups"),
    )
    return jax.shard_map(
        body,
        mesh=mesh,
        in_specs=placed,
        out_specs=(
            P(("groups", "dp"), "tensor"),
            P(("groups", "dp"), "tensor", None),
            P(("groups", "dp"), None, "tensor"),
        ),
        check_vma=False,
    )
```

profile of v0, /device:TPU:0, one launch (start us, length us, event | category | flops | bytes accessed | tf_op | source)
XLA Modules:
  0.0 324.1 jit_solution(16245673808483803480)
XLA Ops:
  7.2 0.7 all-gather.3.cloned.1.call-update
  8.0 0.7 all-gather.5.cloned.1.call-update
  8.7 0.7 slice.3
  9.4 0.7 compare_not_fusion
  10.2 0.1 dynamic-slice.1
  10.3 0.7 compare_select_fusion.1
  10.9 1.3 gather_fusion
  12.2 0.7 and_select_fusion
  12.9 0.1 dynamic-slice
  13.0 0.7 compare_and_fusion
  13.8 1.4 broadcast_select_fusion.1
  15.2 13.8 %all-gather.3.cloned.1.call-done = bf16[8,64,1024]{2,1,0:T(8,128)(2,1)} async-done(((bf16[2,64,1024]{2,1,0:T(8,128)(2,1)}), bf16[8,64,1024]{2,1,0:T(8,128)(2,1)}) %all-gather.3.cloned.1.call-update) | async-done | bytes 1048592 | tf_op jit(solution)/shard_map/all_gather | solution.py:37
  29.0 2.6 gather_fusion.1
  31.6 2.2 convolution_convert_fusion.4
  33.8 19.4 %all-gather.5.cloned.1.call-done = bf16[8,2048,64]{1,2,0:T(8,128)(2,1)} async-done(((bf16[2,2048,64]{1,2,0:T(8,128)(2,1)}), bf16[8,2048,64]{1,2,0:T(8,128)(2,1)}) %all-gather.5.cloned.1.call-update) | async-done | bytes 2097168 | tf_op jit(solution)/shard_map/all_gather | solution.py:36
  53.2 2.2 gather_fusion.2
  55.4 1.5 fusion.2
  57.0 34.7 %all-reduce.5.cloned.1.call-done = (bf16[4,128,64]{1,2,0:T(8,128)(2,1)}, bf16[4,128,64]{1,2,0:T(8,128)(2,1)}) async-done(((bf16[4,128,64]{1,2,0:T(8,128)(2,1)}, bf16[4,128,64]{1,2,0:T(8,128)(2,1)}), (bf16[4,128,64]{1,2,0:T(8,128)(2,1)}, bf16[4,128,64]{1,2,0:T(8,128)(2,1)})) %all-reduce.5.cloned.1.call-update) | async-done | bytes 131088 | tf_op jit(solution)/shard_map/psum | solution.py:51
  91.7 1.3 convolution_bitcast_fusion
  93.0 2.3 convolution_convert_fusion.1
  95.3 0.3 fusion.18
  95.6 1.6 convolution_convert_fusion.2
  97.3 14.7 %convolution_convert_fusion = bf16[512,8192]{1,0:T(8,128)(2,1)} fusion(bf16[512,1024]{1,0:T(8,128)(2,1)} %copy-done.1, bf16[8192,1024]{1,0:T(8,128)(2,1)} %param.9), kind=kOutput, calls=%fused_computation.3 | convolution fusion | flops 8594128896 | bytes 26214400 | tf_op jit(solution)/shard_map/dot_general | solution.py:55
  112.1 0.8 copy-done.3
  112.9 2.7 fusion.6
  115.7 50.1 %all-reduce.7.cloned.1.call-done = (bf16[8,2048,64]{1,0,2:T(8,128)(2,1)}, bf16[8,64,1024]{2,0,1:T(8,128)(2,1)}) async-done(((bf16[8,2048,64]{1,0,2:T(8,128)(2,1)}, bf16[8,64,1024]{2,0,1:T(8,128)(2,1)}), (bf16[8,2048,64]{1,0,2:T(8,128)(2,1)}, bf16[8,64,1024]{2,0,1:T(8,128)(2,1)})) %all-reduce.7.cloned.1.call-update) | async-done | bytes 3145744 | tf_op jit(solution)/shard_map/psum | solution.py:78
  165.8 2.2 dynamic-slice_convert_fusion
  168.0 1.6 copy.16
  169.5 1.4 dynamic-slice_convert_fusion.1
  171.0 1.0 copy.17
  171.9 140.7 %reduce-scatter.2.cloned.1.call-done = bf16[512,2048]{1,0:T(8,128)(2,1)} async-done(((bf16[512,8192]{1,0:T(8,128)(2,1)}), bf16[512,2048]{1,0:T(8,128)(2,1)}) %reduce-scatter.2.cloned.1.call-update) | async-done | bytes 2097168 | tf_op jit(solution)/shard_map/reduce_scatter | solution.py:58
  312.7 4.9 %fusion = bf16[512,2048]{1,0:T(8,128)(2,1)} fusion(f32[4,128,2048]{2,1,0:T(8,128)} %fusion.6, bf16[512,2048]{1,0:T(8,128)(2,1)} %reduce-scatter.2.cloned.1.call-done), kind=kLoop, calls=%fused_computation.5 | loop fusion | flops 3145728 | bytes 8388608 | tf_op jit(solution)/shard_map/convert_element_type | solution.py:64
  (21 shorter events, 0.4 us)
Async XLA Ops:
  7.2 48.3 %copy-start = (bf16[512,2048]{1,0:T(8,128)(2,1)S(1)}, bf16[512,2048]{1,0:T(8,128)(2,1)}, u32[]{:S(2)}) copy-start(bf16[512,2048]{1,0:T(8,128)(2,1)} %param.7) | copy-start | bytes 6291460
  7.2 21.9 %all-gather.3.cloned.1.call-start = ((), (), s32[]{:S(2)}) async-start(), calls=%async_computation.2 | async-start | bytes 1310720 | tf_op jit(solution)/shard_map/all_gather | solution.py:37
  7.9 45.3 %all-gather.5.cloned.1.call-start = ((), (), s32[]{:S(2)}) async-start(), calls=%async_computation.3 | async-start | bytes 2621440 | tf_op jit(solution)/shard_map/all_gather | solution.py:36
  8.7 83.0 %all-reduce.5.cloned.1.call-start = ((), (), s32[]{:S(2)}) async-start(), calls=%async_computation.4 | async-start | bytes 262144 | tf_op jit(solution)/shard_map/psum | solution.py:51
  15.2 18.6 %copy-start.1 = (bf16[512,1024]{1,0:T(8,128)(2,1)}, bf16[512,1024]{1,0:T(8,128)(2,1)S(1)}, u32[]{:S(2)}) copy-start(bf16[512,1024]{1,0:T(8,128)(2,1)S(1)} %broadcast_select_fusion.1) | copy-start | bytes 3145732
  57.0 108.8 %all-reduce.7.cloned.1.call-start = ((), (), s32[]{:S(2)}) async-start(), calls=%async_computation.5 | async-start | bytes 6291456 | tf_op jit(solution)/shard_map/psum | solution.py:78
  93.0 2.4 copy-start.2
  93.0 2.3 copy-start.4
  97.3 215.4 %reduce-scatter.2.cloned.1.call-start = ((), (), s32[]{:S(2)}) async-start(), calls=%async_computation.1 | async-start | bytes 10485760 | tf_op jit(solution)/shard_map/reduce_scatter | solution.py:58
  112.1 0.8 copy-start.3
Sparse Core Ops, SparseCore 0:
  9.6 19.4 all-gather.2
  30.6 22.5 all-gather.4
  57.1 34.5 all-reduce.4
  97.4 68.3 all-reduce.6
  168.1 144.5 reduce-scatter.1
where the time goes:
time: 325 us; the launch traced here: 324 us
  waiting for transfers between devices  260 us (80%)
  matrix products  26.7 us (8%)
  between operations  13.9 us (4%)
  other arithmetic  12.8 us (4%)
  local copies, waits for them, and re-layouts  10.4 us (3%)
    reduce_scatter x1, waiting for transfers between devices, body(): lax.psum_scatter(term.astype(jnp.bfloat16), 'tensor', scatter_dimension=1...  141 us
    psum x1, waiting for transfers between devices, body(): lax.psum(share_down.astype(jnp.bfloat16), 'dp').astype(jnp.float32)  50.1 us
    psum x1, waiting for transfers between devices, body(): lax.psum(grad_part.astype(jnp.bfloat16), 'tensor').astype(jnp.float32)  34.7 us
    all_gather x1, waiting for transfers between devices, body(): lax.all_gather(adapter_down_weight, 'dp', axis=0, tiled=True)  19.4 us
    dot_general x1, matrix products, body(): lax.dot_general(cotan, frozen_query_weight, (((1,), (1,)), ((), ())), pre...  14.7 us
    all_gather x1, waiting for transfers between devices, body(): lax.all_gather(adapter_up_weight, 'dp', axis=0, tiled=True)  13.8 us
  transfers between devices with their start and end apart: 5, of which 5 were waited for; matrix products, arithmetic and copies ran while one was open for 11% of the time, Pallas kernels for 0%

commit v1 on v0

v1 whole, which is shorter than its diff:
```python
import jax
import jax.numpy as jnp
from jax import lax
from jax.sharding import PartitionSpec as P

BLK = 128
BF = jnp.bfloat16
F32 = jnp.float32


def live_mask(owner, counts):
    following = jnp.concatenate([owner[1:], jnp.full((1,), -1, jnp.int32)])
    closing = owner != following
    tails = jnp.take(counts, owner)
    places = jnp.arange(BLK, dtype=jnp.int32)
    return jnp.logical_or(jnp.logical_not(closing)[:, None], places[None, :] < tails[:, None])


def swap(a, axis, size, bit):
    return lax.ppermute(a, axis, [(i, i ^ (1 << bit)) for i in range(size)])


def body(hidden, query_gradient, weight, down, up, owner, counts):
    n = lax.axis_size("tensor")
    nd = lax.axis_size("dp")
    ng = lax.axis_size("groups")
    z = lax.axis_index("tensor")
    me = lax.axis_index("dp")
    width = hidden.shape[1]
    cols = query_gradient.shape[1]
    tokens = hidden.shape[0]
    blocks = tokens // BLK
    owned = down.shape[0]
    rank = down.shape[2]
    share = width // (ng * nd)
    place = lax.axis_index("groups") * nd + me

    ups, downs = [], []
    a = b = query_gradient
    for r in range(1, n):
        a = lax.ppermute(a, "tensor", [(i, i + 1) for i in range(r - 1, n - 1)])
        b = lax.ppermute(b, "tensor", [(i, i - 1) for i in range(n - r, 0, -1)])
        ups.append(a)
        downs.append(b)
    wide = []
    for step in range(1, n):
        to = lax.rem(z + step, n)
        piece = lax.dynamic_slice(weight, (to * width + place * share, 0), (share, cols))
        piece = lax.ppermute(piece, "tensor", [(i, (i + step) % n) for i in range(n)])
        wide.append(lax.all_gather(piece, ("groups", "dp"), axis=0, tiled=True))

    bits = list(range(nd.bit_length() - 2, -1, -1))
    table = jnp.concatenate([jnp.swapaxes(down, 1, 2), up], axis=2)
    for bit in bits:
        table = jnp.concatenate([table, swap(table, "dp", nd, bit)], axis=0)
    first = me * blocks
    members = lax.dynamic_slice_in_dim(owner, first, blocks)
    keep = lax.dynamic_slice_in_dim(live_mask(owner, counts), first, blocks).reshape(-1)
    relative = (members // owned) ^ me
    slot = members % owned
    for j, bit in enumerate(bits):
        slot = slot + (((relative >> bit) & 1) << j) * owned
    chosen = jnp.take(table, slot, axis=0)
    chosen_down, chosen_up = chosen[:, :, :width], chosen[:, :, width:]

    hid = hidden.reshape(blocks, BLK, width)
    cot = query_gradient.reshape(blocks, BLK, cols)
    act = jnp.einsum("bth,brh->btr", hid, chosen_down, preferred_element_type=F32)
    grad = jnp.einsum("btq,brq->btr", cot, chosen_up, preferred_element_type=F32)
    both = jnp.concatenate([act, grad], axis=2).astype(BF)
    for bit in range(n.bit_length() - 1):
        both = (both.astype(F32) + swap(both, "tensor", n, bit).astype(F32)).astype(BF)
    both = jnp.where(keep.reshape(blocks, BLK, 1), both, jnp.zeros_like(both))
    rank_act, rank_grad = both[:, :, :rank], both[:, :, rank:]

    block_down = jnp.einsum("btr,bth->brh", rank_grad, hid, preferred_element_type=F32)
    block_up = jnp.einsum("btr,btq->brq", rank_act, cot, preferred_element_type=F32)
    onehot = (jnp.arange(nd * owned, dtype=jnp.int32)[:, None] == slot[None, :]).astype(F32)
    total = jnp.concatenate(
        [
            jnp.einsum("mb,brh->mrh", onehot, block_down),
            jnp.einsum("mb,brq->mrq", onehot, block_up),
        ],
        axis=2,
    ).astype(BF)
    for bit in reversed(bits):
        half = total.shape[0] // 2
        got = swap(total[half:], "dp", nd, bit)
        total = total[:half].astype(F32) + got.astype(F32)
        if bit != bits[0]:
            total = total.astype(BF)
    grad_down = jnp.swapaxes(total[:, :, :width], 1, 2)
    grad_up = total[:, :, width:]

    def dot(c, w):
        return lax.dot_general(c, w, (((1,), (1,)), ((), ())), preferred_element_type=F32)

    result = dot(query_gradient, lax.dynamic_slice_in_dim(weight, z * width, width, 0))
    for step in range(1, n):
        c = jnp.where(z >= step, ups[step - 1], downs[n - step - 1])
        result = result + dot(c, wide[step - 1])
    result = jnp.where(keep[:, None], result, 0.0)
    extra = jnp.einsum("btr,brh->bth", rank_grad, chosen_down, preferred_element_type=F32)
    result = result + extra.reshape(tokens, width)
    return result.astype(BF), grad_down, grad_up


def solution(mesh):
    return jax.shard_map(
        body,
        mesh=mesh,
        in_specs=(
            P(("groups", "dp"), "tensor"),
            P(("groups", "dp"), "tensor"),
            P(None, "tensor"),
            P(("groups", "dp"), "tensor", None),
            P(("groups", "dp"), None, "tensor"),
            P("groups"),
            P("groups"),
        ),
        out_specs=(
            P(("groups", "dp"), "tensor"),
            P(("groups", "dp"), "tensor", None),
            P(("groups", "dp"), None, "tensor"),
        ),
        check_vma=False,
    )
```

time: 325 us -> 233 us (0.72)
  waiting for transfers between devices: 260 us -> 121 us
  starting transfers between devices: 0.2 us -> 19.2 us
  matrix products: 26.7 us -> 42.4 us
  local copies, waits for them, and re-layouts: 10.4 us -> 21.8 us
    reduce_scatter x1 -> x0, waiting for transfers between devices: 141 us -> none  [body(): lax.psum_scatter(term.astype(jnp.bfloat16), 'tensor', scatter_dimension=1...]
    ppermute x0 -> x15, waiting for transfers between devices: none -> 121 us  [the longest x6 42.3 us: swap(): return lax.ppermute(a, axis, [(i, i ^ 1 << bit) for i in range(size)])]
    psum x2 -> x0, waiting for transfers between devices: 84.8 us -> none  [the longest x1 50.1 us: body(): lax.psum(share_down.astype(jnp.bfloat16), 'dp').astype(jnp.float32)]
    all_gather x2 -> x3, waiting for transfers between devices: 33.2 us -> 0.01 us  [body(): wide.append(lax.all_gather(piece, ('groups', 'dp'), axis=0, tiled=True))]
    ppermute x0 -> x15, starting transfers between devices: none -> 19.1 us  [the longest x3 6.08 us: body(): lax.ppermute(piece, 'tensor', [(i, (i + step) % n) for i in range(n)])]
    dot_general x8 -> x11, matrix products: 26.7 us -> 42.4 us  [the longest x4 32.5 us: dot(): lax.dot_general(c, w, (((1,), (1,)), ((), ())), preferred_element_type=F32)]
    concatenate x0 -> x5, other arithmetic: none -> 7.15 us  [the longest x2 5.11 us: body(): table = jnp.concatenate([table, swap(table, 'dp', nd, bit)], axis=0)]
    convert_element_type x3 -> x2, other arithmetic: 8.51 us -> 2.03 us  [the longest x1 1.99 us: body(): total = total.astype(BF)]
  transfers between devices with their start and end apart: 5 -> 18, of which waited for: 5 -> 10; matrix products, arithmetic and copies ran while one was open for 11% -> 25% of each run, Pallas kernels for 0% -> 0%
where the time goes in v1:
time: 233 us; the launch traced here: 232 us
  waiting for transfers between devices  121 us (52%)
  matrix products  42.4 us (18%)
  local copies, waits for them, and re-layouts  21.8 us (9%)
  starting transfers between devices  19.2 us (8%)
  between operations  14.1 us (6%)
  other arithmetic  13.8 us (6%)
    ppermute x6, waiting for transfers between devices, swap(): return lax.ppermute(a, axis, [(i, i ^ 1 << bit) for i in range(size)])  42.3 us
    ppermute x3, waiting for transfers between devices, body(): lax.ppermute(piece, 'tensor', [(i, (i + step) % n) for i in range(n)])  38.4 us
    dot_general x4, matrix products, dot(): lax.dot_general(c, w, (((1,), (1,)), ((), ())), preferred_element_type=F32)  32.5 us
    ppermute x3, waiting for transfers between devices, body(): a = lax.ppermute(a, 'tensor', [(i, i + 1) for i in range(r - 1, n - 1)])  21.3 us
    ppermute x3, waiting for transfers between devices, body(): b = lax.ppermute(b, 'tensor', [(i, i - 1) for i in range(n - r, 0, -1)])  18.7 us
    unnamed x21, local copies, waits for them, and re-layouts  7.66 us
    ppermute x3, starting transfers between devices, body(): lax.ppermute(piece, 'tensor', [(i, (i + step) % n) for i in range(n)])  6.08 us
    reshape x1, local copies, waits for them, and re-layouts, body(): result = result + extra.reshape(tokens, width)  5.35 us
  transfers between devices with their start and end apart: 18, of which 10 were waited for; matrix products, arithmetic and copies ran while one was open for 25% of the time, Pallas kernels for 0%

profile of v1, /device:TPU:0, one launch (start us, length us, event | category | flops | bytes accessed | tf_op | source)
XLA Modules:
  0.0 232.0 jit_solution(17116489342961883753)
XLA Ops:
  7.3 2.4 %constant_dynamic-slice_fusion = (bf16[256,1024]{1,0:T(8,128)(2,1)}, bf16[256,1024]{1,0:T(8,128)(2,1)S(1)}, bf16[256,1024]{1,0:T(8,128)(2,1)S(1)}) fusion(bf16[8192,1024]{1,0:T(8,128)(2,1)} %param.9, s32[]{:T(128)S(6)} %select_n.87, s32[]{:T(128)S(6)} %select_n.81, s32[]{:T(128)S(6)} %select_n.84), kind=kLoop, calls=%fused_computation.68 | loop fusion | bytes 3145740 | tf_op jit(solution)/shard_map/dynamic_slice | solution.py:48
  9.7 4.0 %collective-permute-start.6 = (bf16[256,1024]{1,0:T(8,128)(2,1)S(1)}, bf16[256,1024]{1,0:T(8,128)(2,1)}, u32[]{:S(2)}, u32[]{:S(2)}) collective-permute-start(bf16[256,1024]{1,0:T(8,128)(2,1)S(1)} %get-tuple-element.13), channel_id=1, source_target_pairs={{0,2},{1,3},{2,0},{3,1},{4,6},{5,7},{6,4},{7,5},{8,10},{9,11},{10,... | collective-permute-start | bytes 1572872 | tf_op jit(solution)/shard_map/ppermute | solution.py:49
  13.7 23.3 %collective-permute-done.6 = bf16[256,1024]{1,0:T(8,128)(2,1)} collective-permute-done((bf16[256,1024]{1,0:T(8,128)(2,1)S(1)}, bf16[256,1024]{1,0:T(8,128)(2,1)}, u32[]{:S(2)}, u32[]{:S(2)}) %collective-permute-start.6) | collective-permute-done | bytes 524320 | tf_op jit(solution)/shard_map/ppermute | solution.py:49
  37.8 15.1 %collective-permute-done.4 = bf16[256,1024]{1,0:T(8,128)(2,1)} collective-permute-done((bf16[256,1024]{1,0:T(8,128)(2,1)S(1)}, bf16[256,1024]{1,0:T(8,128)(2,1)}, u32[]{:S(2)}, u32[]{:S(2)}) %collective-permute-start.4) | collective-permute-done | bytes 524320 | tf_op jit(solution)/shard_map/ppermute | solution.py:49
  53.0 1.6 collective-permute-start.9
  54.6 27.4 %collective-permute-done.9 = bf16[2,64,3072]{2,1,0:T(8,128)(2,1)S(1)} collective-permute-done((bf16[2,64,3072]{2,1,0:T(8,128)(2,1)S(1)}, bf16[2,64,3072]{2,1,0:T(8,128)(2,1)S(1)}, u32[]{:S(2)}, u32[]{:S(2)}) %collective-permute-start.9) | collective-permute-done | bytes 786464 | tf_op jit(solution)/shard_map/ppermute | solution.py:20
  82.1 2.2 pad_maximum_fusion.2
  88.0 2.9 %pad_maximum_fusion = bf16[8,64,3072]{2,1,0:T(8,128)(2,1)} fusion(bf16[4,64,3072]{2,1,0:T(8,128)(2,1)} %collective-permute-done.10, bf16[2,64,3072]{2,1,0:T(8,128)(2,1)S(1)} %collective-permute-done.9, bf16[2,64,1024]{2,1,0:T(8,128)(2,1)} %param.11, bf16[2,64,2048]{2,1,0:T(8,128)(2,1)S(1)} %bitcast.41), kind=kLoop, calls=%fused_computation.10 | loop fusion | flops 12582912 | bytes 6291456 | tf_op jit(solution)/shard_map/concatenate | solution.py:55
  90.9 3.7 %gather_fusion.1 = bf16[4,64,3072]{2,1,0:T(8,128)(2,1)} fusion(bf16[8,64,3072]{2,1,0:T(8,128)(2,1)} %pad_maximum_fusion, s32[1024]{0:T(1024)S(1)} %pad_clamp_fusion), kind=kCustom, calls=%fused_computation.1 | custom fusion | bytes 3145744 | tf_op jit(solution)/shard_map/jit(_take)/gather | solution.py:63
  94.6 1.8 broadcast_select_fusion
  96.4 2.3 fusion.9
  99.9 5.3 %collective-permute-done.11 = bf16[4,128,128]{1,2,0:T(8,128)(2,1)S(1)} collective-permute-done((bf16[4,128,128]{1,2,0:T(8,128)(2,1)S(1)}, bf16[4,128,128]{1,2,0:T(8,128)(2,1)S(1)}, u32[]{:S(2)}, u32[]{:S(2)}) %collective-permute-start.11) | collective-permute-done | bytes 131104 | tf_op jit(solution)/shard_map/ppermute | solution.py:20
  105.7 8.0 %collective-permute-done.12 = bf16[4,128,128]{1,2,0:T(8,128)(2,1)S(1)} collective-permute-done((bf16[4,128,128]{1,2,0:T(8,128)(2,1)S(1)}, bf16[4,128,128]{1,2,0:T(8,128)(2,1)S(1)}, u32[]{:S(2)}, u32[]{:S(2)}) %collective-permute-start.12) | collective-permute-done | bytes 131104 | tf_op jit(solution)/shard_map/ppermute | solution.py:20
  117.8 2.0 pad_maximum_fusion.1
  119.7 2.3 collective-permute-start
  123.4 21.3 %collective-permute-done = bf16[512,1024]{1,0:T(8,128)(2,1)} collective-permute-done((bf16[512,1024]{1,0:T(8,128)(2,1)}, bf16[512,1024]{1,0:T(8,128)(2,1)}, u32[]{:S(2)}, u32[]{:S(2)}) %collective-permute-start) | collective-permute-done | bytes 1048608 | tf_op jit(solution)/shard_map/ppermute | solution.py:41
  144.7 1.7 collective-permute-start.5
  146.4 3.4 %collective-permute-done.1 = bf16[512,1024]{1,0:T(8,128)(2,1)} collective-permute-done((bf16[512,1024]{1,0:T(8,128)(2,1)}, bf16[512,1024]{1,0:T(8,128)(2,1)}, u32[]{:S(2)}, u32[]{:S(2)}) %collective-permute-start.1) | collective-permute-done | bytes 1048608 | tf_op jit(solution)/shard_map/ppermute | solution.py:42
  151.1 2.0 add_convert_fusion
  154.2 1.7 slice.55
  155.9 2.3 collective-permute-start.14
  158.2 6.9 %fusion.5 = f32[2048,512]{1,0:T(8,128)} fusion(bf16[512,1024]{1,0:T(8,128)(2,1)} %param.8, bf16[8192,1024]{1,0:T(8,128)(2,1)} %param.9, s32[]{:T(128)S(6)} %select_n.78), kind=kOutput, calls=%fused_computation.8 | convolution fusion | flops 2147483648 | bytes 9437188 | tf_op jit(solution)/shard_map/dot_general | solution.py:96
  165.1 11.7 %collective-permute-done.2 = bf16[512,1024]{1,0:T(8,128)(2,1)} collective-permute-done((bf16[512,1024]{1,0:T(8,128)(2,1)}, bf16[512,1024]{1,0:T(8,128)(2,1)}, u32[]{:S(2)}, u32[]{:S(2)}) %collective-permute-start.2) | collective-permute-done | bytes 1048608 | tf_op jit(solution)/shard_map/ppermute | solution.py:42
  179.0 2.8 %fusion.20 = f32[4,128,2048]{2,1,0:T(8,128)} fusion(bf16[4,64,3072]{2,1,0:T(8,128)(2,1)S(1)} %copy-done.4, bf16[4,128,128]{1,2,0:T(8,128)(2,1)S(1)} %fusion.24), kind=kOutput, calls=%fused_computation.36 | convolution fusion | flops 134217728 | bytes 5308416 | tf_op jit(solution)/shard_map/btr,brh->bth/dot_general | solution.py:103
  181.8 5.3 %copy.29 = f32[512,2048]{0,1:T(8,128)} copy(f32[512,2048]{1,0:T(8,128)} %bitcast.38) | data formatting | bytes 8388608 | tf_op jit(solution)/shard_map/reshape | solution.py:104
  187.1 2.5 %convert_add_fusion = f32[2,64,3072]{2,0,1:T(2,128)S(1)} fusion(bf16[2,64,3072]{2,0,1:T(2,128)(2,1)} %collective-permute-done.14, bf16[4,64,3072]{2,0,1:T(4,128)(2,1)} %copy-done.5), kind=kLoop, calls=%fused_computation.19 | loop fusion | flops 1179648 | bytes 3145728 | tf_op jit(solution)/shard_map/add | solution.py:89
  189.7 1.6 copy.22
  192.3 6.9 %fusion.13 = f32[512,2048]{0,1:T(8,128)} fusion(bf16[2048,1024]{1,0:T(8,128)(2,1)} %all-gather.6.cloned.1.call-done, bf16[512,1024]{1,0:T(8,128)(2,1)} %collective-permute-done.5, bf16[512,1024]{1,0:T(8,128)(2,1)} %collective-permute-done.2, pred[]{:T(512)S(6)} %ge.21), kind=kOutput, calls=%fused_computation.29 | convolution fusion | flops 2148007936 | bytes 10485761 | tf_op jit(solution)/shard_map/dot_general | solution.py:96
  199.2 3.7 %collective-permute-done.3 = bf16[512,1024]{1,0:T(8,128)(2,1)} collective-permute-done((bf16[512,1024]{1,0:T(8,128)(2,1)}, bf16[512,1024]{1,0:T(8,128)(2,1)}, u32[]{:S(2)}, u32[]{:S(2)}) %collective-permute-start.3) | collective-permute-done | bytes 1048608 | tf_op jit(solution)/shard_map/ppermute | solution.py:42
  202.9 6.9 %fusion.15 = f32[512,2048]{0,1:T(8,128)} fusion(bf16[2048,1024]{1,0:T(8,128)(2,1)} %all-gather.4.cloned.1.call-done, bf16[512,1024]{1,0:T(8,128)(2,1)} %collective-permute-done, bf16[512,1024]{1,0:T(8,128)(2,1)} %collective-permute-done.3, pred[]{:T(512)S(6)} %ge.20), kind=kOutput, calls=%fused_computation.31 | convolution fusion | flops 2148007936 | bytes 10485761 | tf_op jit(solution)/shard_map/dot_general | solution.py:96
  209.8 11.8 %fusion.4 = bf16[512,2048]{0,1:T(8,128)(2,1)} fusion(f32[512,2048]{0,1:T(8,128)} %copy.29, f32[512,2048]{0,1:T(8,128)} %fusion.13, f32[512,2048]{0,1:T(8,128)} %fusion.15, f32[2048,512]{1,0:T(8,128)} %fusion.5, bf16[2048,1024]{1,0:T(8,128)(2,1)} %all-gather.8.cloned.1.call-done, pred[512]{0:T(512)(128)(4,1)S(1)} %fusion.48, ...), kind=kOutput, calls=%fused_computation.7 | convolution fusion | flops 2154299392 | bytes 25166336 | tf_op jit(solution)/shard_map/dot_general | solution.py:96
  221.6 3.9 %copy.21 = bf16[512,2048]{1,0:T(8,128)(2,1)} copy(bf16[512,2048]{0,1:T(8,128)(2,1)} %fusion.4) | data formatting | bytes 4194304
  (68 shorter events, 17.4 us)
Async XLA Ops:
  7.2 91.5 %copy-start = (bf16[512,2048]{1,0:T(8,128)(2,1)S(1)}, bf16[512,2048]{1,0:T(8,128)(2,1)}, u32[]{:S(2)}) copy-start(bf16[512,2048]{1,0:T(8,128)(2,1)} %param.7) | copy-start | bytes 6291460
  7.2 45.8 %copy-start.7 = (bf16[2,64,1024]{2,1,0:T(8,128)(2,1)S(1)}, bf16[2,64,1024]{2,1,0:T(8,128)(2,1)}, u32[]{:S(2)}) copy-start(bf16[2,64,1024]{2,1,0:T(8,128)(2,1)} %param.11) | copy-start | bytes 786436
  7.2 45.8 %copy-start.6 = (bf16[2,2048,64]{1,2,0:T(8,128)(2,1)S(1)}, bf16[2,2048,64]{1,2,0:T(8,128)(2,1)}, u32[]{:S(2)}) copy-start(bf16[2,2048,64]{1,2,0:T(8,128)(2,1)} %param.10) | copy-start | bytes 1572868
  7.2 185.1 %all-gather.6.cloned.1.call-start = ((), (), s32[]{:S(2)}) async-start(), calls=%async_computation.1 | async-start | bytes 4718592 | tf_op jit(solution)/shard_map/all_gather | solution.py:50
  9.7 75.9 %copy-start.8 = (s32[16]{0:T(128)S(1)}, s32[16]{0:T(128)}, u32[]{:S(2)}) copy-start(s32[16]{0:T(128)} %param.12) | copy-start | bytes 196
  9.7 76.0 %copy-start.2 = (s32[8]{0:T(128)S(1)}, s32[8]{0:T(128)}, u32[]{:S(2)}) copy-start(s32[8]{0:T(128)} %param.13) | copy-start | bytes 100
  9.7 27.3 %collective-permute-start.6 = (bf16[256,1024]{1,0:T(8,128)(2,1)S(1)}, bf16[256,1024]{1,0:T(8,128)(2,1)}, u32[]{:S(2)}, u32[]{:S(2)}) collective-permute-start(bf16[256,1024]{1,0:T(8,128)(2,1)S(1)} %get-tuple-element.13), channel_id=1, source_target_pairs={{0,2},{1,3},{2,0},{3,1},{4,6},{5,7},{6,4},{7,5},{8,10},{9,11},{10,... | collective-permute-start | bytes 1572872 | tf_op jit(solution)/shard_map/ppermute | solution.py:49
  37.0 165.8 %all-gather.4.cloned.1.call-start = ((), (), s32[]{:S(2)}) async-start(), calls=%async_computation | async-start | bytes 4718592 | tf_op jit(solution)/shard_map/all_gather | solution.py:50
  37.1 15.8 %collective-permute-start.4 = (bf16[256,1024]{1,0:T(8,128)(2,1)S(1)}, bf16[256,1024]{1,0:T(8,128)(2,1)}, u32[]{:S(2)}, u32[]{:S(2)}) collective-permute-start(bf16[256,1024]{1,0:T(8,128)(2,1)S(1)} %get-tuple-element.12), channel_id=1, source_target_pairs={{0,1},{1,2},{2,3},{3,0},{4,5},{5,6},{6,7},{7,4},{8,9},{9,10},{10,1... | collective-permute-start | bytes 1572872 | tf_op jit(solution)/shard_map/ppermute | solution.py:49
  52.9 156.9 %all-gather.8.cloned.1.call-start = ((), (), s32[]{:S(2)}) async-start(), calls=%async_computation.2 | async-start | bytes 4718592 | tf_op jit(solution)/shard_map/all_gather | solution.py:50
  53.0 29.0 %collective-permute-start.9 = (bf16[2,64,3072]{2,1,0:T(8,128)(2,1)S(1)}, bf16[2,64,3072]{2,1,0:T(8,128)(2,1)S(1)}, u32[]{:S(2)}, u32[]{:S(2)}) collective-permute-start(bf16[2,64,3072]{2,1,0:T(8,128)(2,1)S(1)} %pad_maximum_fusion.3), channel_id=1, source_target_pairs={{0,8},{4,12},{8,0},{12,4},{1,9},{5,13},{9,1},{13,5},{2,10},{6,14},... | collective-permute-start | bytes 2359304 | tf_op jit(solution)/shard_map/ppermute | solution.py:20
  84.3 3.8 %collective-permute-start.10 = (bf16[4,64,3072]{2,1,0:T(8,128)(2,1)}, bf16[4,64,3072]{2,1,0:T(8,128)(2,1)}, u32[]{:S(2)}, u32[]{:S(2)}) collective-permute-start(bf16[4,64,3072]{2,1,0:T(8,128)(2,1)} %pad_maximum_fusion.2), channel_id=1, source_target_pairs={{0,4},{4,0},{8,12},{12,8},{1,5},{5,1},{9,13},{13,9},{2,6},{6,2},{1... | collective-permute-start | bytes 4718600 | tf_op jit(solution)/shard_map/ppermute | solution.py:20
  84.3 21.4 %collective-permute-start.8 = (bf16[256,1024]{1,0:T(8,128)(2,1)}, bf16[256,1024]{1,0:T(8,128)(2,1)}, u32[]{:S(2)}, u32[]{:S(2)}) collective-permute-start(bf16[256,1024]{1,0:T(8,128)(2,1)} %get-tuple-element.11), channel_id=1, source_target_pairs={{0,3},{1,0},{2,1},{3,2},{4,7},{5,4},{6,5},{7,6},{8,11},{9,8},{10,9... | collective-permute-start | bytes 1572872 | tf_op jit(solution)/shard_map/ppermute | solution.py:49
  96.4 2.3 copy-start.3
  99.6 5.6 %collective-permute-start.11 = (bf16[4,128,128]{1,2,0:T(8,128)(2,1)S(1)}, bf16[4,128,128]{1,2,0:T(8,128)(2,1)S(1)}, u32[]{:S(2)}, u32[]{:S(2)}) collective-permute-start(bf16[4,128,128]{1,2,0:T(8,128)(2,1)S(1)} %pad_maximum_fusion.4), channel_id=1, source_target_pairs={{0,1},{1,0},{2,3},{3,2},{4,5},{5,4},{6,7},{7,6},{8,9},{9,8},{10,11... | collective-permute-start | bytes 393224 | tf_op jit(solution)/shard_map/ppermute | solution.py:20
  105.2 8.5 %collective-permute-start.12 = (bf16[4,128,128]{1,2,0:T(8,128)(2,1)S(1)}, bf16[4,128,128]{1,2,0:T(8,128)(2,1)S(1)}, u32[]{:S(2)}, u32[]{:S(2)}) collective-permute-start(bf16[4,128,128]{1,2,0:T(8,128)(2,1)S(1)} %add_convert_fusion.2), channel_id=1, source_target_pairs={{0,2},{1,3},{2,0},{3,1},{4,6},{5,7},{6,4},{7,5},{8,10},{9,11},{10,... | collective-permute-start | bytes 393224 | tf_op jit(solution)/shard_map/ppermute | solution.py:20
  119.7 31.3 %collective-permute-start.13 = (bf16[4,64,3072]{2,0,1:T(4,128)(2,1)}, bf16[4,64,3072]{2,0,1:T(4,128)(2,1)}, u32[]{:S(2)}, u32[]{:S(2)}) collective-permute-start(bf16[4,64,3072]{2,0,1:T(4,128)(2,1)} %pad_maximum_fusion.1), channel_id=1, source_target_pairs={{0,4},{4,0},{8,12},{12,8},{1,5},{5,1},{9,13},{13,9},{2,6},{6,2},{1... | collective-permute-start | bytes 4718600 | tf_op jit(solution)/shard_map/ppermute | solution.py:20
  119.7 25.0 %collective-permute-start = (bf16[512,1024]{1,0:T(8,128)(2,1)}, bf16[512,1024]{1,0:T(8,128)(2,1)}, u32[]{:S(2)}, u32[]{:S(2)}) collective-permute-start(bf16[512,1024]{1,0:T(8,128)(2,1)} %param.8), channel_id=1, source_target_pairs={{0,1},{1,2},{2,3},{4,5},{5,6},{6,7},{8,9},{9,10},{10,11},{12,13},{... | collective-permute-start | bytes 3145736 | tf_op jit(solution)/shard_map/ppermute | solution.py:41
  122.0 27.8 %collective-permute-start.1 = (bf16[512,1024]{1,0:T(8,128)(2,1)}, bf16[512,1024]{1,0:T(8,128)(2,1)}, u32[]{:S(2)}, u32[]{:S(2)}) collective-permute-start(bf16[512,1024]{1,0:T(8,128)(2,1)} %param.8), channel_id=1, source_target_pairs={{3,2},{2,1},{1,0},{7,6},{6,5},{5,4},{11,10},{10,9},{9,8},{15,14},{... | collective-permute-start | bytes 3145736 | tf_op jit(solution)/shard_map/ppermute | solution.py:42
  144.7 33.4 %collective-permute-start.5 = (bf16[512,1024]{1,0:T(8,128)(2,1)}, bf16[512,1024]{1,0:T(8,128)(2,1)}, u32[]{:S(2)}, u32[]{:S(2)}) collective-permute-start(bf16[512,1024]{1,0:T(8,128)(2,1)} %collective-permute-done), channel_id=1, source_target_pairs={{1,2},{2,3},{5,6},{6,7},{9,10},{10,11},{13,14},{14,15},{17,18},{18... | collective-permute-start | bytes 3145736 | tf_op jit(solution)/shard_map/ppermute | solution.py:41
  149.8 27.0 %collective-permute-start.2 = (bf16[512,1024]{1,0:T(8,128)(2,1)}, bf16[512,1024]{1,0:T(8,128)(2,1)}, u32[]{:S(2)}, u32[]{:S(2)}) collective-permute-start(bf16[512,1024]{1,0:T(8,128)(2,1)} %collective-permute-done.1), channel_id=1, source_target_pairs={{2,1},{1,0},{6,5},{5,4},{10,9},{9,8},{14,13},{13,12},{18,17},{17,1... | collective-permute-start | bytes 3145736 | tf_op jit(solution)/shard_map/ppermute | solution.py:42
  153.1 1.2 copy-start.5
  155.9 23.0 %copy-start.4 = (bf16[4,64,3072]{2,1,0:T(8,128)(2,1)S(1)}, bf16[4,64,3072]{2,1,0:T(8,128)(2,1)}, u32[]{:S(2)}) copy-start(bf16[4,64,3072]{2,1,0:T(8,128)(2,1)} %copy-done.3) | copy-start | bytes 4718596
  155.9 31.2 %collective-permute-start.14 = (bf16[2,64,3072]{2,0,1:T(2,128)(2,1)}, bf16[2,64,3072]{2,0,1:T(2,128)(2,1)}, u32[]{:S(2)}, u32[]{:S(2)}) collective-permute-start(bf16[2,64,3072]{2,0,1:T(2,128)(2,1)} %slice.55), channel_id=1, source_target_pairs={{0,8},{4,12},{8,0},{12,4},{1,9},{5,13},{9,1},{13,5},{2,10},{6,14},... | collective-permute-start | bytes 2359304 | tf_op jit(solution)/shard_map/ppermute | solution.py:20
  176.8 26.1 %collective-permute-start.3 = (bf16[512,1024]{1,0:T(8,128)(2,1)}, bf16[512,1024]{1,0:T(8,128)(2,1)}, u32[]{:S(2)}, u32[]{:S(2)}) collective-permute-start(bf16[512,1024]{1,0:T(8,128)(2,1)} %collective-permute-done.2), channel_id=1, source_target_pairs={{1,0},{5,4},{9,8},{13,12},{17,16},{21,20},{25,24},{29,28}} | collective-permute-start | bytes 3145736 | tf_op jit(solution)/shard_map/ppermute | solution.py:42
  178.1 31.7 %collective-permute-start.7 = (bf16[512,1024]{1,0:T(8,128)(2,1)}, bf16[512,1024]{1,0:T(8,128)(2,1)S(1)}, u32[]{:S(2)}, u32[]{:S(2)}) collective-permute-start(bf16[512,1024]{1,0:T(8,128)(2,1)} %collective-permute-done.5), channel_id=1, source_target_pairs={{2,3},{6,7},{10,11},{14,15},{18,19},{22,23},{26,27},{30,31}} | collective-permute-start | bytes 3145736 | tf_op jit(solution)/shard_map/ppermute | solution.py:41
  209.8 15.7 %copy-start.1 = (bf16[512,2048]{1,0:T(8,128)(2,1)S(1)}, bf16[512,2048]{1,0:T(8,128)(2,1)}, u32[]{:S(2)}) copy-start(bf16[512,2048]{1,0:T(8,128)(2,1)} %param.7) | copy-start | bytes 6291460
Sparse Core Ops, SparseCore 0:
  37.2 47.5 all-gather.5
  86.6 38.1 all-gather.3
  126.7 39.3 all-gather.7

commit v2 on v1

v2 whole, which is shorter than its diff:
```python
import functools

import jax
import jax.numpy as jnp
from jax import lax
from jax.experimental import pallas as pl
from jax.experimental.pallas import tpu as pltpu
from jax.sharding import PartitionSpec as P

BLK = 128
PIECE = 256
TILE = 2 * PIECE
BF = jnp.bfloat16
F32 = jnp.float32
VMEM_LIMIT = 56 * 2**20


CHEAP = pl.CostEstimate(flops=1, bytes_accessed=1, transcendentals=0)


def move(name, a, axis, pairs):
    with jax.named_scope(name):
        return lax.ppermute(a, axis, pairs)


def swap(name, a, axis, size, bit):
    return move(name, a, axis, [(i, i ^ (1 << bit)) for i in range(size)])


def together(*values):
    return lax.optimization_barrier(values)


def contract_last(a, b):
    return lax.dot_general(a, b, (((1,), (1,)), ((), ())), preferred_element_type=F32)


def contract_first(a, b):
    return lax.dot_general(a, b, (((0,), (0,)), ((), ())), preferred_element_type=F32)


def params():
    return pltpu.CompilerParams(vmem_limit_bytes=VMEM_LIMIT)


def slot_of(block, ids, owner, *, blocks, owned, bits):
    member = owner[ids[1] * blocks + block]
    relative = (member // owned) ^ ids[1]
    slot = member % owned
    for j, bit in enumerate(bits):
        slot = slot + ((relative >> bit) & 1) * (owned << j)
    return slot


def live_count(block, ids, owner, counts, *, blocks):
    at = ids[1] * blocks + block
    last = owner.shape[0] - 1
    member = owner[at]
    closing = jnp.logical_or(at == last, owner[jnp.minimum(at + 1, last)] != member)
    return jnp.where(closing, counts[member], BLK)


def rank_kernel(ids, owner, counts, hid, cot, *refs, width, blocks, slot, held):
    b = pl.program_id(0)
    count = live_count(b, ids, owner, counts, blocks=blocks)
    parts, out = refs[:-1], refs[-1]
    for i, part in enumerate(parts):

        @pl.when(slot(b, ids, owner) // held == i)
        def _(part=part):
            act = contract_last(hid[...], part[0, :, :width])
            grad = contract_last(cot[...], part[0, :, width:])
            both = jnp.concatenate([act, grad], axis=1)
            rows = lax.broadcasted_iota(jnp.int32, both.shape, 0)
            out[...] = jnp.where(rows < count, both, 0.0).astype(BF)


def rank_partials(ids, owner, counts, hidden, cotan, table, *, blocks, owned, bits):
    width, cols = hidden.shape[1], cotan.shape[1]
    held, rank = table[0].shape[:2]
    slot = functools.partial(slot_of, blocks=blocks, owned=owned, bits=bits)

    def chosen(i):
        def index(b, ids, owner, counts):
            at = slot(b, ids, owner)
            return (jnp.where(at // held == i, at % held, 0), 0, 0)

        return pl.BlockSpec((1, rank, width + cols), index)

    return pl.pallas_call(
        functools.partial(rank_kernel, width=width, blocks=blocks, slot=slot, held=held),
        grid_spec=pltpu.PrefetchScalarGridSpec(
            num_scalar_prefetch=3,
            grid=(blocks,),
            in_specs=[
                pl.BlockSpec((BLK, width), lambda b, *s: (b, 0)),
                pl.BlockSpec((BLK, cols), lambda b, *s: (b, 0)),
            ]
            + [chosen(i) for i in range(len(table))],
            out_specs=pl.BlockSpec((BLK, 2 * rank), lambda b, *s: (b, 0)),
        ),
        out_shape=jax.ShapeDtypeStruct((blocks * BLK, 2 * rank), BF),
        compiler_params=params(),
        cost_estimate=CHEAP,
        name="rank_partials",
    )(ids, owner, counts, hidden, cotan, *table)


def grads_kernel(ids, owner, hid, cot, both, send, keep, acc, *, width, blocks, slot, half):
    step = pl.program_id(0)
    position = jnp.where(step < half, step + half, step - half)
    rank = both.shape[1] // 2
    acc[...] = jnp.zeros_like(acc)
    for b in range(blocks):

        @pl.when(slot(b, ids, owner) == position)
        def _(b=b):
            at = pl.ds(b * BLK, BLK)
            pair = both[at, :].astype(F32)
            acc[:, :width] += contract_first(pair[:, rank:].astype(BF), hid[at, :])
            acc[:, width:] += contract_first(pair[:, :rank].astype(BF), cot[at, :])

    @pl.when(step < half)
    def _():
        send[0] = acc[...].astype(BF)

    @pl.when(step >= half)
    def _():
        keep[0] = acc[...].astype(BF)


def member_grads(ids, owner, hidden, cotan, both, members, *, blocks, owned, bits):
    tokens, width = hidden.shape
    cols = cotan.shape[1]
    rank = both.shape[1] // 2
    half = members // 2
    slot = functools.partial(slot_of, blocks=blocks, owned=owned, bits=bits)
    shape = jax.ShapeDtypeStruct((half, rank, width + cols), BF)
    return pl.pallas_call(
        functools.partial(
            grads_kernel, width=width, blocks=blocks, slot=slot, half=half
        ),
        grid_spec=pltpu.PrefetchScalarGridSpec(
            num_scalar_prefetch=2,
            grid=(members,),
            in_specs=[
                pl.BlockSpec((tokens, width), lambda p, *s: (0, 0)),
                pl.BlockSpec((tokens, cols), lambda p, *s: (0, 0)),
                pl.BlockSpec((tokens, 2 * rank), lambda p, *s: (0, 0)),
            ],
            out_specs=[
                pl.BlockSpec((1, rank, width + cols), lambda p, *s: (jnp.minimum(p, half - 1), 0, 0)),
                pl.BlockSpec((1, rank, width + cols), lambda p, *s: (jnp.maximum(p - half, 0), 0, 0)),
            ],
            scratch_shapes=[pltpu.VMEM((rank, width + cols), F32)],
        ),
        out_shape=[shape, shape],
        compiler_params=params(),
        cost_estimate=CHEAP,
        name="member_grads",
    )(ids, owner, hidden, cotan, both)


def relative_tile(p, ids):
    core = (ids[1] & 1) ^ (p >> 1)
    x, y = ids[0], (ids[1] >> 1) & 1
    at = jnp.where(core == 0, y ^ (p & 1), 2 + (x ^ (p & 1)))
    return at, jnp.where(core == 0, x, y)


def plain_tile(p, ids):
    return p, 0


def tile_part(half, flip):
    return pl.ds(pl.multiple_of((half ^ flip) * PIECE, PIECE), PIECE)


def by_part(p, parts, run):
    if parts == 1:
        run(0)
        return
    for i in range(parts):
        pl.when(p == i)(functools.partial(run, i))


def local_kernel(ids, cot, weight, out):
    out[...] = contract_last(cot[...], weight[...])


def local_products(ids, cotan, weight, width):
    tokens, cols = cotan.shape
    tiles = width // TILE
    return pl.pallas_call(
        local_kernel,
        grid_spec=pltpu.PrefetchScalarGridSpec(
            num_scalar_prefetch=1,
            grid=(tiles,),
            in_specs=[
                pl.BlockSpec((tokens, cols), lambda p, *s: (0, 0)),
                pl.BlockSpec((TILE, cols), lambda p, i: (i[2] * tiles + p, 0)),
            ],
            out_specs=pl.BlockSpec((tokens, TILE), lambda p, *s: (0, p)),
        ),
        out_shape=jax.ShapeDtypeStruct((tokens, width), F32),
        compiler_params=params(),
        cost_estimate=CHEAP,
        name="local_products",
    )(ids, cotan, weight)


def fold_kernel(ids, owner, counts, acc, *refs, terms, parts, tile, first, blocks, slot, table_parts, held, final):
    p = pl.program_id(0)
    xs, refs = refs[:terms], refs[terms:]
    ws, refs = refs[: terms * parts], refs[terms * parts :]
    table, out = refs[:table_parts], refs[-1]
    _, flip = tile(first + p, ids)
    rows = lax.broadcasted_iota(jnp.int32, (BLK, PIECE), 0)

    def run(i):
        total = contract_last(xs[0][...], ws[i][...])
        for t in range(1, terms):
            total += contract_last(xs[t][...], ws[t * parts + i][...])
        for half in range(2):
            to = tile_part(half, flip)
            part = acc[:, to] + total[:, half * PIECE : (half + 1) * PIECE]
            if not final:
                out[:, to] = part
                continue
            for b in range(blocks):
                at = slice(b * BLK, (b + 1) * BLK)
                count = live_count(b, ids, owner, counts, blocks=blocks)
                out[at, to] = jnp.where(rows < count, part[at], 0.0).astype(BF)

    by_part(p, parts, run)
    if table:
        both = refs[table_parts]
        rank = both.shape[1] // 2
        for b in range(blocks):
            at = slice(b * BLK, (b + 1) * BLK)
            place = slot(b, ids, owner)
            for i, part in enumerate(table):

                @pl.when(place // held == i)
                def _(at=at, place=place, part=part):
                    out[at, :] += lax.dot_general(
                        both[at, rank:],
                        part[place % held],
                        (((1,), (0,)), ((), ())),
                        preferred_element_type=F32,
                    )


def fold(ids, owner, counts, acc, xs, ws, tile, first, *, blocks, owned, bits, before=None, final=False, table=(), both=None):
    tokens, width = acc.shape
    cols = xs[0].shape[1]
    parts = len(ws[0])
    flat = [part for w in ws for part in w]
    tiles = parts if parts > 1 else flat[0].shape[0] // TILE
    slot = functools.partial(slot_of, blocks=blocks, owned=owned, bits=bits)
    block = pl.BlockSpec((tokens, TILE), lambda p, i, *s: (0, tile(first + p, i)[0]))
    operands = [ids, owner, counts, acc, *xs, *flat, *table]
    in_specs = [block]
    in_specs += [pl.BlockSpec((tokens, cols), lambda p, *s: (0, 0)) for _ in xs]
    in_specs += [pl.BlockSpec((TILE, cols), lambda p, *s: (p if parts == 1 else 0, 0)) for _ in flat]
    held = 0
    if table:
        held, rank = table[0].shape[:2]
        in_specs += [
            pl.BlockSpec((held, rank, TILE), lambda p, i, *s: (0, 0, tile(first + p, i)[0])) for _ in table
        ]
        operands.append(both)
        in_specs.append(pl.BlockSpec((tokens, 2 * rank), lambda p, *s: (0, 0)))
    alias = {} if final else {3: 0}
    if before is not None:
        alias = {len(operands): 0}
        operands.append(before)
        in_specs.append(pl.BlockSpec(memory_space=pl.ANY))
    return pl.pallas_call(
        functools.partial(
            fold_kernel,
            terms=len(xs),
            parts=parts,
            tile=tile,
            first=first,
            blocks=blocks,
            slot=slot,
            table_parts=len(table),
            held=held,
            final=final,
        ),
        grid_spec=pltpu.PrefetchScalarGridSpec(
            num_scalar_prefetch=3, grid=(tiles,), in_specs=in_specs, out_specs=block
        ),
        out_shape=jax.ShapeDtypeStruct((tokens, width), BF if final else F32),
        input_output_aliases=alias,
        compiler_params=params(),
        cost_estimate=CHEAP,
        name="finish" if final else "fold",
    )(*operands)


def line(cotan, n, z):
    ups, downs = [], []
    a = b = cotan
    for r in range(1, n):
        a = lax.ppermute(a, "tensor", [(i, i + 1) for i in range(r - 1, n - 1)])
        b = lax.ppermute(b, "tensor", [(i, i - 1) for i in range(n - r, 0, -1)])
        ups.append(a)
        downs.append(b)
    return [jnp.where(z >= s, ups[s - 1], downs[n - s - 1]) for s in range(1, n)]


def body(hidden, query_gradient, weight, down, up, owner, counts):
    n = lax.axis_size("tensor")
    nd = lax.axis_size("dp")
    ng = lax.axis_size("groups")
    x, me, z = lax.axis_index("groups"), lax.axis_index("dp"), lax.axis_index("tensor")
    middle = jnp.logical_and(z > 0, z < n - 1)
    ids = jnp.stack([x, me, z, middle.astype(jnp.int32)]).astype(jnp.int32)
    tokens, width = hidden.shape
    cols = query_gradient.shape[1]
    owned = down.shape[0]
    share = width // (ng * nd)
    bits = tuple(range(nd.bit_length() - 2, -1, -1))
    half = tokens // 2
    sizes = dict(blocks=tokens // BLK, owned=owned, bits=bits)
    fast = (ng, nd, n, share) == (2, 4, 4, PIECE)

    if fast:
        y, core = me // 2, me % 2
        place = jnp.where(core == 0, 2 * y + x, 4 + 2 * x + y)
        turn_a = [(i, i ^ (4 if i % 2 == 0 else 2)) for i in range(8)]
        turn_b = [(i, i ^ (2 if i % 2 == 0 else 4)) for i in range(8)]
        turn_c = [(i, i ^ 1) for i in range(8)]
        outer, inner = [(0, 1), (1, 0), (2, 3), (3, 2)], [(1, 2), (2, 1)]
        outward = [(1, 0), (2, 3)]
    else:
        place = x * nd + me
    copies = ("groups", "dp")

    def cut(to):
        return lax.dynamic_slice(weight, (to * width + place * share, 0), (share, cols))

    def piece(step, own):
        return move(f"piece{step}", own, "tensor", [(i, i ^ step) for i in range(n)])

    def turned(name, own, pairs):
        return jnp.concatenate([own, move(name, own, copies, pairs)], axis=0)

    def more(bit, parts):
        return parts + [swap(f"table{bit}_{i}", part, "dp", nd, bit) for i, part in enumerate(parts)]

    def ranks(table):
        return rank_partials(ids, owner, counts, hidden, query_gradient, table, **sizes)

    def rank_sum(bit, both):
        got = swap(f"rank_sum{bit}", both, "tensor", n, bit)
        return (both.astype(F32) + got.astype(F32)).astype(BF)

    def grads(both):
        return member_grads(ids, owner, hidden, query_gradient, both, nd * owned, **sizes)

    def grad_sum(send, keep):
        for bit in reversed(bits):
            total = keep.astype(F32) + swap(f"grads{bit}", send, "dp", nd, bit).astype(F32)
            if bit != bits[0]:
                rest = total.shape[0] // 2
                keep, send = total[:rest], total[rest:].astype(BF)
        return jnp.swapaxes(total[:, :, :width], 1, 2), total[:, :, width:]

    def local():
        return local_products(ids, query_gradient, weight, width)

    def folded(acc, xs, ws, tile, first, **more):
        return fold(ids, owner, counts, acc, xs, ws, tile, first, **sizes, **more)

    table = [jnp.concatenate([jnp.swapaxes(down, 1, 2), up], axis=2)]
    if fast:
        by_one = move("outer", query_gradient, "tensor", outer)
        across = move("inner", query_gradient, "tensor", inner)
        table = more(bits[0], table)
        cuts = [cut(z ^ d) for d in (1, 2, 3)]
        acc = local()
        by_one, across, cuts, table, acc = together(by_one, across, cuts, table, acc)

        piece1, piece3 = piece(1, cuts[0]), piece(3, cuts[2])
        table = more(bits[1], table)
        both = ranks(table)
        shares = [move(f"ranks{d}", both, "tensor", [(i, i ^ d) for i in range(n)]) for d in (1, 2, 3)]
        both = sum((a.astype(F32) for a in shares), both.astype(F32)).astype(BF)
        by_one, across, piece1, piece3, both = together(by_one, across, piece1, piece3, both)

        end_two = move("inner_out", across, "tensor", outward)
        by_two = move("outer_in", by_one, "tensor", inner)
        wide1 = turned("turn_a1", piece1, turn_a)
        wide3 = turned("turn_a3", piece3, turn_a)
        send, keep = grads(both)
        end_two, by_two, wide1, wide3, send, cut2 = together(end_two, by_two, wide1, wide3, send, cuts[1])

        piece2 = piece(2, cut2)
        end_upper = move("outer_in_out0", by_two[:half], "tensor", outward)
        wide1 = [wide1, move("turn_b1", wide1, copies, turn_b)]
        wide3 = [wide3, move("turn_b3", wide3, copies, turn_b)]
        two = jnp.where(middle, by_two, end_two)
        piece2, end_upper, wide1, wide3, by_two, two, send = together(
            piece2, end_upper, wide1, wide3, by_two, two, send
        )

        wide2 = turned("turn_a2", piece2, turn_a)
        other1 = [move(f"turn_c1{i}", part, copies, turn_c) for i, part in enumerate(wide1)]
        got = swap("grads0", send, "dp", nd, bits[1])
        wide2, other1, got = together(wide2, other1, got)

        rest = got.shape[0] // 2
        total = keep.astype(F32) + got.astype(F32)
        send = total[rest:].astype(BF)
        end_lower = move("outer_in_out1", by_two[half:], "tensor", outward)
        wide2 = [wide2, move("turn_b2", wide2, copies, turn_b)]
        other3 = [move(f"turn_c3{i}", part, copies, turn_c) for i, part in enumerate(wide3)]
        acc = folded(acc, [by_one], [wide1 + other1], relative_tile, 0, table=table, both=both)
        wide2, acc, end_lower, other3, send = together(wide2, acc, end_lower, other3, send)

        got = swap("grads1", send, "dp", nd, bits[0])
        other2 = [move(f"turn_c2{i}", part, copies, turn_c) for i, part in enumerate(wide2)]
        three = jnp.where(middle, across, jnp.concatenate([end_upper, end_lower], axis=0))
        result = folded(acc, [two, three], [wide2, wide3], relative_tile, 0, final=True)
        result = folded(acc, [two, three], [other2, other3], relative_tile, 2, before=result, final=True)
        got = together(got, result)[0]
        total = total[:rest] + got.astype(F32)
        grad_down, grad_up = jnp.swapaxes(total[:, :, :width], 1, 2), total[:, :, width:]
    else:
        xs = line(query_gradient, n, z)
        wides = []
        for step in range(1, n):
            own = move(f"piece{step}", cut(lax.rem(z + step, n)), "tensor", [(i, (i + step) % n) for i in range(n)])
            wides.append((lax.all_gather(own, copies, axis=0, tiled=True),))
        for bit in bits:
            table = [jnp.concatenate(more(bit, table), axis=0)]
        both = ranks(table)
        for bit in range(n.bit_length() - 1):
            both = rank_sum(bit, both)
        grad_down, grad_up = grad_sum(*grads(both))
        acc = folded(local(), xs[:1], wides[:1], plain_tile, 0, table=table, both=both)
        result = folded(acc, xs[1:], wides[1:], plain_tile, 0, final=True)
    return result, grad_down, grad_up


def solution(mesh):
    return jax.shard_map(
        body,
        mesh=mesh,
        in_specs=(
            P(("groups", "dp"), "tensor"),
            P(("groups", "dp"), "tensor"),
            P(None, "tensor"),
            P(("groups", "dp"), "tensor", None),
            P(("groups", "dp"), None, "tensor"),
            P("groups"),
            P("groups"),
        ),
        out_specs=(
            P(("groups", "dp"), "tensor"),
            P(("groups", "dp"), "tensor", None),
            P(("groups", "dp"), None, "tensor"),
        ),
        check_vma=False,
    )
```

time: 233 us -> 178 us (0.76)
  waiting for transfers between devices: 121 us -> 72 us
  Pallas kernels: 0 us -> 48.2 us
  matrix products: 42.4 us -> 0 us
  starting transfers between devices: 19.2 us -> 38.1 us
  local copies, waits for them, and re-layouts: 21.8 us -> 8.11 us
  between operations: 14.1 us -> 0.95 us
  other arithmetic: 13.8 us -> 9.38 us
    ppermute x15 -> x29, waiting for transfers between devices: 121 us -> 72 us  [move(): return lax.ppermute(a, axis, pairs)]
    pallas_call x0 -> x6, Pallas kernels: none -> 48.2 us  [the longest x3 27.2 us: fold(): pl.pallas_call(functools.partial(fold_kernel, terms=len(xs), parts=parts,...]
    dot_general x11 -> x0, matrix products: 42.4 us -> none  [the longest x4 32.5 us: dot(): lax.dot_general(c, w, (((1,), (1,)), ((), ())), preferred_element_type=F32)]
    ppermute x15 -> x29, starting transfers between devices: 19.1 us -> 38.1 us  [move(): return lax.ppermute(a, axis, pairs)]
    concatenate x5 -> x4, other arithmetic: 7.15 us -> 1.38 us  [the longest x1 1.18 us: body(): table = [jnp.concatenate([jnp.swapaxes(down, 1, 2), up], axis=2)]]
    reshape x1 -> x0, local copies, waits for them, and re-layouts: 5.35 us -> none  [body(): result = result + extra.reshape(tokens, width)]
    gather x2 -> x0, local copies, waits for them, and re-layouts: 4.33 us -> none  [the longest x1 3.68 us: body(): chosen = jnp.take(table, slot, axis=0)]
    unnamed x21 -> x36, local copies, waits for them, and re-layouts: 7.66 us -> 3.78 us
  transfers between devices with their start and end apart: 18 -> 29, of which waited for: 10 -> 10; matrix products, arithmetic and copies ran while one was open for 25% -> 7% of each run, Pallas kernels for 0% -> 27%
where the time goes in v2:
time: 178 us; the launch traced here: 177 us
  waiting for transfers between devices  72 us (40%)
  Pallas kernels  48.2 us (27%)
  starting transfers between devices  38.1 us (21%)
  other arithmetic  9.38 us (5%)
  local copies, waits for them, and re-layouts  8.11 us (5%)
    ppermute x29, waiting for transfers between devices, move(): return lax.ppermute(a, axis, pairs)  72 us
    ppermute x29, starting transfers between devices, move(): return lax.ppermute(a, axis, pairs)  38.1 us
    pallas_call x3, Pallas kernels, fold(): pl.pallas_call(functools.partial(fold_kernel, terms=len(xs), parts=parts,...  27.2 us
    pallas_call x1, Pallas kernels, member_grads(): pl.pallas_call(functools.partial(grads_kernel, width=width, blocks=blocks...  7.57 us
    pallas_call x1, Pallas kernels, local_products(): pl.pallas_call(local_kernel, grid_spec=pltpu.PrefetchScalarGridSpec(num_s...  7.19 us
    pallas_call x1, Pallas kernels, rank_partials(): pl.pallas_call(functools.partial(rank_kernel, width=width, blocks=blocks,...  6.19 us
    unnamed x36, local copies, waits for them, and re-layouts  3.78 us
  transfers between devices with their start and end apart: 29, of which 10 were waited for; matrix products, arithmetic and copies ran while one was open for 7% of the time, Pallas kernels for 27%

profile of v2, /device:TPU:0, one launch (start us, length us, event | category | flops | bytes accessed | tf_op | source)
XLA Modules:
  0.0 176.7 jit_solution(2562525963434811977)
XLA Ops:
  0.6 3.1 %collective-permute-start = (bf16[512,1024]{1,0:T(8,128)(2,1)}, bf16[512,1024]{1,0:T(8,128)(2,1)S(1)}, u32[]{:S(2)}, u32[]{:S(2)}) collective-permute-start(bf16[512,1024]{1,0:T(8,128)(2,1)} %cot.5), channel_id=1, source_target_pairs={{0,1},{1,0},{2,3},{3,2},{4,5},{5,4},{6,7},{7,6},{8,9},{9,8},{10,11... | collective-permute-start | bytes 3145736 | tf_op jit(solution)/shard_map/outer/ppermute | solution.py:23
  3.7 1.7 collective-permute-start.1
  6.6 1.6 collective-permute-start.2
  8.8 7.2 %local_products.1.acc = f32[512,2048]{1,0:T(8,128)} custom-call(s32[4]{0:T(128)} %pad_add_fusion.ids, bf16[512,1024]{1,0:T(8,128)(2,1)} %cot.5, bf16[8192,1024]{1,0:T(8,128)(2,1)} %weight.1), custom_call_target="tpu_custom_call" | custom-call | flops 1 | bytes 1 | tf_op jit(solution)/shard_map/local_products/pallas_call | solution.py:194
  16.0 1.5 constant_dynamic-slice_fusion
  17.5 8.2 %collective-permute-done.2.refs_1_.refs_6_ = bf16[2,64,3072]{2,1,0:T(8,128)(2,1)S(1)} collective-permute-done((bf16[2,64,3072]{2,1,0:T(8,128)(2,1)S(1)}, bf16[2,64,3072]{2,1,0:T(8,128)(2,1)S(1)}, u32[]{:S(2)}, u32[]{:S(2)}) %collective-permute-start.2) | collective-permute-done | bytes 786464 | tf_op jit(solution)/shard_map/table1_0/ppermute | solution.py:23
  25.6 1.5 collective-permute-done.refs_0_
  27.7 4.8 %collective-permute-start.3 = (bf16[256,1024]{1,0:T(8,128)(2,1)S(1)}, bf16[256,1024]{1,0:T(8,128)(2,1)S(1)}, u32[]{:S(2)}, u32[]{:S(2)}) collective-permute-start(bf16[256,1024]{1,0:T(8,128)(2,1)S(1)} %get-tuple-element.47), channel_id=1, source_target_pairs={{0,1},{1,0},{2,3},{3,2},{4,5},{5,4},{6,7},{7,6},{8,9},{9,8},{10,11... | collective-permute-start | bytes 1572872 | tf_op jit(solution)/shard_map/piece1/ppermute | solution.py:23
  32.5 2.6 %collective-permute-start.4 = (bf16[256,1024]{1,0:T(8,128)(2,1)S(1)}, bf16[256,1024]{1,0:T(8,128)(2,1)S(1)}, u32[]{:S(2)}, u32[]{:S(2)}) collective-permute-start(bf16[256,1024]{1,0:T(8,128)(2,1)S(1)} %get-tuple-element.48), channel_id=1, source_target_pairs={{0,3},{1,2},{2,1},{3,0},{4,7},{5,6},{6,5},{7,4},{8,11},{9,10},{10,... | collective-permute-start | bytes 1572872 | tf_op jit(solution)/shard_map/piece3/ppermute | solution.py:23
  36.9 6.2 %rank_partials.1 = bf16[512,128]{1,0:T(8,128)(2,1)} custom-call(s32[4]{0:T(128)} %pad_add_fusion.ids, s32[16]{0:T(128)} %owner.9, s32[8]{0:T(128)} %counts.7, bf16[512,2048]{1,0:T(8,128)(2,1)} %hid.3, bf16[512,1024]{1,0:T(8,128)(2,1)} %cot.5, bf16[2,64,3072]{2,1,0:T(8,128)(2,1)} %copy-done, bf16[2,64,3072]{2,1,0:T(8,128)(2,1)} %copy-done.4, ...), custom_call_target="tpu_custom_call" | custom-call | flops 1 | bytes 1 | tf_op jit(solution)/shard_map/rank_partials/pallas_call | solution.py:90
  43.1 1.7 collective-permute-start.8
  44.8 2.6 %collective-permute-start.9 = (bf16[512,128]{1,0:T(8,128)(2,1)}, bf16[512,128]{1,0:T(8,128)(2,1)S(1)}, u32[]{:S(2)}, u32[]{:S(2)}) collective-permute-start(bf16[512,128]{1,0:T(8,128)(2,1)} %rank_partials.1), channel_id=1, source_target_pairs={{0,3},{1,2},{2,1},{3,0},{4,7},{5,6},{6,5},{7,4},{8,11},{9,10},{10,... | collective-permute-start | bytes 393224 | tf_op jit(solution)/shard_map/ranks3/ppermute | solution.py:23
  47.5 14.8 %collective-permute-done.7 = bf16[512,128]{1,0:T(8,128)(2,1)S(1)} collective-permute-done((bf16[512,128]{1,0:T(8,128)(2,1)}, bf16[512,128]{1,0:T(8,128)(2,1)S(1)}, u32[]{:S(2)}, u32[]{:S(2)}) %collective-permute-start.7) | collective-permute-done | bytes 131104 | tf_op jit(solution)/shard_map/ranks1/ppermute | solution.py:23
  62.3 4.4 %collective-permute-done.9 = bf16[512,128]{1,0:T(8,128)(2,1)S(1)} collective-permute-done((bf16[512,128]{1,0:T(8,128)(2,1)}, bf16[512,128]{1,0:T(8,128)(2,1)S(1)}, u32[]{:S(2)}, u32[]{:S(2)}) %collective-permute-start.9) | collective-permute-done | bytes 131104 | tf_op jit(solution)/shard_map/ranks3/ppermute | solution.py:23
  66.7 1.6 add_convert_fusion.both.refs_9_
  70.3 1.6 collective-permute-start.13
  72.4 7.6 %member_grads.1 = (bf16[4,64,3072]{2,1,0:T(8,128)(2,1)}, bf16[4,64,3072]{2,1,0:T(8,128)(2,1)}) custom-call(s32[4]{0:T(128)} %pad_add_fusion.ids, s32[16]{0:T(128)} %owner.9, bf16[512,2048]{1,0:T(8,128)(2,1)} %hid.3, bf16[512,1024]{1,0:T(8,128)(2,1)} %cot.5, bf16[512,128]{1,0:T(8,128)(2,1)} %add_convert_fusion.both.refs_9_), custom_call_target="tpu_custom_call" | custom-call | flops 1 | bytes 1 | tf_op jit(solution)/shard_map/member_grads/pallas_call | solution.py:139
  80.1 5.1 %collective-permute-done.12 = bf16[256,1024]{1,0:T(8,128)(2,1)S(1)} collective-permute-done((bf16[256,1024]{1,0:T(8,128)(2,1)S(1)}, bf16[256,1024]{1,0:T(8,128)(2,1)S(1)}, u32[]{:S(2)}, u32[]{:S(2)}) %collective-permute-start.12) | collective-permute-done | bytes 524320 | tf_op jit(solution)/shard_map/turn_a1/ppermute | solution.py:23
  85.3 9.7 %collective-permute-done.10 = bf16[512,1024]{1,0:T(8,128)(2,1)S(1)} collective-permute-done((bf16[512,1024]{1,0:T(8,128)(2,1)}, bf16[512,1024]{1,0:T(8,128)(2,1)S(1)}, u32[]{:S(2)}, u32[]{:S(2)}) %collective-permute-start.10) | collective-permute-done | bytes 1048608 | tf_op jit(solution)/shard_map/inner_out/ppermute | solution.py:23
  95.0 1.4 collective-permute-start.16
  98.4 4.7 %collective-permute-start.14 = (bf16[256,1024]{1,0:T(8,128)(2,1)S(1)}, bf16[256,1024]{1,0:T(8,128)(2,1)S(1)}, u32[]{:S(2)}, u32[]{:S(2)}) collective-permute-start(bf16[256,1024]{1,0:T(8,128)(2,1)S(1)} %get-tuple-element.58), channel_id=1, source_target_pairs={{0,2},{1,3},{2,0},{3,1},{4,6},{5,7},{6,4},{7,5},{8,10},{9,11},{10,... | collective-permute-start | bytes 1572872 | tf_op jit(solution)/shard_map/piece2/ppermute | solution.py:23
  104.2 8.1 %collective-permute-done.15 = bf16[256,1024]{1,0:T(8,128)(2,1)S(1)} collective-permute-done((bf16[256,1024]{1,0:T(8,128)(2,1)S(1)}, bf16[256,1024]{1,0:T(8,128)(2,1)S(1)}, u32[]{:S(2)}, u32[]{:S(2)}) %collective-permute-start.15) | collective-permute-done | bytes 524320 | tf_op jit(solution)/shard_map/outer_in_out0/ppermute | solution.py:23
  112.3 12.4 %collective-permute-done.14 = bf16[256,1024]{1,0:T(8,128)(2,1)S(1)} collective-permute-done((bf16[256,1024]{1,0:T(8,128)(2,1)S(1)}, bf16[256,1024]{1,0:T(8,128)(2,1)S(1)}, u32[]{:S(2)}, u32[]{:S(2)}) %collective-permute-start.14) | collective-permute-done | bytes 524320 | tf_op jit(solution)/shard_map/piece2/ppermute | solution.py:23
  125.4 1.5 collective-permute-start.18
  127.0 7.6 %collective-permute-done.18 = bf16[256,1024]{1,0:T(8,128)(2,1)S(1)} collective-permute-done((bf16[256,1024]{1,0:T(8,128)(2,1)S(1)}, bf16[256,1024]{1,0:T(8,128)(2,1)S(1)}, u32[]{:S(2)}, u32[]{:S(2)}) %collective-permute-start.18) | collective-permute-done | bytes 524320 | tf_op jit(solution)/shard_map/turn_a2/ppermute | solution.py:23
  134.7 1.5 collective-permute-start.22
  137.1 1.6 collective-permute-start.23
  138.7 12.6 %fold.1.acc = f32[512,2048]{1,0:T(8,128)} custom-call(s32[4]{0:T(128)} %pad_add_fusion.ids, s32[16]{0:T(128)} %owner.9, s32[8]{0:T(128)} %counts.7, f32[512,2048]{1,0:T(8,128)} %local_products.1.acc, bf16[512,1024]{1,0:T(8,128)(2,1)} %copy-done.9, bf16[512,1024]{1,0:T(8,128)(2,1)} %copy-done.2, ...), custom_call_target="tpu_custom_call", output_to_operand_aliasing={{}: (3, {})} | custom-call | flops 1 | bytes 1 | tf_op jit(solution)/shard_map/fold/pallas_call | solution.py:279
  151.3 2.0 %convert_add_fusion = f32[4,64,3072]{2,1,0:T(8,128)S(1)} fusion(bf16[4,64,3072]{2,1,0:T(8,128)(2,1)} %copy-done.8, bf16[4,64,3072]{2,1,0:T(8,128)(2,1)S(1)} %copy-done.7), kind=kLoop, calls=%fused_computation | loop fusion | flops 2359296 | bytes 6291456 | tf_op jit(solution)/shard_map/add | solution.py:416
  155.7 2.4 %maximum_select_fusion.refs_1_ = bf16[512,1024]{1,0:T(8,128)(2,1)} fusion(bf16[512,1024]{1,0:T(8,128)(2,1)} %collective-permute-done.1, bf16[256,1024]{1,0:T(8,128)(2,1)} %collective-permute-done.23, bf16[256,1024]{1,0:T(8,128)(2,1)S(1)} %copy-done.16, pred[]{:T(512)S(6)} %and.16), kind=kLoop, calls=%fused_computation.7 | loop fusion | flops 2621440 | bytes 3145729 | tf_op jit(solution)/shard_map/jit(_where)/select_n | solution.py:426
  158.1 7.3 %finish.2.refs_6_ = bf16[512,2048]{1,0:T(8,128)(2,1)} custom-call(s32[4]{0:T(128)} %pad_add_fusion.ids, s32[16]{0:T(128)} %owner.9, s32[8]{0:T(128)} %counts.7, f32[512,2048]{1,0:T(8,128)} %fold.1.acc, bf16[512,1024]{1,0:T(8,128)(2,1)} %broadcast_select_fusion.refs_0_, bf16[512,1024]{1,0:T(8,128)(2,1)} %maximum_select_fusion.refs_1_, ...), custom_call_target="tpu_custom_call" | custom-call | flops 1 | bytes 1 | tf_op jit(solution)/shard_map/finish/pallas_call | solution.py:279
  167.4 7.3 %finish.3 = bf16[512,2048]{1,0:T(8,128)(2,1)} custom-call(s32[4]{0:T(128)} %pad_add_fusion.ids, s32[16]{0:T(128)} %owner.9, s32[8]{0:T(128)} %counts.7, f32[512,2048]{1,0:T(8,128)} %fold.1.acc, bf16[512,1024]{1,0:T(8,128)(2,1)} %broadcast_select_fusion.refs_0_, bf16[512,1024]{1,0:T(8,128)(2,1)} %maximum_select_fusion.refs_1_, ...), custom_call_target="tpu_custom_call", output_to_operand_aliasing={{}: (10, {})} | custom-call | flops 1 | bytes 1 | tf_op jit(solution)/shard_map/finish/pallas_call | solution.py:279
  (84 shorter events, 18.0 us)
Async XLA Ops:
  0.6 26.5 %collective-permute-start = (bf16[512,1024]{1,0:T(8,128)(2,1)}, bf16[512,1024]{1,0:T(8,128)(2,1)S(1)}, u32[]{:S(2)}, u32[]{:S(2)}) collective-permute-start(bf16[512,1024]{1,0:T(8,128)(2,1)} %cot.5), channel_id=1, source_target_pairs={{0,1},{1,0},{2,3},{3,2},{4,5},{5,4},{6,7},{7,6},{8,9},{9,8},{10,11... | collective-permute-start | bytes 3145736 | tf_op jit(solution)/shard_map/outer/ppermute | solution.py:23
  3.7 23.4 %collective-permute-start.1 = (bf16[512,1024]{1,0:T(8,128)(2,1)}, bf16[512,1024]{1,0:T(8,128)(2,1)}, u32[]{:S(2)}, u32[]{:S(2)}) collective-permute-start(bf16[512,1024]{1,0:T(8,128)(2,1)} %cot.5), channel_id=1, source_target_pairs={{1,2},{2,1},{5,6},{6,5},{9,10},{10,9},{13,14},{14,13},{17,18},{18,... | collective-permute-start | bytes 3145736 | tf_op jit(solution)/shard_map/inner/ppermute | solution.py:23
  6.6 19.1 %collective-permute-start.2 = (bf16[2,64,3072]{2,1,0:T(8,128)(2,1)S(1)}, bf16[2,64,3072]{2,1,0:T(8,128)(2,1)S(1)}, u32[]{:S(2)}, u32[]{:S(2)}) collective-permute-start(bf16[2,64,3072]{2,1,0:T(8,128)(2,1)S(1)} %pad_maximum_fusion.3.refs_0_.refs_5_), channel_id=1, source_target_pairs={{0,8},{4,12},{8,0},{12,4},{1,9},{5,13},{9,1},{13,5},{2,10},{6,14},... | collective-permute-start | bytes 2359304 | tf_op jit(solution)/shard_map/table1_0/ppermute | solution.py:23
  27.1 58.2 %copy-start.9 = (bf16[512,1024]{1,0:T(8,128)(2,1)}, bf16[512,1024]{1,0:T(8,128)(2,1)S(1)}, u32[]{:S(2)}) copy-start(bf16[512,1024]{1,0:T(8,128)(2,1)S(1)} %collective-permute-done.refs_0_) | copy-start | bytes 3145732
  27.1 8.0 %collective-permute-start.5 = (bf16[2,64,3072]{2,1,0:T(8,128)(2,1)S(1)}, bf16[2,64,3072]{2,1,0:T(8,128)(2,1)S(1)}, u32[]{:S(2)}, u32[]{:S(2)}) collective-permute-start(bf16[2,64,3072]{2,1,0:T(8,128)(2,1)S(1)} %pad_maximum_fusion.3.refs_0_.refs_5_), channel_id=1, source_target_pairs={{0,4},{4,0},{8,12},{12,8},{1,5},{5,1},{9,13},{13,9},{2,6},{6,2},{1... | collective-permute-start | bytes 2359304 | tf_op jit(solution)/shard_map/table0_0/ppermute | solution.py:23
  27.2 7.9 %collective-permute-start.6 = (bf16[2,64,3072]{2,1,0:T(8,128)(2,1)S(1)}, bf16[2,64,3072]{2,1,0:T(8,128)(2,1)S(1)}, u32[]{:S(2)}, u32[]{:S(2)}) collective-permute-start(bf16[2,64,3072]{2,1,0:T(8,128)(2,1)S(1)} %collective-permute-done.2.refs_1_.refs_6_), channel_id=1, source_target_pairs={{0,4},{4,0},{8,12},{12,8},{1,5},{5,1},{9,13},{13,9},{2,6},{6,2},{1... | collective-permute-start | bytes 2359304 | tf_op jit(solution)/shard_map/table0_1/ppermute | solution.py:23
  27.7 40.6 %collective-permute-start.3 = (bf16[256,1024]{1,0:T(8,128)(2,1)S(1)}, bf16[256,1024]{1,0:T(8,128)(2,1)S(1)}, u32[]{:S(2)}, u32[]{:S(2)}) collective-permute-start(bf16[256,1024]{1,0:T(8,128)(2,1)S(1)} %get-tuple-element.47), channel_id=1, source_target_pairs={{0,1},{1,0},{2,3},{3,2},{4,5},{5,4},{6,7},{7,6},{8,9},{9,8},{10,11... | collective-permute-start | bytes 1572872 | tf_op jit(solution)/shard_map/piece1/ppermute | solution.py:23
  32.5 35.8 %collective-permute-start.4 = (bf16[256,1024]{1,0:T(8,128)(2,1)S(1)}, bf16[256,1024]{1,0:T(8,128)(2,1)S(1)}, u32[]{:S(2)}, u32[]{:S(2)}) collective-permute-start(bf16[256,1024]{1,0:T(8,128)(2,1)S(1)} %get-tuple-element.48), channel_id=1, source_target_pairs={{0,3},{1,2},{2,1},{3,0},{4,7},{5,6},{6,5},{7,4},{8,11},{9,10},{10,... | collective-permute-start | bytes 1572872 | tf_op jit(solution)/shard_map/piece3/ppermute | solution.py:23
  43.1 19.2 %collective-permute-start.7 = (bf16[512,128]{1,0:T(8,128)(2,1)}, bf16[512,128]{1,0:T(8,128)(2,1)S(1)}, u32[]{:S(2)}, u32[]{:S(2)}) collective-permute-start(bf16[512,128]{1,0:T(8,128)(2,1)} %rank_partials.1), channel_id=1, source_target_pairs={{0,1},{1,0},{2,3},{3,2},{4,5},{5,4},{6,7},{7,6},{8,9},{9,8},{10,11... | collective-permute-start | bytes 393224 | tf_op jit(solution)/shard_map/ranks1/ppermute | solution.py:23
  43.1 19.2 %collective-permute-start.8 = (bf16[512,128]{1,0:T(8,128)(2,1)}, bf16[512,128]{1,0:T(8,128)(2,1)S(1)}, u32[]{:S(2)}, u32[]{:S(2)}) collective-permute-start(bf16[512,128]{1,0:T(8,128)(2,1)} %rank_partials.1), channel_id=1, source_target_pairs={{0,2},{1,3},{2,0},{3,1},{4,6},{5,7},{6,4},{7,5},{8,10},{9,11},{10,... | collective-permute-start | bytes 393224 | tf_op jit(solution)/shard_map/ranks2/ppermute | solution.py:23
  44.8 21.8 %collective-permute-start.9 = (bf16[512,128]{1,0:T(8,128)(2,1)}, bf16[512,128]{1,0:T(8,128)(2,1)S(1)}, u32[]{:S(2)}, u32[]{:S(2)}) collective-permute-start(bf16[512,128]{1,0:T(8,128)(2,1)} %rank_partials.1), channel_id=1, source_target_pairs={{0,3},{1,2},{2,1},{3,0},{4,7},{5,6},{6,5},{7,4},{8,11},{9,10},{10,... | collective-permute-start | bytes 393224 | tf_op jit(solution)/shard_map/ranks3/ppermute | solution.py:23
  68.3 26.7 %collective-permute-start.10 = (bf16[512,1024]{1,0:T(8,128)(2,1)}, bf16[512,1024]{1,0:T(8,128)(2,1)S(1)}, u32[]{:S(2)}, u32[]{:S(2)}) collective-permute-start(bf16[512,1024]{1,0:T(8,128)(2,1)} %collective-permute-done.1), channel_id=1, source_target_pairs={{1,0},{2,3},{5,4},{6,7},{9,8},{10,11},{13,12},{14,15},{17,16},{18,... | collective-permute-start | bytes 3145736 | tf_op jit(solution)/shard_map/inner_out/ppermute | solution.py:23
  69.6 25.4 %collective-permute-start.11 = (bf16[512,1024]{1,0:T(8,128)(2,1)S(1)}, bf16[512,1024]{1,0:T(8,128)(2,1)S(1)}, u32[]{:S(2)}, u32[]{:S(2)}) collective-permute-start(bf16[512,1024]{1,0:T(8,128)(2,1)S(1)} %collective-permute-done.refs_0_), channel_id=1, source_target_pairs={{1,2},{2,1},{5,6},{6,5},{9,10},{10,9},{13,14},{14,13},{17,18},{18,... | collective-permute-start | bytes 3145736 | tf_op jit(solution)/shard_map/outer_in/ppermute | solution.py:23
  70.3 9.7 %collective-permute-start.13 = (bf16[256,1024]{1,0:T(8,128)(2,1)S(1)}, bf16[256,1024]{1,0:T(8,128)(2,1)S(1)}, u32[]{:S(2)}, u32[]{:S(2)}) collective-permute-start(bf16[256,1024]{1,0:T(8,128)(2,1)S(1)} %collective-permute-done.4), channel_id=1, source_target_pairs={{0,16},{4,12},{8,24},{12,4},{16,0},{20,28},{24,8},{28,20},{1,17},{... | collective-permute-start | bytes 1572872 | tf_op jit(solution)/shard_map/turn_a3/ppermute | solution.py:23
  71.9 13.3 %collective-permute-start.12 = (bf16[256,1024]{1,0:T(8,128)(2,1)S(1)}, bf16[256,1024]{1,0:T(8,128)(2,1)S(1)}, u32[]{:S(2)}, u32[]{:S(2)}) collective-permute-start(bf16[256,1024]{1,0:T(8,128)(2,1)S(1)} %collective-permute-done.3), channel_id=1, source_target_pairs={{0,16},{4,12},{8,24},{12,4},{16,0},{20,28},{24,8},{28,20},{1,17},{... | collective-permute-start | bytes 1572872 | tf_op jit(solution)/shard_map/turn_a1/ppermute | solution.py:23
  80.1 46.8 %copy-start.1 = (bf16[512,1024]{1,0:T(8,128)(2,1)}, bf16[512,1024]{1,0:T(8,128)(2,1)S(1)}, u32[]{:S(2)}) copy-start(bf16[512,1024]{1,0:T(8,128)(2,1)S(1)} %pad_maximum_fusion.1.refs_4_) | copy-start | bytes 3145732
  85.3 39.5 %copy-start.2 = (bf16[512,1024]{1,0:T(8,128)(2,1)}, bf16[512,1024]{1,0:T(8,128)(2,1)S(1)}, u32[]{:S(2)}) copy-start(bf16[512,1024]{1,0:T(8,128)(2,1)S(1)} %pad_maximum_fusion.refs_1_) | copy-start | bytes 3145732
  95.0 29.7 %collective-permute-start.16 = (bf16[512,1024]{1,0:T(8,128)(2,1)S(1)}, bf16[512,1024]{1,0:T(8,128)(2,1)S(1)}, u32[]{:S(2)}, u32[]{:S(2)}) collective-permute-start(bf16[512,1024]{1,0:T(8,128)(2,1)S(1)} %pad_maximum_fusion.refs_1_), channel_id=1, source_target_pairs={{0,8},{4,20},{8,0},{12,28},{16,24},{20,4},{24,16},{28,12},{1,9},{5... | collective-permute-start | bytes 3145736 | tf_op jit(solution)/shard_map/turn_b1/ppermute | solution.py:23
  96.5 28.2 %collective-permute-start.17 = (bf16[512,1024]{1,0:T(8,128)(2,1)S(1)}, bf16[512,1024]{1,0:T(8,128)(2,1)}, u32[]{:S(2)}, u32[]{:S(2)}) collective-permute-start(bf16[512,1024]{1,0:T(8,128)(2,1)S(1)} %pad_maximum_fusion.1.refs_4_), channel_id=1, source_target_pairs={{0,8},{4,20},{8,0},{12,28},{16,24},{20,4},{24,16},{28,12},{1,9},{5... | collective-permute-start | bytes 3145736 | tf_op jit(solution)/shard_map/turn_b3/ppermute | solution.py:23
  97.1 15.2 %collective-permute-start.15 = (bf16[256,1024]{1,0:T(8,128)(2,1)S(1)}, bf16[256,1024]{1,0:T(8,128)(2,1)S(1)}, u32[]{:S(2)}, u32[]{:S(2)}) collective-permute-start(bf16[256,1024]{1,0:T(8,128)(2,1)S(1)} %slice.19), channel_id=1, source_target_pairs={{1,0},{2,3},{5,4},{6,7},{9,8},{10,11},{13,12},{14,15},{17,16},{18,... | collective-permute-start | bytes 1572872 | tf_op jit(solution)/shard_map/outer_in_out0/ppermute | solution.py:23
  98.4 26.3 %collective-permute-start.14 = (bf16[256,1024]{1,0:T(8,128)(2,1)S(1)}, bf16[256,1024]{1,0:T(8,128)(2,1)S(1)}, u32[]{:S(2)}, u32[]{:S(2)}) collective-permute-start(bf16[256,1024]{1,0:T(8,128)(2,1)S(1)} %get-tuple-element.58), channel_id=1, source_target_pairs={{0,2},{1,3},{2,0},{3,1},{4,6},{5,7},{6,4},{7,5},{8,10},{9,11},{10,... | collective-permute-start | bytes 1572872 | tf_op jit(solution)/shard_map/piece2/ppermute | solution.py:23
  124.7 10.0 %collective-permute-start.21 = (bf16[4,64,3072]{2,1,0:T(8,128)(2,1)S(1)}, bf16[4,64,3072]{2,1,0:T(8,128)(2,1)S(1)}, u32[]{:S(2)}, u32[]{:S(2)}) collective-permute-start(bf16[4,64,3072]{2,1,0:T(8,128)(2,1)S(1)} %copy-done.17), channel_id=1, source_target_pairs={{0,4},{4,0},{8,12},{12,8},{1,5},{5,1},{9,13},{13,9},{2,6},{6,2},{1... | collective-permute-start | bytes 4718600 | tf_op jit(solution)/shard_map/grads0/ppermute | solution.py:23
  124.8 9.8 %collective-permute-start.19 = (bf16[512,1024]{1,0:T(8,128)(2,1)S(1)}, bf16[512,1024]{1,0:T(8,128)(2,1)S(1)}, u32[]{:S(2)}, u32[]{:S(2)}) collective-permute-start(bf16[512,1024]{1,0:T(8,128)(2,1)S(1)} %pad_maximum_fusion.refs_1_), channel_id=1, source_target_pairs={{0,4},{4,0},{8,12},{12,8},{16,20},{20,16},{24,28},{28,24},{1,5},{5... | collective-permute-start | bytes 3145736 | tf_op jit(solution)/shard_map/turn_c10/ppermute | solution.py:23
  125.3 9.4 %collective-permute-start.20 = (bf16[512,1024]{1,0:T(8,128)(2,1)S(1)}, bf16[512,1024]{1,0:T(8,128)(2,1)S(1)}, u32[]{:S(2)}, u32[]{:S(2)}) collective-permute-start(bf16[512,1024]{1,0:T(8,128)(2,1)S(1)} %collective-permute-done.16.refs_2_), channel_id=1, source_target_pairs={{0,4},{4,0},{8,12},{12,8},{16,20},{20,16},{24,28},{28,24},{1,5},{5... | collective-permute-start | bytes 3145736 | tf_op jit(solution)/shard_map/turn_c11/ppermute | solution.py:23
  125.4 9.2 %collective-permute-start.18 = (bf16[256,1024]{1,0:T(8,128)(2,1)S(1)}, bf16[256,1024]{1,0:T(8,128)(2,1)S(1)}, u32[]{:S(2)}, u32[]{:S(2)}) collective-permute-start(bf16[256,1024]{1,0:T(8,128)(2,1)S(1)} %collective-permute-done.14), channel_id=1, source_target_pairs={{0,16},{4,12},{8,24},{12,4},{16,0},{20,28},{24,8},{28,20},{1,17},{... | collective-permute-start | bytes 1572872 | tf_op jit(solution)/shard_map/turn_a2/ppermute | solution.py:23
  126.9 26.8 %collective-permute-start.24 = (bf16[512,1024]{1,0:T(8,128)(2,1)S(1)}, bf16[512,1024]{1,0:T(8,128)(2,1)}, u32[]{:S(2)}, u32[]{:S(2)}) collective-permute-start(bf16[512,1024]{1,0:T(8,128)(2,1)S(1)} %pad_maximum_fusion.1.refs_4_), channel_id=1, source_target_pairs={{0,4},{4,0},{8,12},{12,8},{16,20},{20,16},{24,28},{28,24},{1,5},{5... | collective-permute-start | bytes 3145736 | tf_op jit(solution)/shard_map/turn_c30/ppermute | solution.py:23
  134.6 19.1 %collective-permute-start.25 = (bf16[512,1024]{1,0:T(8,128)(2,1)}, bf16[512,1024]{1,0:T(8,128)(2,1)}, u32[]{:S(2)}, u32[]{:S(2)}) collective-permute-start(bf16[512,1024]{1,0:T(8,128)(2,1)} %collective-permute-done.17.refs_5_), channel_id=1, source_target_pairs={{0,4},{4,0},{8,12},{12,8},{16,20},{20,16},{24,28},{28,24},{1,5},{5... | collective-permute-start | bytes 3145736 | tf_op jit(solution)/shard_map/turn_c31/ppermute | solution.py:23
  134.7 19.0 %collective-permute-start.22 = (bf16[512,1024]{1,0:T(8,128)(2,1)S(1)}, bf16[512,1024]{1,0:T(8,128)(2,1)}, u32[]{:S(2)}, u32[]{:S(2)}) collective-permute-start(bf16[512,1024]{1,0:T(8,128)(2,1)S(1)} %pad_maximum_fusion.2.refs_2_), channel_id=1, source_target_pairs={{0,8},{4,20},{8,0},{12,28},{16,24},{20,4},{24,16},{28,12},{1,9},{5... | collective-permute-start | bytes 3145736 | tf_op jit(solution)/shard_map/turn_b2/ppermute | solution.py:23
  137.1 16.6 %collective-permute-start.23 = (bf16[256,1024]{1,0:T(8,128)(2,1)}, bf16[256,1024]{1,0:T(8,128)(2,1)}, u32[]{:S(2)}, u32[]{:S(2)}) collective-permute-start(bf16[256,1024]{1,0:T(8,128)(2,1)} %slice.20), channel_id=1, source_target_pairs={{1,0},{2,3},{5,4},{6,7},{9,8},{10,11},{13,12},{14,15},{17,16},{18,... | collective-permute-start | bytes 1572872 | tf_op jit(solution)/shard_map/outer_in_out1/ppermute | solution.py:23
  153.7 11.7 %collective-permute-start.26 = (bf16[512,1024]{1,0:T(8,128)(2,1)S(1)}, bf16[512,1024]{1,0:T(8,128)(2,1)S(1)}, u32[]{:S(2)}, u32[]{:S(2)}) collective-permute-start(bf16[512,1024]{1,0:T(8,128)(2,1)S(1)} %pad_maximum_fusion.2.refs_2_), channel_id=1, source_target_pairs={{0,4},{4,0},{8,12},{12,8},{16,20},{20,16},{24,28},{28,24},{1,5},{5... | collective-permute-start | bytes 3145736 | tf_op jit(solution)/shard_map/turn_c20/ppermute | solution.py:23
  154.0 11.5 %collective-permute-start.27 = (bf16[512,1024]{1,0:T(8,128)(2,1)}, bf16[512,1024]{1,0:T(8,128)(2,1)S(1)}, u32[]{:S(2)}, u32[]{:S(2)}) collective-permute-start(bf16[512,1024]{1,0:T(8,128)(2,1)} %collective-permute-done.22.refs_3_), channel_id=1, source_target_pairs={{0,4},{4,0},{8,12},{12,8},{16,20},{20,16},{24,28},{28,24},{1,5},{5... | collective-permute-start | bytes 3145736 | tf_op jit(solution)/shard_map/turn_c21/ppermute | solution.py:23
  154.3 20.4 %collective-permute-start.28 = (bf16[2,64,3072]{2,1,0:T(8,128)(2,1)S(1)}, bf16[2,64,3072]{2,1,0:T(8,128)(2,1)S(1)}, u32[]{:S(2)}, u32[]{:S(2)}) collective-permute-start(bf16[2,64,3072]{2,1,0:T(8,128)(2,1)S(1)} %slice.32), channel_id=1, source_target_pairs={{0,8},{4,12},{8,0},{12,4},{1,9},{5,13},{9,1},{13,5},{2,10},{6,14},... | collective-permute-start | bytes 2359304 | tf_op jit(solution)/shard_map/grads1/ppermute | solution.py:23
  (15 other events, 150.1 us)

commit v3 on v2

--- a/solution.py
+++ b/solution.py
@@ -12,7 +12,6 @@
 TILE = 2 * PIECE
 BF = jnp.bfloat16
 F32 = jnp.float32
-VMEM_LIMIT = 56 * 2**20
 
 
 CHEAP = pl.CostEstimate(flops=1, bytes_accessed=1, transcendentals=0)
@@ -39,8 +38,8 @@
     return lax.dot_general(a, b, (((0,), (0,)), ((), ())), preferred_element_type=F32)
 
 
-def params():
-    return pltpu.CompilerParams(vmem_limit_bytes=VMEM_LIMIT)
+def params(mib):
+    return pltpu.CompilerParams(vmem_limit_bytes=mib * 2**20)
 
 
 def slot_of(block, ids, owner, *, blocks, owned, bits):
@@ -100,13 +99,14 @@
             out_specs=pl.BlockSpec((BLK, 2 * rank), lambda b, *s: (b, 0)),
         ),
         out_shape=jax.ShapeDtypeStruct((blocks * BLK, 2 * rank), BF),
-        compiler_params=params(),
+        compiler_params=params(16),
         cost_estimate=CHEAP,
         name="rank_partials",
     )(ids, owner, counts, hidden, cotan, *table)
 
 
-def grads_kernel(ids, owner, hid, cot, both, send, keep, acc, *, width, blocks, slot, half):
+def grads_kernel(ids, owner, hid, cot, both, *refs, width, blocks, slot, half):
+    sends, keep, acc = refs[:half], refs[half], refs[half + 1]
     step = pl.program_id(0)
     position = jnp.where(step < half, step + half, step - half)
     rank = both.shape[1] // 2
@@ -120,9 +120,11 @@
             acc[:, :width] += contract_first(pair[:, rank:].astype(BF), hid[at, :])
             acc[:, width:] += contract_first(pair[:, :rank].astype(BF), cot[at, :])
 
-    @pl.when(step < half)
-    def _():
-        send[0] = acc[...].astype(BF)
+    for i, send in enumerate(sends):
+
+        @pl.when(step == i)
+        def _(send=send):
+            send[0] = acc[...].astype(BF)
 
     @pl.when(step >= half)
     def _():
@@ -135,8 +137,8 @@
     rank = both.shape[1] // 2
     half = members // 2
     slot = functools.partial(slot_of, blocks=blocks, owned=owned, bits=bits)
-    shape = jax.ShapeDtypeStruct((half, rank, width + cols), BF)
-    return pl.pallas_call(
+    shape = lambda count: jax.ShapeDtypeStruct((count, rank, width + cols), BF)
+    *sends, keep = pl.pallas_call(
         functools.partial(
             grads_kernel, width=width, blocks=blocks, slot=slot, half=half
         ),
@@ -148,17 +150,16 @@
                 pl.BlockSpec((tokens, cols), lambda p, *s: (0, 0)),
                 pl.BlockSpec((tokens, 2 * rank), lambda p, *s: (0, 0)),
             ],
-            out_specs=[
-                pl.BlockSpec((1, rank, width + cols), lambda p, *s: (jnp.minimum(p, half - 1), 0, 0)),
-                pl.BlockSpec((1, rank, width + cols), lambda p, *s: (jnp.maximum(p - half, 0), 0, 0)),
-            ],
+            out_specs=[pl.BlockSpec((1, rank, width + cols), lambda p, *s: (0, 0, 0)) for _ in range(half)]
+            + [pl.BlockSpec((1, rank, width + cols), lambda p, *s: (jnp.maximum(p - half, 0), 0, 0))],
             scratch_shapes=[pltpu.VMEM((rank, width + cols), F32)],
         ),
-        out_shape=[shape, shape],
-        compiler_params=params(),
+        out_shape=[shape(1)] * half + [shape(half)],
+        compiler_params=params(16),
         cost_estimate=CHEAP,
         name="member_grads",
     )(ids, owner, hidden, cotan, both)
+    return sends, keep
 
 
 def relative_tile(p, ids):
@@ -203,7 +204,7 @@
             out_specs=pl.BlockSpec((tokens, TILE), lambda p, *s: (0, p)),
         ),
         out_shape=jax.ShapeDtypeStruct((tokens, width), F32),
-        compiler_params=params(),
+        compiler_params=params(16),
         cost_estimate=CHEAP,
         name="local_products",
     )(ids, cotan, weight)
@@ -294,7 +295,7 @@
         ),
         out_shape=jax.ShapeDtypeStruct((tokens, width), BF if final else F32),
         input_output_aliases=alias,
-        compiler_params=params(),
+        compiler_params=params(28),
         cost_estimate=CHEAP,
         name="finish" if final else "fold",
     )(*operands)
@@ -323,7 +324,6 @@
     owned = down.shape[0]
     share = width // (ng * nd)
     bits = tuple(range(nd.bit_length() - 2, -1, -1))
-    half = tokens // 2
     sizes = dict(blocks=tokens // BLK, owned=owned, bits=bits)
     fast = (ng, nd, n, share) == (2, 4, 4, PIECE)
 
@@ -361,7 +361,8 @@
     def grads(both):
         return member_grads(ids, owner, hidden, query_gradient, both, nd * owned, **sizes)
 
-    def grad_sum(send, keep):
+    def grad_sum(sends, keep):
+        send = jnp.concatenate(sends, axis=0)
         for bit in reversed(bits):
             total = keep.astype(F32) + swap(f"grads{bit}", send, "dp", nd, bit).astype(F32)
             if bit != bits[0]:
@@ -377,58 +378,53 @@
 
     table = [jnp.concatenate([jnp.swapaxes(down, 1, 2), up], axis=2)]
     if fast:
+        cuts = [cut(z ^ d) for d in (1, 2, 3)]
+        piece1, piece3 = piece(1, cuts[0]), piece(3, cuts[2])
+        table = more(bits[0], table)
+        acc = local()
+        piece1, piece3, cut2, table, acc = together(piece1, piece3, cuts[1], table, acc)
+
         by_one = move("outer", query_gradient, "tensor", outer)
         across = move("inner", query_gradient, "tensor", inner)
-        table = more(bits[0], table)
-        cuts = [cut(z ^ d) for d in (1, 2, 3)]
-        acc = local()
-        by_one, across, cuts, table, acc = together(by_one, across, cuts, table, acc)
-
-        piece1, piece3 = piece(1, cuts[0]), piece(3, cuts[2])
+        wide1 = turned("turn_a1", piece1, turn_a)
+        wide3 = turned("turn_a3", piece3, turn_a)
         table = more(bits[1], table)
         both = ranks(table)
         shares = [move(f"ranks{d}", both, "tensor", [(i, i ^ d) for i in range(n)]) for d in (1, 2, 3)]
         both = sum((a.astype(F32) for a in shares), both.astype(F32)).astype(BF)
-        by_one, across, piece1, piece3, both = together(by_one, across, piece1, piece3, both)
+        by_one, across, wide1, wide3, both, cut2 = together(by_one, across, wide1, wide3, both, cut2)
+
+        piece2 = piece(2, cut2)
+        wide1 = [wide1, move("turn_b1", wide1, copies, turn_b)]
+        wide3 = [wide3, move("turn_b3", wide3, copies, turn_b)]
+        sends, keep = grads(both)
+        rest = len(sends) // 2
+        got = [swap(f"grads0_{i}", one, "dp", nd, bits[1]) for i, one in enumerate(sends)]
+        by_one, across, piece2, wide1, wide3, far = together(by_one, across, piece2, wide1, wide3, got[rest:])
 
         end_two = move("inner_out", across, "tensor", outward)
         by_two = move("outer_in", by_one, "tensor", inner)
-        wide1 = turned("turn_a1", piece1, turn_a)
-        wide3 = turned("turn_a3", piece3, turn_a)
-        send, keep = grads(both)
-        end_two, by_two, wide1, wide3, send, cut2 = together(end_two, by_two, wide1, wide3, send, cuts[1])
-
-        piece2 = piece(2, cut2)
-        end_upper = move("outer_in_out0", by_two[:half], "tensor", outward)
-        wide1 = [wide1, move("turn_b1", wide1, copies, turn_b)]
-        wide3 = [wide3, move("turn_b3", wide3, copies, turn_b)]
+        wide2 = turned("turn_a2", piece2, turn_a)
+        far = keep[rest:].astype(F32) + jnp.concatenate(far, axis=0).astype(F32)
+        far = swap("grads1", far.astype(BF), "dp", nd, bits[0])
+        end_two, by_two, wide2, far = together(end_two, by_two, wide2, far)
+
+        end_three = move("outer_in_out", by_two, "tensor", outward)
+        wide2 = [wide2, move("turn_b2", wide2, copies, turn_b)]
+        other1 = [move(f"turn_c1{i}", part, copies, turn_c) for i, part in enumerate(wide1)]
+        acc = folded(acc, [by_one], [wide1 + other1], relative_tile, 0, table=table, both=both)
         two = jnp.where(middle, by_two, end_two)
-        piece2, end_upper, wide1, wide3, by_two, two, send = together(
-            piece2, end_upper, wide1, wide3, by_two, two, send
+        total = keep[:rest].astype(F32) + jnp.concatenate(got[:rest], axis=0).astype(F32) + far.astype(F32)
+        grad_down, grad_up = jnp.swapaxes(total[:, :, :width], 1, 2), total[:, :, width:]
+        wide2, acc, end_three, two, grad_down, grad_up = together(
+            wide2, acc, end_three, two, grad_down, grad_up
         )
 
-        wide2 = turned("turn_a2", piece2, turn_a)
-        other1 = [move(f"turn_c1{i}", part, copies, turn_c) for i, part in enumerate(wide1)]
-        got = swap("grads0", send, "dp", nd, bits[1])
-        wide2, other1, got = together(wide2, other1, got)
-
-        rest = got.shape[0] // 2
-        total = keep.astype(F32) + got.astype(F32)
-        send = total[rest:].astype(BF)
-        end_lower = move("outer_in_out1", by_two[half:], "tensor", outward)
-        wide2 = [wide2, move("turn_b2", wide2, copies, turn_b)]
+        other2 = [move(f"turn_c2{i}", part, copies, turn_c) for i, part in enumerate(wide2)]
         other3 = [move(f"turn_c3{i}", part, copies, turn_c) for i, part in enumerate(wide3)]
-        acc = folded(acc, [by_one], [wide1 + other1], relative_tile, 0, table=table, both=both)
-        wide2, acc, end_lower, other3, send = together(wide2, acc, end_lower, other3, send)
-
-        got = swap("grads1", send, "dp", nd, bits[0])
-        other2 = [move(f"turn_c2{i}", part, copies, turn_c) for i, part in enumerate(wide2)]
-        three = jnp.where(middle, across, jnp.concatenate([end_upper, end_lower], axis=0))
+        three = jnp.where(middle, across, end_three)
         result = folded(acc, [two, three], [wide2, wide3], relative_tile, 0, final=True)
         result = folded(acc, [two, three], [other2, other3], relative_tile, 2, before=result, final=True)
-        got = together(got, result)[0]
-        total = total[:rest] + got.astype(F32)
-        grad_down, grad_up = jnp.swapaxes(total[:, :, :width], 1, 2), total[:, :, width:]
     else:
         xs = line(query_gradient, n, z)
         wides = []

time: 178 us -> 165 us (0.927)
  Pallas kernels: 48.2 us -> 27.9 us
  waiting for transfers between devices: 72 us -> 82 us
  other arithmetic: 9.38 us -> 4.42 us
  local copies, waits for them, and re-layouts: 8.11 us -> 10.1 us
    ppermute x29 -> x31, waiting for transfers between devices: 72 us -> 82 us  [move(): return lax.ppermute(a, axis, pairs)]
    pallas_call x3, Pallas kernels: 27.2 us -> 17.6 us  [fold(): pl.pallas_call(functools.partial(fold_kernel, terms=len(xs), parts=parts,...]
    pallas_call x1, Pallas kernels: 7.57 us -> 3.43 us  [member_grads(): pl.pallas_call(functools.partial(grads_kernel, width=width, blocks=blocks...]
    pallas_call x1, Pallas kernels: 7.19 us -> 3.8 us  [local_products(): pl.pallas_call(local_kernel, grid_spec=pltpu.PrefetchScalarGridSpec(num_s...]
    pallas_call x1, Pallas kernels: 6.19 us -> 3 us  [rank_partials(): pl.pallas_call(functools.partial(rank_kernel, width=width, blocks=blocks,...]
    select_n x1, other arithmetic: 2.43 us -> 0.11 us  [body(): three = jnp.where(middle, across, end_three)]
    concatenate x3, other arithmetic: 0.21 us -> 2.29 us  [turned(): return jnp.concatenate([own, move(name, own, copies, pairs)], axis=0)]
    unnamed x36 -> x10, local copies, waits for them, and re-layouts: 3.78 us -> 5.79 us
  transfers between devices with their start and end apart: 29 -> 31, of which waited for: 10 -> 14; matrix products, arithmetic and copies ran while one was open for 7% -> 5% of each run, Pallas kernels for 27% -> 14%
where the time goes in v3:
time: 165 us; the launch traced here: 164 us
  waiting for transfers between devices  82 us (50%)
  starting transfers between devices  39 us (24%)
  Pallas kernels  27.9 us (17%)
  local copies, waits for them, and re-layouts  10.1 us (6%)
  other arithmetic  4.42 us (3%)
    ppermute x31, waiting for transfers between devices, move(): return lax.ppermute(a, axis, pairs)  82 us
    ppermute x31, starting transfers between devices, move(): return lax.ppermute(a, axis, pairs)  39 us
    pallas_call x3, Pallas kernels, fold(): pl.pallas_call(functools.partial(fold_kernel, terms=len(xs), parts=parts,...  17.6 us
    unnamed x10, local copies, waits for them, and re-layouts  5.79 us
    pallas_call x1, Pallas kernels, local_products(): pl.pallas_call(local_kernel, grid_spec=pltpu.PrefetchScalarGridSpec(num_s...  3.8 us
    pallas_call x1, Pallas kernels, member_grads(): pl.pallas_call(functools.partial(grads_kernel, width=width, blocks=blocks...  3.43 us
  transfers between devices with their start and end apart: 31, of which 14 were waited for; matrix products, arithmetic and copies ran while one was open for 5% of the time, Pallas kernels for 14%

profile of v3, /device:TPU:0, one launch (start us, length us, event | category | flops | bytes accessed | tf_op | source)
XLA Modules:
  0.0 164.3 jit_solution(9383145208869522408)
XLA Ops:
  0.6 1.3 pad_maximum_fusion.3.refs_0_.refs_5_
  1.9 3.0 %collective-permute-start.4 = (bf16[2,64,3072]{2,1,0:T(8,128)(2,1)S(1)}, bf16[2,64,3072]{2,1,0:T(8,128)(2,1)S(1)}, u32[]{:S(2)}, u32[]{:S(2)}) collective-permute-start(bf16[2,64,3072]{2,1,0:T(8,128)(2,1)S(1)} %pad_maximum_fusion.3.refs_0_.refs_5_), channel_id=1, source_target_pairs={{0,8},{4,12},{8,0},{12,4},{1,9},{5,13},{9,1},{13,5},{2,10},{6,14},... | collective-permute-start | bytes 2359304 | tf_op jit(solution)/shard_map/table1_0/ppermute | solution.py:22
  4.9 2.4 %constant_dynamic-slice_fusion = (bf16[256,1024]{1,0:T(8,128)(2,1)S(1)}, bf16[256,1024]{1,0:T(8,128)(2,1)}, bf16[256,1024]{1,0:T(8,128)(2,1)}) fusion(bf16[8192,1024]{1,0:T(8,128)(2,1)} %weight.1, s32[]{:T(128)S(6)} %select_n.40, s32[]{:T(128)S(6)} %select_n.39, s32[]{:T(128)S(6)} %select_n.38), kind=kLoop, calls=%fused_computation.10 | loop fusion | bytes 3145740 | tf_op jit(solution)/shard_map/dynamic_slice | solution.py:343
  7.4 1.6 collective-permute-start.2
  9.0 2.5 %collective-permute-start.3 = (bf16[256,1024]{1,0:T(8,128)(2,1)}, bf16[256,1024]{1,0:T(8,128)(2,1)}, u32[]{:S(2)}, u32[]{:S(2)}) collective-permute-start(bf16[256,1024]{1,0:T(8,128)(2,1)} %get-tuple-element.78), channel_id=1, source_target_pairs={{0,3},{1,2},{2,1},{3,0},{4,7},{5,6},{6,5},{7,4},{8,11},{9,10},{10,... | collective-permute-start | bytes 1572872 | tf_op jit(solution)/shard_map/piece3/ppermute | solution.py:22
  11.5 5.8 %copy-done = bf16[8192,1024]{1,0:T(8,128)(2,1)S(1)} copy-done((bf16[8192,1024]{1,0:T(8,128)(2,1)S(1)}, bf16[8192,1024]{1,0:T(8,128)(2,1)}, u32[]{:S(2)}) %copy-start) | copy-done | bytes 16777240
  17.3 3.8 %local_products.1.acc = f32[512,2048]{1,0:T(8,128)S(1)} custom-call(s32[4]{0:T(128)S(1)} %pad_add_fusion.ids, bf16[512,1024]{1,0:T(8,128)(2,1)S(1)} %copy-done.1, bf16[8192,1024]{1,0:T(8,128)(2,1)S(1)} %copy-done), custom_call_target="tpu_custom_call" | custom-call | flops 1 | bytes 1 | tf_op jit(solution)/shard_map/local_products/pallas_call | solution.py:195
  21.6 12.8 %collective-permute-done.3 = bf16[256,1024]{1,0:T(8,128)(2,1)} collective-permute-done((bf16[256,1024]{1,0:T(8,128)(2,1)}, bf16[256,1024]{1,0:T(8,128)(2,1)}, u32[]{:S(2)}, u32[]{:S(2)}) %collective-permute-start.3) | collective-permute-done | bytes 524320 | tf_op jit(solution)/shard_map/piece3/ppermute | solution.py:22
  34.5 1.5 collective-permute-start.6
  37.8 6.1 %collective-permute-done.6 = bf16[256,1024]{1,0:T(8,128)(2,1)S(1)} collective-permute-done((bf16[256,1024]{1,0:T(8,128)(2,1)}, bf16[256,1024]{1,0:T(8,128)(2,1)S(1)}, u32[]{:S(2)}, u32[]{:S(2)}) %collective-permute-start.6) | collective-permute-done | bytes 524320 | tf_op jit(solution)/shard_map/turn_a3/ppermute | solution.py:22
  43.9 1.5 collective-permute-start.5
  45.3 1.1 pad_maximum_fusion.1.refs_4_
  46.5 3.0 %rank_partials.1 = bf16[512,128]{1,0:T(8,128)(2,1)S(1)} custom-call(s32[4]{0:T(128)S(1)} %pad_add_fusion.ids, s32[16]{0:T(128)S(1)} %copy-done.3, s32[8]{0:T(128)S(1)} %copy-done.4, bf16[512,2048]{1,0:T(8,128)(2,1)S(1)} %copy-done.2, bf16[512,1024]{1,0:T(8,128)(2,1)S(1)} %copy-done.1, bf16[2,64,3072]{2,1,0:T(8,128)(2,1)S(1)} %pad_maximum_fusion.3.refs_0_.refs_5_, ...), custom_call_target="tpu_custom_call" | custom-call | flops 1 | bytes 1 | tf_op jit(solution)/shard_map/rank_partials/pallas_call | solution.py:89
  49.5 1.8 %collective-permute-start.10 = (bf16[512,128]{1,0:T(8,128)(2,1)S(1)}, bf16[512,128]{1,0:T(8,128)(2,1)S(1)}, u32[]{:S(2)}, u32[]{:S(2)}) collective-permute-start(bf16[512,128]{1,0:T(8,128)(2,1)S(1)} %rank_partials.1), channel_id=1, source_target_pairs={{0,2},{1,3},{2,0},{3,1},{4,6},{5,7},{6,4},{7,5},{8,10},{9,11},{10,... | collective-permute-start | bytes 393224 | tf_op jit(solution)/shard_map/ranks2/ppermute | solution.py:22
  51.3 1.2 collective-permute-start.11
  53.8 1.1 pad_maximum_fusion.refs_1_
  54.9 19.4 %collective-permute-done.10 = bf16[512,128]{1,0:T(8,128)(2,1)S(1)} collective-permute-done((bf16[512,128]{1,0:T(8,128)(2,1)S(1)}, bf16[512,128]{1,0:T(8,128)(2,1)S(1)}, u32[]{:S(2)}, u32[]{:S(2)}) %collective-permute-start.10) | collective-permute-done | bytes 131104 | tf_op jit(solution)/shard_map/ranks2/ppermute | solution.py:22
  75.0 1.5 collective-permute-start.14
  76.5 2.1 %collective-permute-start.12 = (bf16[256,1024]{1,0:T(8,128)(2,1)S(1)}, bf16[256,1024]{1,0:T(8,128)(2,1)S(1)}, u32[]{:S(2)}, u32[]{:S(2)}) collective-permute-start(bf16[256,1024]{1,0:T(8,128)(2,1)S(1)} %get-tuple-element.47), channel_id=1, source_target_pairs={{0,2},{1,3},{2,0},{3,1},{4,6},{5,7},{6,4},{7,5},{8,10},{9,11},{10,... | collective-permute-start | bytes 1572872 | tf_op jit(solution)/shard_map/piece2/ppermute | solution.py:22
  78.6 3.4 %member_grads.1 = (bf16[1,64,3072]{2,1,0:T(8,128)(2,1)S(1)}, bf16[1,64,3072]{2,1,0:T(8,128)(2,1)S(1)}, bf16[1,64,3072]{2,1,0:T(8,128)(2,1)S(1)}, bf16[1,64,3072]...) custom-call(s32[4]{0:T(128)S(1)} %pad_add_fusion.ids, s32[16]{0:T(128)S(1)} %copy-done.3, bf16[512,2048]{1,0:T(8,128)(2,1)S(1)} %copy-done.2, ...), custom_call_target="tpu_custom_call" | custom-call | flops 1 | bytes 1 | tf_op jit(solution)/shard_map/member_grads/pallas_call | solution.py:141
  82.6 1.2 collective-permute-done.15
  84.4 15.8 %collective-permute-done.12 = bf16[256,1024]{1,0:T(8,128)(2,1)S(1)} collective-permute-done((bf16[256,1024]{1,0:T(8,128)(2,1)S(1)}, bf16[256,1024]{1,0:T(8,128)(2,1)S(1)}, u32[]{:S(2)}, u32[]{:S(2)}) %collective-permute-start.12) | collective-permute-done | bytes 524320 | tf_op jit(solution)/shard_map/piece2/ppermute | solution.py:22
  100.5 1.3 collective-permute-start.17
  103.9 8.6 %collective-permute-done.19 = bf16[256,1024]{1,0:T(8,128)(2,1)S(1)} collective-permute-done((bf16[256,1024]{1,0:T(8,128)(2,1)S(1)}, bf16[256,1024]{1,0:T(8,128)(2,1)S(1)}, u32[]{:S(2)}, u32[]{:S(2)}) %collective-permute-start.19) | collective-permute-done | bytes 524320 | tf_op jit(solution)/shard_map/turn_a2/ppermute | solution.py:22
  112.5 12.3 %collective-permute-start.26 = (bf16[1,64,3072]{2,1,0:T(8,128)(2,1)S(1)}, bf16[1,64,3072]{2,1,0:T(8,128)(2,1)S(1)}, u32[]{:S(2)}, u32[]{:S(2)}) collective-permute-start(bf16[1,64,3072]{2,1,0:T(8,128)(2,1)S(1)} %get-tuple-element.66), channel_id=1, source_target_pairs={{0,4},{4,0},{8,12},{12,8},{1,5},{5,1},{9,13},{13,9},{2,6},{6,2},{1... | collective-permute-start | bytes 1179656 | tf_op jit(solution)/shard_map/grads0_1/ppermute | solution.py:22
  126.3 1.5 collective-permute-start.24
  129.2 9.2 %fold.1.acc = f32[512,2048]{1,0:T(8,128)S(1)} custom-call(s32[4]{0:T(128)S(1)} %pad_add_fusion.ids, s32[16]{0:T(128)S(1)} %copy-done.3, s32[8]{0:T(128)S(1)} %copy-done.4, f32[512,2048]{1,0:T(8,128)S(1)} %local_products.1.acc, bf16[512,1024]{1,0:T(8,128)(2,1)S(1)} %collective-permute-done.refs_0_, ...), custom_call_target="tpu_custom_call", output_to_operand_aliasing={{}: (3, {})} | custom-call | flops 1 | bytes 1 | tf_op jit(solution)/shard_map/fold/pallas_call | solution.py:280
  138.4 0.8 slice.17
  139.3 1.0 slice_bitcast_fusion
  140.6 14.6 %collective-permute-done.24 = bf16[512,1024]{1,0:T(8,128)(2,1)S(1)} collective-permute-done((bf16[512,1024]{1,0:T(8,128)(2,1)S(1)}, bf16[512,1024]{1,0:T(8,128)(2,1)S(1)}, u32[]{:S(2)}, u32[]{:S(2)}) %collective-permute-start.24) | collective-permute-done | bytes 1048608 | tf_op jit(solution)/shard_map/outer_in_out/ppermute | solution.py:22
  155.8 4.2 %finish.2.refs_6_ = bf16[512,2048]{1,0:T(8,128)(2,1)} custom-call(s32[4]{0:T(128)S(1)} %pad_add_fusion.ids, s32[16]{0:T(128)S(1)} %copy-done.3, s32[8]{0:T(128)S(1)} %copy-done.4, f32[512,2048]{1,0:T(8,128)S(1)} %fold.1.acc, bf16[512,1024]{1,0:T(8,128)(2,1)S(1)} %broadcast_select_fusion.1.refs_0_, bf16[512,1024]{1,0:T(8,128)(2,1)S(1)} %broadcast_select_fusion.refs_1_, ...), custom_call_target="tpu_custom_call" | custom-call | flops 1 | bytes 1 | tf_op jit(solution)/shard_map/finish/pallas_call | solution.py:280
  160.0 4.2 %finish.3 = bf16[512,2048]{1,0:T(8,128)(2,1)} custom-call(s32[4]{0:T(128)S(1)} %pad_add_fusion.ids, s32[16]{0:T(128)S(1)} %copy-done.3, s32[8]{0:T(128)S(1)} %copy-done.4, f32[512,2048]{1,0:T(8,128)S(1)} %fold.1.acc, bf16[512,1024]{1,0:T(8,128)(2,1)S(1)} %broadcast_select_fusion.1.refs_0_, ...), custom_call_target="tpu_custom_call", output_to_operand_aliasing={{}: (10, {})} | custom-call | flops 1 | bytes 1 | tf_op jit(solution)/shard_map/finish/pallas_call | solution.py:280
  (59 shorter events, 11.8 us)
Async XLA Ops:
  1.9 32.5 %collective-permute-start.4 = (bf16[2,64,3072]{2,1,0:T(8,128)(2,1)S(1)}, bf16[2,64,3072]{2,1,0:T(8,128)(2,1)S(1)}, u32[]{:S(2)}, u32[]{:S(2)}) collective-permute-start(bf16[2,64,3072]{2,1,0:T(8,128)(2,1)S(1)} %pad_maximum_fusion.3.refs_0_.refs_5_), channel_id=1, source_target_pairs={{0,8},{4,12},{8,0},{12,4},{1,9},{5,13},{9,1},{13,5},{2,10},{6,14},... | collective-permute-start | bytes 2359304 | tf_op jit(solution)/shard_map/table1_0/ppermute | solution.py:22
  7.4 14.3 %collective-permute-start.2 = (bf16[256,1024]{1,0:T(8,128)(2,1)}, bf16[256,1024]{1,0:T(8,128)(2,1)}, u32[]{:S(2)}, u32[]{:S(2)}) collective-permute-start(bf16[256,1024]{1,0:T(8,128)(2,1)} %get-tuple-element.79), channel_id=1, source_target_pairs={{0,1},{1,0},{2,3},{3,2},{4,5},{5,4},{6,7},{7,6},{8,9},{9,8},{10,11... | collective-permute-start | bytes 1572872 | tf_op jit(solution)/shard_map/piece1/ppermute | solution.py:22
  9.0 25.5 %collective-permute-start.3 = (bf16[256,1024]{1,0:T(8,128)(2,1)}, bf16[256,1024]{1,0:T(8,128)(2,1)}, u32[]{:S(2)}, u32[]{:S(2)}) collective-permute-start(bf16[256,1024]{1,0:T(8,128)(2,1)} %get-tuple-element.78), channel_id=1, source_target_pairs={{0,3},{1,2},{2,1},{3,0},{4,7},{5,6},{6,5},{7,4},{8,11},{9,10},{10,... | collective-permute-start | bytes 1572872 | tf_op jit(solution)/shard_map/piece3/ppermute | solution.py:22
  21.1 25.4 %copy-start.2 = (bf16[512,2048]{1,0:T(8,128)(2,1)S(1)}, bf16[512,2048]{1,0:T(8,128)(2,1)}, u32[]{:S(2)}) copy-start(bf16[512,2048]{1,0:T(8,128)(2,1)} %hid.3) | copy-start | bytes 6291460
  34.5 9.4 %collective-permute-start.6 = (bf16[256,1024]{1,0:T(8,128)(2,1)}, bf16[256,1024]{1,0:T(8,128)(2,1)S(1)}, u32[]{:S(2)}, u32[]{:S(2)}) collective-permute-start(bf16[256,1024]{1,0:T(8,128)(2,1)} %collective-permute-done.3), channel_id=1, source_target_pairs={{0,16},{4,12},{8,24},{12,4},{16,0},{20,28},{24,8},{28,20},{1,17},{... | collective-permute-start | bytes 1572872 | tf_op jit(solution)/shard_map/turn_a3/ppermute | solution.py:22
  35.9 10.5 %collective-permute-start.7 = (bf16[2,64,3072]{2,1,0:T(8,128)(2,1)S(1)}, bf16[2,64,3072]{2,1,0:T(8,128)(2,1)S(1)}, u32[]{:S(2)}, u32[]{:S(2)}) collective-permute-start(bf16[2,64,3072]{2,1,0:T(8,128)(2,1)S(1)} %pad_maximum_fusion.3.refs_0_.refs_5_), channel_id=1, source_target_pairs={{0,4},{4,0},{8,12},{12,8},{1,5},{5,1},{9,13},{13,9},{2,6},{6,2},{1... | collective-permute-start | bytes 2359304 | tf_op jit(solution)/shard_map/table0_0/ppermute | solution.py:22
  36.0 10.5 %collective-permute-start.8 = (bf16[2,64,3072]{2,1,0:T(8,128)(2,1)S(1)}, bf16[2,64,3072]{2,1,0:T(8,128)(2,1)S(1)}, u32[]{:S(2)}, u32[]{:S(2)}) collective-permute-start(bf16[2,64,3072]{2,1,0:T(8,128)(2,1)S(1)} %collective-permute-done.4.refs_1_.refs_6_), channel_id=1, source_target_pairs={{0,4},{4,0},{8,12},{12,8},{1,5},{5,1},{9,13},{13,9},{2,6},{6,2},{1... | collective-permute-start | bytes 2359304 | tf_op jit(solution)/shard_map/table0_1/ppermute | solution.py:22
  36.5 37.9 %collective-permute-start = (bf16[512,1024]{1,0:T(8,128)(2,1)S(1)}, bf16[512,1024]{1,0:T(8,128)(2,1)S(1)}, u32[]{:S(2)}, u32[]{:S(2)}) collective-permute-start(bf16[512,1024]{1,0:T(8,128)(2,1)S(1)} %copy-done.1), channel_id=1, source_target_pairs={{0,1},{1,0},{2,3},{3,2},{4,5},{5,4},{6,7},{7,6},{8,9},{9,8},{10,11... | collective-permute-start | bytes 3145736 | tf_op jit(solution)/shard_map/outer/ppermute | solution.py:22
  37.0 37.4 %collective-permute-start.1 = (bf16[512,1024]{1,0:T(8,128)(2,1)S(1)}, bf16[512,1024]{1,0:T(8,128)(2,1)S(1)}, u32[]{:S(2)}, u32[]{:S(2)}) collective-permute-start(bf16[512,1024]{1,0:T(8,128)(2,1)S(1)} %copy-done.1), channel_id=1, source_target_pairs={{1,2},{2,1},{5,6},{6,5},{9,10},{10,9},{13,14},{14,13},{17,18},{18,... | collective-permute-start | bytes 3145736 | tf_op jit(solution)/shard_map/inner/ppermute | solution.py:22
  43.9 9.4 %collective-permute-start.5 = (bf16[256,1024]{1,0:T(8,128)(2,1)}, bf16[256,1024]{1,0:T(8,128)(2,1)S(1)}, u32[]{:S(2)}, u32[]{:S(2)}) collective-permute-start(bf16[256,1024]{1,0:T(8,128)(2,1)} %collective-permute-done.2), channel_id=1, source_target_pairs={{0,16},{4,12},{8,24},{12,4},{16,0},{20,28},{24,8},{28,20},{1,17},{... | collective-permute-start | bytes 1572872 | tf_op jit(solution)/shard_map/turn_a1/ppermute | solution.py:22
  49.5 24.8 %collective-permute-start.10 = (bf16[512,128]{1,0:T(8,128)(2,1)S(1)}, bf16[512,128]{1,0:T(8,128)(2,1)S(1)}, u32[]{:S(2)}, u32[]{:S(2)}) collective-permute-start(bf16[512,128]{1,0:T(8,128)(2,1)S(1)} %rank_partials.1), channel_id=1, source_target_pairs={{0,2},{1,3},{2,0},{3,1},{4,6},{5,7},{6,4},{7,5},{8,10},{9,11},{10,... | collective-permute-start | bytes 393224 | tf_op jit(solution)/shard_map/ranks2/ppermute | solution.py:22
  51.3 23.0 %collective-permute-start.11 = (bf16[512,128]{1,0:T(8,128)(2,1)S(1)}, bf16[512,128]{1,0:T(8,128)(2,1)S(1)}, u32[]{:S(2)}, u32[]{:S(2)}) collective-permute-start(bf16[512,128]{1,0:T(8,128)(2,1)S(1)} %rank_partials.1), channel_id=1, source_target_pairs={{0,3},{1,2},{2,1},{3,0},{4,7},{5,6},{6,5},{7,4},{8,11},{9,10},{10,... | collective-permute-start | bytes 393224 | tf_op jit(solution)/shard_map/ranks3/ppermute | solution.py:22
  53.2 21.1 %collective-permute-start.9 = (bf16[512,128]{1,0:T(8,128)(2,1)S(1)}, bf16[512,128]{1,0:T(8,128)(2,1)S(1)}, u32[]{:S(2)}, u32[]{:S(2)}) collective-permute-start(bf16[512,128]{1,0:T(8,128)(2,1)S(1)} %rank_partials.1), channel_id=1, source_target_pairs={{0,1},{1,0},{2,3},{3,2},{4,5},{5,4},{6,7},{7,6},{8,9},{9,8},{10,11... | collective-permute-start | bytes 393224 | tf_op jit(solution)/shard_map/ranks1/ppermute | solution.py:22
  74.4 25.8 %collective-permute-start.13 = (bf16[512,1024]{1,0:T(8,128)(2,1)S(1)}, bf16[512,1024]{1,0:T(8,128)(2,1)S(1)}, u32[]{:S(2)}, u32[]{:S(2)}) collective-permute-start(bf16[512,1024]{1,0:T(8,128)(2,1)S(1)} %pad_maximum_fusion.refs_1_), channel_id=1, source_target_pairs={{0,8},{4,20},{8,0},{12,28},{16,24},{20,4},{24,16},{28,12},{1,9},{5... | collective-permute-start | bytes 3145736 | tf_op jit(solution)/shard_map/turn_b1/ppermute | solution.py:22
  75.0 25.5 %collective-permute-start.14 = (bf16[512,1024]{1,0:T(8,128)(2,1)S(1)}, bf16[512,1024]{1,0:T(8,128)(2,1)S(1)}, u32[]{:S(2)}, u32[]{:S(2)}) collective-permute-start(bf16[512,1024]{1,0:T(8,128)(2,1)S(1)} %pad_maximum_fusion.1.refs_4_), channel_id=1, source_target_pairs={{0,8},{4,20},{8,0},{12,28},{16,24},{20,4},{24,16},{28,12},{1,9},{5... | collective-permute-start | bytes 3145736 | tf_op jit(solution)/shard_map/turn_b3/ppermute | solution.py:22
  76.5 23.7 %collective-permute-start.12 = (bf16[256,1024]{1,0:T(8,128)(2,1)S(1)}, bf16[256,1024]{1,0:T(8,128)(2,1)S(1)}, u32[]{:S(2)}, u32[]{:S(2)}) collective-permute-start(bf16[256,1024]{1,0:T(8,128)(2,1)S(1)} %get-tuple-element.47), channel_id=1, source_target_pairs={{0,2},{1,3},{2,0},{3,1},{4,6},{5,7},{6,4},{7,5},{8,10},{9,11},{10,... | collective-permute-start | bytes 1572872 | tf_op jit(solution)/shard_map/piece2/ppermute | solution.py:22
  82.0 1.8 %collective-permute-start.15 = (bf16[1,64,3072]{2,1,0:T(8,128)(2,1)S(1)}, bf16[1,64,3072]{2,1,0:T(8,128)(2,1)S(1)}, u32[]{:S(2)}, u32[]{:S(2)}) collective-permute-start(bf16[1,64,3072]{2,1,0:T(8,128)(2,1)S(1)} %get-tuple-element.51), channel_id=1, source_target_pairs={{0,4},{4,0},{8,12},{12,8},{1,5},{5,1},{9,13},{13,9},{2,6},{6,2},{1... | collective-permute-start | bytes 1179656 | tf_op jit(solution)/shard_map/grads0_2/ppermute | solution.py:22
  82.1 2.3 %collective-permute-start.16 = (bf16[1,64,3072]{2,1,0:T(8,128)(2,1)S(1)}, bf16[1,64,3072]{2,1,0:T(8,128)(2,1)S(1)}, u32[]{:S(2)}, u32[]{:S(2)}) collective-permute-start(bf16[1,64,3072]{2,1,0:T(8,128)(2,1)S(1)} %get-tuple-element.52), channel_id=1, source_target_pairs={{0,4},{4,0},{8,12},{12,8},{1,5},{5,1},{9,13},{13,9},{2,6},{6,2},{1... | collective-permute-start | bytes 1179656 | tf_op jit(solution)/shard_map/grads0_3/ppermute | solution.py:22
  100.5 24.7 %collective-permute-start.17 = (bf16[512,1024]{1,0:T(8,128)(2,1)S(1)}, bf16[512,1024]{1,0:T(8,128)(2,1)S(1)}, u32[]{:S(2)}, u32[]{:S(2)}) collective-permute-start(bf16[512,1024]{1,0:T(8,128)(2,1)S(1)} %collective-permute-done.1), channel_id=1, source_target_pairs={{1,0},{2,3},{5,4},{6,7},{9,8},{10,11},{13,12},{14,15},{17,16},{18,... | collective-permute-start | bytes 3145736 | tf_op jit(solution)/shard_map/inner_out/ppermute | solution.py:22
  102.0 22.8 %collective-permute-start.20 = (bf16[2,64,3072]{2,1,0:T(8,128)(2,1)S(1)}, bf16[2,64,3072]{2,1,0:T(8,128)(2,1)S(1)}, u32[]{:S(2)}, u32[]{:S(2)}) collective-permute-start(bf16[2,64,3072]{2,1,0:T(8,128)(2,1)S(1)} %add_convert_fusion), channel_id=1, source_target_pairs={{0,8},{4,12},{8,0},{12,4},{1,9},{5,13},{9,1},{13,5},{2,10},{6,14},... | collective-permute-start | bytes 2359304 | tf_op jit(solution)/shard_map/grads1/ppermute | solution.py:22
  102.6 22.8 %collective-permute-start.18 = (bf16[512,1024]{1,0:T(8,128)(2,1)S(1)}, bf16[512,1024]{1,0:T(8,128)(2,1)S(1)}, u32[]{:S(2)}, u32[]{:S(2)}) collective-permute-start(bf16[512,1024]{1,0:T(8,128)(2,1)S(1)} %collective-permute-done.refs_0_), channel_id=1, source_target_pairs={{1,2},{2,1},{5,6},{6,5},{9,10},{10,9},{13,14},{14,13},{17,18},{18,... | collective-permute-start | bytes 3145736 | tf_op jit(solution)/shard_map/outer_in/ppermute | solution.py:22
  103.3 9.2 %collective-permute-start.19 = (bf16[256,1024]{1,0:T(8,128)(2,1)S(1)}, bf16[256,1024]{1,0:T(8,128)(2,1)S(1)}, u32[]{:S(2)}, u32[]{:S(2)}) collective-permute-start(bf16[256,1024]{1,0:T(8,128)(2,1)S(1)} %collective-permute-done.12), channel_id=1, source_target_pairs={{0,16},{4,12},{8,24},{12,4},{16,0},{20,28},{24,8},{28,20},{1,17},{... | collective-permute-start | bytes 1572872 | tf_op jit(solution)/shard_map/turn_a2/ppermute | solution.py:22
  103.9 21.9 %collective-permute-start.25 = (bf16[1,64,3072]{2,1,0:T(8,128)(2,1)S(1)}, bf16[1,64,3072]{2,1,0:T(8,128)(2,1)S(1)}, u32[]{:S(2)}, u32[]{:S(2)}) collective-permute-start(bf16[1,64,3072]{2,1,0:T(8,128)(2,1)S(1)} %get-tuple-element.65), channel_id=1, source_target_pairs={{0,4},{4,0},{8,12},{12,8},{1,5},{5,1},{9,13},{13,9},{2,6},{6,2},{1... | collective-permute-start | bytes 1179656 | tf_op jit(solution)/shard_map/grads0_0/ppermute | solution.py:22
  112.5 13.8 %collective-permute-start.26 = (bf16[1,64,3072]{2,1,0:T(8,128)(2,1)S(1)}, bf16[1,64,3072]{2,1,0:T(8,128)(2,1)S(1)}, u32[]{:S(2)}, u32[]{:S(2)}) collective-permute-start(bf16[1,64,3072]{2,1,0:T(8,128)(2,1)S(1)} %get-tuple-element.66), channel_id=1, source_target_pairs={{0,4},{4,0},{8,12},{12,8},{1,5},{5,1},{9,13},{13,9},{2,6},{6,2},{1... | collective-permute-start | bytes 1179656 | tf_op jit(solution)/shard_map/grads0_1/ppermute | solution.py:22
  124.8 3.3 %collective-permute-start.22 = (bf16[512,1024]{1,0:T(8,128)(2,1)S(1)}, bf16[512,1024]{1,0:T(8,128)(2,1)S(1)}, u32[]{:S(2)}, u32[]{:S(2)}) collective-permute-start(bf16[512,1024]{1,0:T(8,128)(2,1)S(1)} %pad_maximum_fusion.refs_1_), channel_id=1, source_target_pairs={{0,4},{4,0},{8,12},{12,8},{16,20},{20,16},{24,28},{28,24},{1,5},{5... | collective-permute-start | bytes 3145736 | tf_op jit(solution)/shard_map/turn_c10/ppermute | solution.py:22
  125.2 4.0 %collective-permute-start.23 = (bf16[512,1024]{1,0:T(8,128)(2,1)S(1)}, bf16[512,1024]{1,0:T(8,128)(2,1)S(1)}, u32[]{:S(2)}, u32[]{:S(2)}) collective-permute-start(bf16[512,1024]{1,0:T(8,128)(2,1)S(1)} %collective-permute-done.13.refs_2_), channel_id=1, source_target_pairs={{0,4},{4,0},{8,12},{12,8},{16,20},{20,16},{24,28},{28,24},{1,5},{5... | collective-permute-start | bytes 3145736 | tf_op jit(solution)/shard_map/turn_c11/ppermute | solution.py:22
  125.4 34.6 %collective-permute-start.29 = (bf16[512,1024]{1,0:T(8,128)(2,1)S(1)}, bf16[512,1024]{1,0:T(8,128)(2,1)S(1)}, u32[]{:S(2)}, u32[]{:S(2)}) collective-permute-start(bf16[512,1024]{1,0:T(8,128)(2,1)S(1)} %pad_maximum_fusion.1.refs_4_), channel_id=1, source_target_pairs={{0,4},{4,0},{8,12},{12,8},{16,20},{20,16},{24,28},{28,24},{1,5},{5... | collective-permute-start | bytes 3145736 | tf_op jit(solution)/shard_map/turn_c30/ppermute | solution.py:22
  125.8 14.8 %collective-permute-start.21 = (bf16[512,1024]{1,0:T(8,128)(2,1)S(1)}, bf16[512,1024]{1,0:T(8,128)(2,1)S(1)}, u32[]{:S(2)}, u32[]{:S(2)}) collective-permute-start(bf16[512,1024]{1,0:T(8,128)(2,1)S(1)} %pad_maximum_fusion.2.refs_2_), channel_id=1, source_target_pairs={{0,8},{4,20},{8,0},{12,28},{16,24},{20,4},{24,16},{28,12},{1,9},{5... | collective-permute-start | bytes 3145736 | tf_op jit(solution)/shard_map/turn_b2/ppermute | solution.py:22
  126.3 28.8 %collective-permute-start.24 = (bf16[512,1024]{1,0:T(8,128)(2,1)S(1)}, bf16[512,1024]{1,0:T(8,128)(2,1)S(1)}, u32[]{:S(2)}, u32[]{:S(2)}) collective-permute-start(bf16[512,1024]{1,0:T(8,128)(2,1)S(1)} %collective-permute-done.18), channel_id=1, source_target_pairs={{1,0},{2,3},{5,4},{6,7},{9,8},{10,11},{13,12},{14,15},{17,16},{18,... | collective-permute-start | bytes 3145736 | tf_op jit(solution)/shard_map/outer_in_out/ppermute | solution.py:22
  128.1 31.9 %collective-permute-start.30 = (bf16[512,1024]{1,0:T(8,128)(2,1)S(1)}, bf16[512,1024]{1,0:T(8,128)(2,1)S(1)}, u32[]{:S(2)}, u32[]{:S(2)}) collective-permute-start(bf16[512,1024]{1,0:T(8,128)(2,1)S(1)} %collective-permute-done.14.refs_5_), channel_id=1, source_target_pairs={{0,4},{4,0},{8,12},{12,8},{16,20},{20,16},{24,28},{28,24},{1,5},{5... | collective-permute-start | bytes 3145736 | tf_op jit(solution)/shard_map/turn_c31/ppermute | solution.py:22
  155.2 4.9 %collective-permute-start.27 = (bf16[512,1024]{1,0:T(8,128)(2,1)S(1)}, bf16[512,1024]{1,0:T(8,128)(2,1)S(1)}, u32[]{:S(2)}, u32[]{:S(2)}) collective-permute-start(bf16[512,1024]{1,0:T(8,128)(2,1)S(1)} %pad_maximum_fusion.2.refs_2_), channel_id=1, source_target_pairs={{0,4},{4,0},{8,12},{12,8},{16,20},{20,16},{24,28},{28,24},{1,5},{5... | collective-permute-start | bytes 3145736 | tf_op jit(solution)/shard_map/turn_c20/ppermute | solution.py:22
  155.2 4.9 %collective-permute-start.28 = (bf16[512,1024]{1,0:T(8,128)(2,1)S(1)}, bf16[512,1024]{1,0:T(8,128)(2,1)S(1)}, u32[]{:S(2)}, u32[]{:S(2)}) collective-permute-start(bf16[512,1024]{1,0:T(8,128)(2,1)S(1)} %collective-permute-done.21.refs_3_), channel_id=1, source_target_pairs={{0,4},{4,0},{8,12},{12,8},{16,20},{20,16},{24,28},{28,24},{1,5},{5... | collective-permute-start | bytes 3145736 | tf_op jit(solution)/shard_map/turn_c21/ppermute | solution.py:22
  (4 other events, 67.4 us)

commit v4 on v3

--- a/solution.py
+++ b/solution.py
@@ -59,16 +59,16 @@
     return jnp.where(closing, counts[member], BLK)
 
 
-def rank_kernel(ids, owner, counts, hid, cot, *refs, width, blocks, slot, held):
+def rank_kernel(ids, owner, counts, hid, cot, *refs, blocks, slot, held):
     b = pl.program_id(0)
     count = live_count(b, ids, owner, counts, blocks=blocks)
     parts, out = refs[:-1], refs[-1]
-    for i, part in enumerate(parts):
+    for i in range(len(parts) // 2):
 
         @pl.when(slot(b, ids, owner) // held == i)
-        def _(part=part):
-            act = contract_last(hid[...], part[0, :, :width])
-            grad = contract_last(cot[...], part[0, :, width:])
+        def _(down=parts[2 * i], up=parts[2 * i + 1]):
+            act = contract_last(hid[...], down[0])
+            grad = contract_last(cot[...], up[0])
             both = jnp.concatenate([act, grad], axis=1)
             rows = lax.broadcasted_iota(jnp.int32, both.shape, 0)
             out[...] = jnp.where(rows < count, both, 0.0).astype(BF)
@@ -76,18 +76,18 @@
 
 def rank_partials(ids, owner, counts, hidden, cotan, table, *, blocks, owned, bits):
     width, cols = hidden.shape[1], cotan.shape[1]
-    held, rank = table[0].shape[:2]
+    held, rank = table[0][0].shape[:2]
     slot = functools.partial(slot_of, blocks=blocks, owned=owned, bits=bits)
 
-    def chosen(i):
+    def chosen(i, size):
         def index(b, ids, owner, counts):
             at = slot(b, ids, owner)
             return (jnp.where(at // held == i, at % held, 0), 0, 0)
 
-        return pl.BlockSpec((1, rank, width + cols), index)
+        return pl.BlockSpec((1, rank, size), index)
 
     return pl.pallas_call(
-        functools.partial(rank_kernel, width=width, blocks=blocks, slot=slot, held=held),
+        functools.partial(rank_kernel, blocks=blocks, slot=slot, held=held),
         grid_spec=pltpu.PrefetchScalarGridSpec(
             num_scalar_prefetch=3,
             grid=(blocks,),
@@ -95,14 +95,14 @@
                 pl.BlockSpec((BLK, width), lambda b, *s: (b, 0)),
                 pl.BlockSpec((BLK, cols), lambda b, *s: (b, 0)),
             ]
-            + [chosen(i) for i in range(len(table))],
+            + [chosen(i, size) for i in range(len(table)) for size in (width, cols)],
             out_specs=pl.BlockSpec((BLK, 2 * rank), lambda b, *s: (b, 0)),
         ),
         out_shape=jax.ShapeDtypeStruct((blocks * BLK, 2 * rank), BF),
         compiler_params=params(16),
         cost_estimate=CHEAP,
         name="rank_partials",
-    )(ids, owner, counts, hidden, cotan, *table)
+    )(ids, owner, counts, hidden, cotan, *[one for pair in table for one in pair])
 
 
 def grads_kernel(ids, owner, hid, cot, both, *refs, width, blocks, slot, half):
@@ -349,7 +349,10 @@
         return jnp.concatenate([own, move(name, own, copies, pairs)], axis=0)
 
     def more(bit, parts):
-        return parts + [swap(f"table{bit}_{i}", part, "dp", nd, bit) for i, part in enumerate(parts)]
+        return parts + [
+            (swap(f"down{bit}_{i}", down, "dp", nd, bit), swap(f"up{bit}_{i}", up, "dp", nd, bit))
+            for i, (down, up) in enumerate(parts)
+        ]
 
     def ranks(table):
         return rank_partials(ids, owner, counts, hidden, query_gradient, table, **sizes)
@@ -376,13 +379,12 @@
     def folded(acc, xs, ws, tile, first, **more):
         return fold(ids, owner, counts, acc, xs, ws, tile, first, **sizes, **more)
 
-    table = [jnp.concatenate([jnp.swapaxes(down, 1, 2), up], axis=2)]
     if fast:
-        cuts = [cut(z ^ d) for d in (1, 2, 3)]
-        piece1, piece3 = piece(1, cuts[0]), piece(3, cuts[2])
-        table = more(bits[0], table)
+        piece1, piece3 = piece(1, cut(z ^ 1)), piece(3, cut(z ^ 3))
+        table = more(bits[0], [(jnp.swapaxes(down, 1, 2), up)])
+        cut2 = cut(z ^ 2)
         acc = local()
-        piece1, piece3, cut2, table, acc = together(piece1, piece3, cuts[1], table, acc)
+        piece1, piece3, cut2, table, acc = together(piece1, piece3, cut2, table, acc)
 
         by_one = move("outer", query_gradient, "tensor", outer)
         across = move("inner", query_gradient, "tensor", inner)
@@ -390,13 +392,13 @@
         wide3 = turned("turn_a3", piece3, turn_a)
         table = more(bits[1], table)
         both = ranks(table)
-        shares = [move(f"ranks{d}", both, "tensor", [(i, i ^ d) for i in range(n)]) for d in (1, 2, 3)]
-        both = sum((a.astype(F32) for a in shares), both.astype(F32)).astype(BF)
+        both = rank_sum(1, both)
         by_one, across, wide1, wide3, both, cut2 = together(by_one, across, wide1, wide3, both, cut2)
 
         piece2 = piece(2, cut2)
         wide1 = [wide1, move("turn_b1", wide1, copies, turn_b)]
         wide3 = [wide3, move("turn_b3", wide3, copies, turn_b)]
+        both = rank_sum(0, both)
         sends, keep = grads(both)
         rest = len(sends) // 2
         got = [swap(f"grads0_{i}", one, "dp", nd, bits[1]) for i, one in enumerate(sends)]
@@ -412,7 +414,7 @@
         end_three = move("outer_in_out", by_two, "tensor", outward)
         wide2 = [wide2, move("turn_b2", wide2, copies, turn_b)]
         other1 = [move(f"turn_c1{i}", part, copies, turn_c) for i, part in enumerate(wide1)]
-        acc = folded(acc, [by_one], [wide1 + other1], relative_tile, 0, table=table, both=both)
+        acc = folded(acc, [by_one], [wide1 + other1], relative_tile, 0, table=[pair[0] for pair in table], both=both)
         two = jnp.where(middle, by_two, end_two)
         total = keep[:rest].astype(F32) + jnp.concatenate(got[:rest], axis=0).astype(F32) + far.astype(F32)
         grad_down, grad_up = jnp.swapaxes(total[:, :, :width], 1, 2), total[:, :, width:]
@@ -426,18 +428,19 @@
         result = folded(acc, [two, three], [wide2, wide3], relative_tile, 0, final=True)
         result = folded(acc, [two, three], [other2, other3], relative_tile, 2, before=result, final=True)
     else:
+        table = [(jnp.swapaxes(down, 1, 2), up)]
         xs = line(query_gradient, n, z)
         wides = []
         for step in range(1, n):
             own = move(f"piece{step}", cut(lax.rem(z + step, n)), "tensor", [(i, (i + step) % n) for i in range(n)])
             wides.append((lax.all_gather(own, copies, axis=0, tiled=True),))
         for bit in bits:
-            table = [jnp.concatenate(more(bit, table), axis=0)]
+            table = [tuple(jnp.concatenate(pair, axis=0) for pair in zip(*more(bit, table)))]
         both = ranks(table)
         for bit in range(n.bit_length() - 1):
             both = rank_sum(bit, both)
         grad_down, grad_up = grad_sum(*grads(both))
-        acc = folded(local(), xs[:1], wides[:1], plain_tile, 0, table=table, both=both)
+        acc = folded(local(), xs[:1], wides[:1], plain_tile, 0, table=[pair[0] for pair in table], both=both)
         result = folded(acc, xs[1:], wides[1:], plain_tile, 0, final=True)
     return result, grad_down, grad_up
 

time: 165 us -> 159 us (0.964)
  waiting for transfers between devices: 82 us -> 75.4 us
  starting transfers between devices: 39 us -> 41.1 us
    ppermute x31 -> x33, waiting for transfers between devices: 82 us -> 75.4 us  [move(): return lax.ppermute(a, axis, pairs)]
    ppermute x31 -> x33, starting transfers between devices: 39 us -> 41.1 us  [move(): return lax.ppermute(a, axis, pairs)]
    unnamed x10 -> x14, local copies, waits for them, and re-layouts: 5.79 us -> 5.79 us
  transfers between devices with their start and end apart: 31 -> 33, of which waited for: 14 -> 16; matrix products, arithmetic and copies ran while one was open for 5% -> 3% of each run, Pallas kernels for 14% -> 15%
where the time goes in v4:
time: 159 us
  waiting for transfers between devices  75.4 us (47%)
  starting transfers between devices  41.1 us (26%)
  Pallas kernels  28.1 us (18%)
  local copies, waits for them, and re-layouts  10.3 us (6%)
  other arithmetic  3.16 us (2%)
    ppermute x33, waiting for transfers between devices, move(): return lax.ppermute(a, axis, pairs)  75.4 us
    ppermute x33, starting transfers between devices, move(): return lax.ppermute(a, axis, pairs)  41.1 us
    pallas_call x3, Pallas kernels, fold(): pl.pallas_call(functools.partial(fold_kernel, terms=len(xs), parts=parts,...  17.6 us
    unnamed x14, local copies, waits for them, and re-layouts  5.79 us
    pallas_call x1, Pallas kernels, local_products(): pl.pallas_call(local_kernel, grid_spec=pltpu.PrefetchScalarGridSpec(num_s...  3.8 us
    pallas_call x1, Pallas kernels, member_grads(): pl.pallas_call(functools.partial(grads_kernel, width=width, blocks=blocks...  3.44 us
    pallas_call x1, Pallas kernels, rank_partials(): pl.pallas_call(functools.partial(rank_kernel, blocks=blocks, slot=slot, h...  3.25 us
  transfers between devices with their start and end apart: 33, of which 16 were waited for; matrix products, arithmetic and copies ran while one was open for 3% of the time, Pallas kernels for 15%

profile of v4, /device:TPU:0, one launch (start us, length us, event | category | flops | bytes accessed | tf_op | source)
XLA Modules:
  0.0 158.9 jit_solution(8821921193184694767)
XLA Ops:
  0.7 2.6 %constant_dynamic-slice_fusion = (bf16[256,1024]{1,0:T(8,128)(2,1)S(1)}, bf16[256,1024]{1,0:T(8,128)(2,1)}, bf16[256,1024]{1,0:T(8,128)(2,1)}) fusion(bf16[8192,1024]{1,0:T(8,128)(2,1)} %weight.1, s32[]{:T(128)S(6)} %select_n.40, s32[]{:T(128)S(6)} %select_n.39, s32[]{:T(128)S(6)} %select_n.38), kind=kLoop, calls=%fused_computation.10 | loop fusion | bytes 3145740 | tf_op jit(solution)/shard_map/dynamic_slice | solution.py:343
  3.3 3.0 %collective-permute-start.2 = (bf16[256,1024]{1,0:T(8,128)(2,1)}, bf16[256,1024]{1,0:T(8,128)(2,1)}, u32[]{:S(2)}, u32[]{:S(2)}) collective-permute-start(bf16[256,1024]{1,0:T(8,128)(2,1)} %get-tuple-element.83), channel_id=1, source_target_pairs={{0,1},{1,0},{2,3},{3,2},{4,5},{5,4},{6,7},{7,6},{8,9},{9,8},{10,11... | collective-permute-start | bytes 1572872 | tf_op jit(solution)/shard_map/piece1/ppermute | solution.py:22
  6.3 2.5 %collective-permute-start.3 = (bf16[256,1024]{1,0:T(8,128)(2,1)}, bf16[256,1024]{1,0:T(8,128)(2,1)}, u32[]{:S(2)}, u32[]{:S(2)}) collective-permute-start(bf16[256,1024]{1,0:T(8,128)(2,1)} %get-tuple-element.82), channel_id=1, source_target_pairs={{0,3},{1,2},{2,1},{3,0},{4,7},{5,6},{6,5},{7,4},{8,11},{9,10},{10,... | collective-permute-start | bytes 1572872 | tf_op jit(solution)/shard_map/piece3/ppermute | solution.py:22
  8.8 1.5 collective-permute-start.4
  10.9 5.8 %copy-done = bf16[8192,1024]{1,0:T(8,128)(2,1)S(1)} copy-done((bf16[8192,1024]{1,0:T(8,128)(2,1)S(1)}, bf16[8192,1024]{1,0:T(8,128)(2,1)}, u32[]{:S(2)}) %copy-start) | copy-done | bytes 16777240
  16.7 3.8 %local_products.1.acc = f32[512,2048]{1,0:T(8,128)S(1)} custom-call(s32[4]{0:T(128)S(1)} %pad_add_fusion.ids, bf16[512,1024]{1,0:T(8,128)(2,1)S(1)} %copy-done.1, bf16[8192,1024]{1,0:T(8,128)(2,1)S(1)} %copy-done), custom_call_target="tpu_custom_call" | custom-call | flops 1 | bytes 1 | tf_op jit(solution)/shard_map/local_products/pallas_call | solution.py:195
  20.5 7.0 %collective-permute-done.5.refs_3_ = bf16[2,64,1024]{2,1,0:T(8,128)(2,1)S(1)} collective-permute-done((bf16[2,64,1024]{2,1,0:T(8,128)(2,1)S(1)}, bf16[2,64,1024]{2,1,0:T(8,128)(2,1)S(1)}, u32[]{:S(2)}, u32[]{:S(2)}) %collective-permute-start.5) | collective-permute-done | bytes 262176 | tf_op jit(solution)/shard_map/up1_0/ppermute | solution.py:22
  27.5 4.6 %collective-permute-done.3 = bf16[256,1024]{1,0:T(8,128)(2,1)} collective-permute-done((bf16[256,1024]{1,0:T(8,128)(2,1)}, bf16[256,1024]{1,0:T(8,128)(2,1)}, u32[]{:S(2)}, u32[]{:S(2)}) %collective-permute-start.3) | collective-permute-done | bytes 524320 | tf_op jit(solution)/shard_map/piece3/ppermute | solution.py:22
  34.7 1.5 collective-permute-start.7
  36.8 3.3 %rank_partials.1 = bf16[512,128]{1,0:T(8,128)(2,1)S(1)} custom-call(s32[4]{0:T(128)S(1)} %pad_add_fusion.ids, s32[16]{0:T(128)S(1)} %copy-done.5, s32[8]{0:T(128)S(1)} %copy-done.6, bf16[512,2048]{1,0:T(8,128)(2,1)S(1)} %copy-done.2, bf16[512,1024]{1,0:T(8,128)(2,1)S(1)} %copy-done.1, bf16[2,64,2048]{2,1,0:T(8,128)(2,1)S(1)} %bitcast.9, ...), custom_call_target="tpu_custom_call" | custom-call | flops 1 | bytes 1 | tf_op jit(solution)/shard_map/rank_partials/pallas_call | solution.py:89
  40.0 3.5 %collective-permute-start.12 = (bf16[512,128]{1,0:T(8,128)(2,1)S(1)}, bf16[512,128]{1,0:T(8,128)(2,1)S(1)}, u32[]{:S(2)}, u32[]{:S(2)}) collective-permute-start(bf16[512,128]{1,0:T(8,128)(2,1)S(1)} %rank_partials.1), channel_id=1, source_target_pairs={{0,2},{1,3},{2,0},{3,1},{4,6},{5,7},{6,4},{7,5},{8,10},{9,11},{10,... | collective-permute-start | bytes 393224 | tf_op jit(solution)/shard_map/rank_sum1/ppermute | solution.py:22
  44.1 1.1 pad_maximum_fusion.1.refs_4_
  45.2 4.5 %collective-permute-done.6 = bf16[256,1024]{1,0:T(8,128)(2,1)S(1)} collective-permute-done((bf16[256,1024]{1,0:T(8,128)(2,1)}, bf16[256,1024]{1,0:T(8,128)(2,1)S(1)}, u32[]{:S(2)}, u32[]{:S(2)}) %collective-permute-start.6) | collective-permute-done | bytes 524320 | tf_op jit(solution)/shard_map/turn_a1/ppermute | solution.py:22
  49.7 1.1 pad_maximum_fusion.refs_1_
  50.9 16.0 %collective-permute-done.12 = bf16[512,128]{1,0:T(8,128)(2,1)S(1)} collective-permute-done((bf16[512,128]{1,0:T(8,128)(2,1)S(1)}, bf16[512,128]{1,0:T(8,128)(2,1)S(1)}, u32[]{:S(2)}, u32[]{:S(2)}) %collective-permute-start.12) | collective-permute-done | bytes 131104 | tf_op jit(solution)/shard_map/rank_sum1/ppermute | solution.py:22
  66.9 1.6 collective-permute-start.14
  69.0 2.0 %collective-permute-start.13 = (bf16[256,1024]{1,0:T(8,128)(2,1)S(1)}, bf16[256,1024]{1,0:T(8,128)(2,1)S(1)}, u32[]{:S(2)}, u32[]{:S(2)}) collective-permute-start(bf16[256,1024]{1,0:T(8,128)(2,1)S(1)} %get-tuple-element.51), channel_id=1, source_target_pairs={{0,2},{1,3},{2,0},{3,1},{4,6},{5,7},{6,4},{7,5},{8,10},{9,11},{10,... | collective-permute-start | bytes 1572872 | tf_op jit(solution)/shard_map/piece2/ppermute | solution.py:22
  71.0 4.2 %collective-permute-done.16 = bf16[512,128]{1,0:T(8,128)(2,1)S(1)} collective-permute-done((bf16[512,128]{1,0:T(8,128)(2,1)S(1)}, bf16[512,128]{1,0:T(8,128)(2,1)S(1)}, u32[]{:S(2)}, u32[]{:S(2)}) %collective-permute-start.16) | collective-permute-done | bytes 131104 | tf_op jit(solution)/shard_map/rank_sum0/ppermute | solution.py:22
  75.3 3.4 %member_grads.1 = (bf16[1,64,3072]{2,1,0:T(8,128)(2,1)S(1)}, bf16[1,64,3072]{2,1,0:T(8,128)(2,1)S(1)}, bf16[1,64,3072]{2,1,0:T(8,128)(2,1)S(1)}, bf16[1,64,3072]...) custom-call(s32[4]{0:T(128)S(1)} %pad_add_fusion.ids, s32[16]{0:T(128)S(1)} %copy-done.5, bf16[512,2048]{1,0:T(8,128)(2,1)S(1)} %copy-done.2, ...), custom_call_target="tpu_custom_call" | custom-call | flops 1 | bytes 1 | tf_op jit(solution)/shard_map/member_grads/pallas_call | solution.py:141
  79.3 1.2 collective-permute-done.17
  81.1 12.7 %collective-permute-done.13 = bf16[256,1024]{1,0:T(8,128)(2,1)S(1)} collective-permute-done((bf16[256,1024]{1,0:T(8,128)(2,1)S(1)}, bf16[256,1024]{1,0:T(8,128)(2,1)S(1)}, u32[]{:S(2)}, u32[]{:S(2)}) %collective-permute-start.13) | collective-permute-done | bytes 524320 | tf_op jit(solution)/shard_map/piece2/ppermute | solution.py:22
  93.9 1.3 collective-permute-start.19
  95.4 1.6 collective-permute-start.22
  97.7 1.6 collective-permute-start.21
  99.2 7.7 %collective-permute-done.21 = bf16[256,1024]{1,0:T(8,128)(2,1)S(1)} collective-permute-done((bf16[256,1024]{1,0:T(8,128)(2,1)S(1)}, bf16[256,1024]{1,0:T(8,128)(2,1)S(1)}, u32[]{:S(2)}, u32[]{:S(2)}) %collective-permute-start.21) | collective-permute-done | bytes 524320 | tf_op jit(solution)/shard_map/turn_a2/ppermute | solution.py:22
  106.9 12.2 %collective-permute-start.28 = (bf16[1,64,3072]{2,1,0:T(8,128)(2,1)S(1)}, bf16[1,64,3072]{2,1,0:T(8,128)(2,1)S(1)}, u32[]{:S(2)}, u32[]{:S(2)}) collective-permute-start(bf16[1,64,3072]{2,1,0:T(8,128)(2,1)S(1)} %get-tuple-element.70), channel_id=1, source_target_pairs={{0,4},{4,0},{8,12},{12,8},{1,5},{5,1},{9,13},{13,9},{2,6},{6,2},{1... | collective-permute-start | bytes 1179656 | tf_op jit(solution)/shard_map/grads0_1/ppermute | solution.py:22
  120.0 1.5 collective-permute-start.23
  121.5 1.5 collective-permute-start.26
  123.4 9.2 %fold.1.acc = f32[512,2048]{1,0:T(8,128)S(1)} custom-call(s32[4]{0:T(128)S(1)} %pad_add_fusion.ids, s32[16]{0:T(128)S(1)} %copy-done.5, s32[8]{0:T(128)S(1)} %copy-done.6, f32[512,2048]{1,0:T(8,128)S(1)} %local_products.1.acc, bf16[512,1024]{1,0:T(8,128)(2,1)S(1)} %collective-permute-done.refs_0_, ...), custom_call_target="tpu_custom_call", output_to_operand_aliasing={{}: (3, {})} | custom-call | flops 1 | bytes 1 | tf_op jit(solution)/shard_map/fold/pallas_call | solution.py:280
  134.8 15.1 %collective-permute-done.26 = bf16[512,1024]{1,0:T(8,128)(2,1)S(1)} collective-permute-done((bf16[512,1024]{1,0:T(8,128)(2,1)S(1)}, bf16[512,1024]{1,0:T(8,128)(2,1)S(1)}, u32[]{:S(2)}, u32[]{:S(2)}) %collective-permute-start.26) | collective-permute-done | bytes 1048608 | tf_op jit(solution)/shard_map/outer_in_out/ppermute | solution.py:22
  150.5 4.2 %finish.2.refs_6_ = bf16[512,2048]{1,0:T(8,128)(2,1)} custom-call(s32[4]{0:T(128)S(1)} %pad_add_fusion.ids, s32[16]{0:T(128)S(1)} %copy-done.5, s32[8]{0:T(128)S(1)} %copy-done.6, f32[512,2048]{1,0:T(8,128)S(1)} %fold.1.acc, bf16[512,1024]{1,0:T(8,128)(2,1)S(1)} %broadcast_select_fusion.1.refs_0_, bf16[512,1024]{1,0:T(8,128)(2,1)S(1)} %broadcast_select_fusion.refs_1_, ...), custom_call_target="tpu_custom_call" | custom-call | flops 1 | bytes 1 | tf_op jit(solution)/shard_map/finish/pallas_call | solution.py:280
  154.7 4.2 %finish.3 = bf16[512,2048]{1,0:T(8,128)(2,1)} custom-call(s32[4]{0:T(128)S(1)} %pad_add_fusion.ids, s32[16]{0:T(128)S(1)} %copy-done.5, s32[8]{0:T(128)S(1)} %copy-done.6, f32[512,2048]{1,0:T(8,128)S(1)} %fold.1.acc, bf16[512,1024]{1,0:T(8,128)(2,1)S(1)} %broadcast_select_fusion.1.refs_0_, ...), custom_call_target="tpu_custom_call", output_to_operand_aliasing={{}: (10, {})} | custom-call | flops 1 | bytes 1 | tf_op jit(solution)/shard_map/finish/pallas_call | solution.py:280
  (67 shorter events, 11.1 us)
Async XLA Ops:
  3.3 24.2 %collective-permute-start.2 = (bf16[256,1024]{1,0:T(8,128)(2,1)}, bf16[256,1024]{1,0:T(8,128)(2,1)}, u32[]{:S(2)}, u32[]{:S(2)}) collective-permute-start(bf16[256,1024]{1,0:T(8,128)(2,1)} %get-tuple-element.83), channel_id=1, source_target_pairs={{0,1},{1,0},{2,3},{3,2},{4,5},{5,4},{6,7},{7,6},{8,9},{9,8},{10,11... | collective-permute-start | bytes 1572872 | tf_op jit(solution)/shard_map/piece1/ppermute | solution.py:22
  6.3 25.8 %collective-permute-start.3 = (bf16[256,1024]{1,0:T(8,128)(2,1)}, bf16[256,1024]{1,0:T(8,128)(2,1)}, u32[]{:S(2)}, u32[]{:S(2)}) collective-permute-start(bf16[256,1024]{1,0:T(8,128)(2,1)} %get-tuple-element.82), channel_id=1, source_target_pairs={{0,3},{1,2},{2,1},{3,0},{4,7},{5,6},{6,5},{7,4},{8,11},{9,10},{10,... | collective-permute-start | bytes 1572872 | tf_op jit(solution)/shard_map/piece3/ppermute | solution.py:22
  8.8 23.3 %collective-permute-start.4 = (bf16[2,64,2048]{2,1,0:T(8,128)(2,1)S(1)}, bf16[2,64,2048]{2,1,0:T(8,128)(2,1)S(1)}, u32[]{:S(2)}, u32[]{:S(2)}) collective-permute-start(bf16[2,64,2048]{2,1,0:T(8,128)(2,1)S(1)} %bitcast.7), channel_id=1, source_target_pairs={{0,8},{4,12},{8,0},{12,4},{1,9},{5,13},{9,1},{13,5},{2,10},{6,14},... | collective-permute-start | bytes 1572872 | tf_op jit(solution)/shard_map/down1_0/ppermute | solution.py:22
  10.3 17.2 %collective-permute-start.5 = (bf16[2,64,1024]{2,1,0:T(8,128)(2,1)S(1)}, bf16[2,64,1024]{2,1,0:T(8,128)(2,1)S(1)}, u32[]{:S(2)}, u32[]{:S(2)}) collective-permute-start(bf16[2,64,1024]{2,1,0:T(8,128)(2,1)S(1)} %copy-done.4), channel_id=1, source_target_pairs={{0,8},{4,12},{8,0},{12,4},{1,9},{5,13},{9,1},{13,5},{2,10},{6,14},... | collective-permute-start | bytes 786440 | tf_op jit(solution)/shard_map/up1_0/ppermute | solution.py:22
  32.1 4.2 %collective-permute-start.10 = (bf16[2,64,2048]{2,1,0:T(8,128)(2,1)S(1)}, bf16[2,64,2048]{2,1,0:T(8,128)(2,1)S(1)}, u32[]{:S(2)}, u32[]{:S(2)}) collective-permute-start(bf16[2,64,2048]{2,1,0:T(8,128)(2,1)S(1)} %collective-permute-done.4.refs_2_.refs_6_), channel_id=1, source_target_pairs={{0,4},{4,0},{8,12},{12,8},{1,5},{5,1},{9,13},{13,9},{2,6},{6,2},{1... | collective-permute-start | bytes 1572872 | tf_op jit(solution)/shard_map/down0_1/ppermute | solution.py:22
  32.1 2.3 %collective-permute-start.11 = (bf16[2,64,1024]{2,1,0:T(8,128)(2,1)S(1)}, bf16[2,64,1024]{2,1,0:T(8,128)(2,1)S(1)}, u32[]{:S(2)}, u32[]{:S(2)}) collective-permute-start(bf16[2,64,1024]{2,1,0:T(8,128)(2,1)S(1)} %collective-permute-done.5.refs_3_), channel_id=1, source_target_pairs={{0,4},{4,0},{8,12},{12,8},{1,5},{5,1},{9,13},{13,9},{2,6},{6,2},{1... | collective-permute-start | bytes 786440 | tf_op jit(solution)/shard_map/up0_1/ppermute | solution.py:22
  32.6 2.1 %collective-permute-start.9 = (bf16[2,64,1024]{2,1,0:T(8,128)(2,1)S(1)}, bf16[2,64,1024]{2,1,0:T(8,128)(2,1)S(1)}, u32[]{:S(2)}, u32[]{:S(2)}) collective-permute-start(bf16[2,64,1024]{2,1,0:T(8,128)(2,1)S(1)} %copy-done.4), channel_id=1, source_target_pairs={{0,4},{4,0},{8,12},{12,8},{1,5},{5,1},{9,13},{13,9},{2,6},{6,2},{1... | collective-permute-start | bytes 786440 | tf_op jit(solution)/shard_map/up0_0/ppermute | solution.py:22
  32.6 34.3 %collective-permute-start = (bf16[512,1024]{1,0:T(8,128)(2,1)S(1)}, bf16[512,1024]{1,0:T(8,128)(2,1)S(1)}, u32[]{:S(2)}, u32[]{:S(2)}) collective-permute-start(bf16[512,1024]{1,0:T(8,128)(2,1)S(1)} %copy-done.1), channel_id=1, source_target_pairs={{0,1},{1,0},{2,3},{3,2},{4,5},{5,4},{6,7},{7,6},{8,9},{9,8},{10,11... | collective-permute-start | bytes 3145736 | tf_op jit(solution)/shard_map/outer/ppermute | solution.py:22
  33.2 33.7 %collective-permute-start.1 = (bf16[512,1024]{1,0:T(8,128)(2,1)S(1)}, bf16[512,1024]{1,0:T(8,128)(2,1)S(1)}, u32[]{:S(2)}, u32[]{:S(2)}) collective-permute-start(bf16[512,1024]{1,0:T(8,128)(2,1)S(1)} %copy-done.1), channel_id=1, source_target_pairs={{1,2},{2,1},{5,6},{6,5},{9,10},{10,9},{13,14},{14,13},{17,18},{18,... | collective-permute-start | bytes 3145736 | tf_op jit(solution)/shard_map/inner/ppermute | solution.py:22
  34.4 2.4 %collective-permute-start.8 = (bf16[2,64,2048]{2,1,0:T(8,128)(2,1)S(1)}, bf16[2,64,2048]{2,1,0:T(8,128)(2,1)S(1)}, u32[]{:S(2)}, u32[]{:S(2)}) collective-permute-start(bf16[2,64,2048]{2,1,0:T(8,128)(2,1)S(1)} %bitcast.8), channel_id=1, source_target_pairs={{0,4},{4,0},{8,12},{12,8},{1,5},{5,1},{9,13},{13,9},{2,6},{6,2},{1... | collective-permute-start | bytes 1572872 | tf_op jit(solution)/shard_map/down0_0/ppermute | solution.py:22
  34.7 9.4 %collective-permute-start.7 = (bf16[256,1024]{1,0:T(8,128)(2,1)}, bf16[256,1024]{1,0:T(8,128)(2,1)S(1)}, u32[]{:S(2)}, u32[]{:S(2)}) collective-permute-start(bf16[256,1024]{1,0:T(8,128)(2,1)} %collective-permute-done.3), channel_id=1, source_target_pairs={{0,16},{4,12},{8,24},{12,4},{16,0},{20,28},{24,8},{28,20},{1,17},{... | collective-permute-start | bytes 1572872 | tf_op jit(solution)/shard_map/turn_a3/ppermute | solution.py:22
  36.2 13.5 %collective-permute-start.6 = (bf16[256,1024]{1,0:T(8,128)(2,1)}, bf16[256,1024]{1,0:T(8,128)(2,1)S(1)}, u32[]{:S(2)}, u32[]{:S(2)}) collective-permute-start(bf16[256,1024]{1,0:T(8,128)(2,1)} %collective-permute-done.2), channel_id=1, source_target_pairs={{0,16},{4,12},{8,24},{12,4},{16,0},{20,28},{24,8},{28,20},{1,17},{... | collective-permute-start | bytes 1572872 | tf_op jit(solution)/shard_map/turn_a1/ppermute | solution.py:22
  40.0 26.8 %collective-permute-start.12 = (bf16[512,128]{1,0:T(8,128)(2,1)S(1)}, bf16[512,128]{1,0:T(8,128)(2,1)S(1)}, u32[]{:S(2)}, u32[]{:S(2)}) collective-permute-start(bf16[512,128]{1,0:T(8,128)(2,1)S(1)} %rank_partials.1), channel_id=1, source_target_pairs={{0,2},{1,3},{2,0},{3,1},{4,6},{5,7},{6,4},{7,5},{8,10},{9,11},{10,... | collective-permute-start | bytes 393224 | tf_op jit(solution)/shard_map/rank_sum1/ppermute | solution.py:22
  66.9 27.0 %collective-permute-start.14 = (bf16[512,1024]{1,0:T(8,128)(2,1)S(1)}, bf16[512,1024]{1,0:T(8,128)(2,1)S(1)}, u32[]{:S(2)}, u32[]{:S(2)}) collective-permute-start(bf16[512,1024]{1,0:T(8,128)(2,1)S(1)} %pad_maximum_fusion.refs_1_), channel_id=1, source_target_pairs={{0,8},{4,20},{8,0},{12,28},{16,24},{20,4},{24,16},{28,12},{1,9},{5... | collective-permute-start | bytes 3145736 | tf_op jit(solution)/shard_map/turn_b1/ppermute | solution.py:22
  68.5 25.4 %collective-permute-start.15 = (bf16[512,1024]{1,0:T(8,128)(2,1)S(1)}, bf16[512,1024]{1,0:T(8,128)(2,1)S(1)}, u32[]{:S(2)}, u32[]{:S(2)}) collective-permute-start(bf16[512,1024]{1,0:T(8,128)(2,1)S(1)} %pad_maximum_fusion.1.refs_4_), channel_id=1, source_target_pairs={{0,8},{4,20},{8,0},{12,28},{16,24},{20,4},{24,16},{28,12},{1,9},{5... | collective-permute-start | bytes 3145736 | tf_op jit(solution)/shard_map/turn_b3/ppermute | solution.py:22
  69.0 6.3 %collective-permute-start.16 = (bf16[512,128]{1,0:T(8,128)(2,1)S(1)}, bf16[512,128]{1,0:T(8,128)(2,1)S(1)}, u32[]{:S(2)}, u32[]{:S(2)}) collective-permute-start(bf16[512,128]{1,0:T(8,128)(2,1)S(1)} %add_convert_fusion.2), channel_id=1, source_target_pairs={{0,1},{1,0},{2,3},{3,2},{4,5},{5,4},{6,7},{7,6},{8,9},{9,8},{10,11... | collective-permute-start | bytes 393224 | tf_op jit(solution)/shard_map/rank_sum0/ppermute | solution.py:22
  69.0 24.9 %collective-permute-start.13 = (bf16[256,1024]{1,0:T(8,128)(2,1)S(1)}, bf16[256,1024]{1,0:T(8,128)(2,1)S(1)}, u32[]{:S(2)}, u32[]{:S(2)}) collective-permute-start(bf16[256,1024]{1,0:T(8,128)(2,1)S(1)} %get-tuple-element.51), channel_id=1, source_target_pairs={{0,2},{1,3},{2,0},{3,1},{4,6},{5,7},{6,4},{7,5},{8,10},{9,11},{10,... | collective-permute-start | bytes 1572872 | tf_op jit(solution)/shard_map/piece2/ppermute | solution.py:22
  78.8 2.3 %collective-permute-start.18 = (bf16[1,64,3072]{2,1,0:T(8,128)(2,1)S(1)}, bf16[1,64,3072]{2,1,0:T(8,128)(2,1)S(1)}, u32[]{:S(2)}, u32[]{:S(2)}) collective-permute-start(bf16[1,64,3072]{2,1,0:T(8,128)(2,1)S(1)} %get-tuple-element.56), channel_id=1, source_target_pairs={{0,4},{4,0},{8,12},{12,8},{1,5},{5,1},{9,13},{13,9},{2,6},{6,2},{1... | collective-permute-start | bytes 1179656 | tf_op jit(solution)/shard_map/grads0_3/ppermute | solution.py:22
  93.9 25.4 %collective-permute-start.19 = (bf16[512,1024]{1,0:T(8,128)(2,1)S(1)}, bf16[512,1024]{1,0:T(8,128)(2,1)S(1)}, u32[]{:S(2)}, u32[]{:S(2)}) collective-permute-start(bf16[512,1024]{1,0:T(8,128)(2,1)S(1)} %collective-permute-done.1), channel_id=1, source_target_pairs={{1,0},{2,3},{5,4},{6,7},{9,8},{10,11},{13,12},{14,15},{17,16},{18,... | collective-permute-start | bytes 3145736 | tf_op jit(solution)/shard_map/inner_out/ppermute | solution.py:22
  95.4 23.7 %collective-permute-start.22 = (bf16[2,64,3072]{2,1,0:T(8,128)(2,1)S(1)}, bf16[2,64,3072]{2,1,0:T(8,128)(2,1)S(1)}, u32[]{:S(2)}, u32[]{:S(2)}) collective-permute-start(bf16[2,64,3072]{2,1,0:T(8,128)(2,1)S(1)} %add_convert_fusion), channel_id=1, source_target_pairs={{0,8},{4,12},{8,0},{12,4},{1,9},{5,13},{9,1},{13,5},{2,10},{6,14},... | collective-permute-start | bytes 2359304 | tf_op jit(solution)/shard_map/grads1/ppermute | solution.py:22
  96.9 22.7 %collective-permute-start.20 = (bf16[512,1024]{1,0:T(8,128)(2,1)S(1)}, bf16[512,1024]{1,0:T(8,128)(2,1)S(1)}, u32[]{:S(2)}, u32[]{:S(2)}) collective-permute-start(bf16[512,1024]{1,0:T(8,128)(2,1)S(1)} %collective-permute-done.refs_0_), channel_id=1, source_target_pairs={{1,2},{2,1},{5,6},{6,5},{9,10},{10,9},{13,14},{14,13},{17,18},{18,... | collective-permute-start | bytes 3145736 | tf_op jit(solution)/shard_map/outer_in/ppermute | solution.py:22
  97.7 9.2 %collective-permute-start.21 = (bf16[256,1024]{1,0:T(8,128)(2,1)S(1)}, bf16[256,1024]{1,0:T(8,128)(2,1)S(1)}, u32[]{:S(2)}, u32[]{:S(2)}) collective-permute-start(bf16[256,1024]{1,0:T(8,128)(2,1)S(1)} %collective-permute-done.13), channel_id=1, source_target_pairs={{0,16},{4,12},{8,24},{12,4},{16,0},{20,28},{24,8},{28,20},{1,17},{... | collective-permute-start | bytes 1572872 | tf_op jit(solution)/shard_map/turn_a2/ppermute | solution.py:22
  99.2 20.7 %collective-permute-start.27 = (bf16[1,64,3072]{2,1,0:T(8,128)(2,1)S(1)}, bf16[1,64,3072]{2,1,0:T(8,128)(2,1)S(1)}, u32[]{:S(2)}, u32[]{:S(2)}) collective-permute-start(bf16[1,64,3072]{2,1,0:T(8,128)(2,1)S(1)} %get-tuple-element.69), channel_id=1, source_target_pairs={{0,4},{4,0},{8,12},{12,8},{1,5},{5,1},{9,13},{13,9},{2,6},{6,2},{1... | collective-permute-start | bytes 1179656 | tf_op jit(solution)/shard_map/grads0_0/ppermute | solution.py:22
  106.9 14.6 %collective-permute-start.28 = (bf16[1,64,3072]{2,1,0:T(8,128)(2,1)S(1)}, bf16[1,64,3072]{2,1,0:T(8,128)(2,1)S(1)}, u32[]{:S(2)}, u32[]{:S(2)}) collective-permute-start(bf16[1,64,3072]{2,1,0:T(8,128)(2,1)S(1)} %get-tuple-element.70), channel_id=1, source_target_pairs={{0,4},{4,0},{8,12},{12,8},{1,5},{5,1},{9,13},{13,9},{2,6},{6,2},{1... | collective-permute-start | bytes 1179656 | tf_op jit(solution)/shard_map/grads0_1/ppermute | solution.py:22
  119.1 4.2 %collective-permute-start.24 = (bf16[512,1024]{1,0:T(8,128)(2,1)S(1)}, bf16[512,1024]{1,0:T(8,128)(2,1)S(1)}, u32[]{:S(2)}, u32[]{:S(2)}) collective-permute-start(bf16[512,1024]{1,0:T(8,128)(2,1)S(1)} %pad_maximum_fusion.refs_1_), channel_id=1, source_target_pairs={{0,4},{4,0},{8,12},{12,8},{16,20},{20,16},{24,28},{28,24},{1,5},{5... | collective-permute-start | bytes 3145736 | tf_op jit(solution)/shard_map/turn_c10/ppermute | solution.py:22
  119.3 4.1 %collective-permute-start.25 = (bf16[512,1024]{1,0:T(8,128)(2,1)S(1)}, bf16[512,1024]{1,0:T(8,128)(2,1)S(1)}, u32[]{:S(2)}, u32[]{:S(2)}) collective-permute-start(bf16[512,1024]{1,0:T(8,128)(2,1)S(1)} %collective-permute-done.14.refs_2_), channel_id=1, source_target_pairs={{0,4},{4,0},{8,12},{12,8},{16,20},{20,16},{24,28},{28,24},{1,5},{5... | collective-permute-start | bytes 3145736 | tf_op jit(solution)/shard_map/turn_c11/ppermute | solution.py:22
  119.7 35.0 %collective-permute-start.31 = (bf16[512,1024]{1,0:T(8,128)(2,1)S(1)}, bf16[512,1024]{1,0:T(8,128)(2,1)S(1)}, u32[]{:S(2)}, u32[]{:S(2)}) collective-permute-start(bf16[512,1024]{1,0:T(8,128)(2,1)S(1)} %pad_maximum_fusion.1.refs_4_), channel_id=1, source_target_pairs={{0,4},{4,0},{8,12},{12,8},{16,20},{20,16},{24,28},{28,24},{1,5},{5... | collective-permute-start | bytes 3145736 | tf_op jit(solution)/shard_map/turn_c30/ppermute | solution.py:22
  120.0 14.8 %collective-permute-start.23 = (bf16[512,1024]{1,0:T(8,128)(2,1)S(1)}, bf16[512,1024]{1,0:T(8,128)(2,1)S(1)}, u32[]{:S(2)}, u32[]{:S(2)}) collective-permute-start(bf16[512,1024]{1,0:T(8,128)(2,1)S(1)} %pad_maximum_fusion.2.refs_2_), channel_id=1, source_target_pairs={{0,8},{4,20},{8,0},{12,28},{16,24},{20,4},{24,16},{28,12},{1,9},{5... | collective-permute-start | bytes 3145736 | tf_op jit(solution)/shard_map/turn_b2/ppermute | solution.py:22
  121.5 28.4 %collective-permute-start.26 = (bf16[512,1024]{1,0:T(8,128)(2,1)S(1)}, bf16[512,1024]{1,0:T(8,128)(2,1)S(1)}, u32[]{:S(2)}, u32[]{:S(2)}) collective-permute-start(bf16[512,1024]{1,0:T(8,128)(2,1)S(1)} %collective-permute-done.20), channel_id=1, source_target_pairs={{1,0},{2,3},{5,4},{6,7},{9,8},{10,11},{13,12},{14,15},{17,16},{18,... | collective-permute-start | bytes 3145736 | tf_op jit(solution)/shard_map/outer_in_out/ppermute | solution.py:22
  123.3 31.4 %collective-permute-start.32 = (bf16[512,1024]{1,0:T(8,128)(2,1)S(1)}, bf16[512,1024]{1,0:T(8,128)(2,1)S(1)}, u32[]{:S(2)}, u32[]{:S(2)}) collective-permute-start(bf16[512,1024]{1,0:T(8,128)(2,1)S(1)} %collective-permute-done.15.refs_5_), channel_id=1, source_target_pairs={{0,4},{4,0},{8,12},{12,8},{16,20},{20,16},{24,28},{28,24},{1,5},{5... | collective-permute-start | bytes 3145736 | tf_op jit(solution)/shard_map/turn_c31/ppermute | solution.py:22
  149.8 4.9 %collective-permute-start.29 = (bf16[512,1024]{1,0:T(8,128)(2,1)S(1)}, bf16[512,1024]{1,0:T(8,128)(2,1)S(1)}, u32[]{:S(2)}, u32[]{:S(2)}) collective-permute-start(bf16[512,1024]{1,0:T(8,128)(2,1)S(1)} %pad_maximum_fusion.2.refs_2_), channel_id=1, source_target_pairs={{0,4},{4,0},{8,12},{12,8},{16,20},{20,16},{24,28},{28,24},{1,5},{5... | collective-permute-start | bytes 3145736 | tf_op jit(solution)/shard_map/turn_c20/ppermute | solution.py:22
  150.1 4.6 %collective-permute-start.30 = (bf16[512,1024]{1,0:T(8,128)(2,1)S(1)}, bf16[512,1024]{1,0:T(8,128)(2,1)S(1)}, u32[]{:S(2)}, u32[]{:S(2)}) collective-permute-start(bf16[512,1024]{1,0:T(8,128)(2,1)S(1)} %collective-permute-done.23.refs_3_), channel_id=1, source_target_pairs={{0,4},{4,0},{8,12},{12,8},{16,20},{20,16},{24,28},{28,24},{1,5},{5... | collective-permute-start | bytes 3145736 | tf_op jit(solution)/shard_map/turn_c21/ppermute | solution.py:22
  (8 other events, 95.9 us)

commit v5 on v4

--- a/solution.py
+++ b/solution.py
@@ -395,32 +395,44 @@
         both = rank_sum(1, both)
         by_one, across, wide1, wide3, both, cut2 = together(by_one, across, wide1, wide3, both, cut2)
 
+        half = tokens // 2
+        one0, one1, over0, over1 = by_one[:half], by_one[half:], across[:half], across[half:]
         piece2 = piece(2, cut2)
+        end_two0 = move("inner_out0", over0, "tensor", outward)
         wide1 = [wide1, move("turn_b1", wide1, copies, turn_b)]
         wide3 = [wide3, move("turn_b3", wide3, copies, turn_b)]
         both = rank_sum(0, both)
         sends, keep = grads(both)
         rest = len(sends) // 2
+        one0, one1, over1, end_two0, piece2, wide1, wide3, sends = together(
+            one0, one1, over1, end_two0, piece2, wide1, wide3, sends
+        )
+
+        end_two1 = move("inner_out1", over1, "tensor", outward)
+        two0 = move("outer_in0", one0, "tensor", inner)
+        two1 = move("outer_in1", one1, "tensor", inner)
+        end_three0 = move("outer_in_out0", two0, "tensor", outward)
+        wide2 = turned("turn_a2", piece2, turn_a)
         got = [swap(f"grads0_{i}", one, "dp", nd, bits[1]) for i, one in enumerate(sends)]
-        by_one, across, piece2, wide1, wide3, far = together(by_one, across, piece2, wide1, wide3, got[rest:])
-
-        end_two = move("inner_out", across, "tensor", outward)
-        by_two = move("outer_in", by_one, "tensor", inner)
-        wide2 = turned("turn_a2", piece2, turn_a)
-        far = keep[rest:].astype(F32) + jnp.concatenate(far, axis=0).astype(F32)
+        far = keep[rest:].astype(F32) + jnp.concatenate(got[rest:], axis=0).astype(F32)
         far = swap("grads1", far.astype(BF), "dp", nd, bits[0])
-        end_two, by_two, wide2, far = together(end_two, by_two, wide2, far)
-
-        end_three = move("outer_in_out", by_two, "tensor", outward)
+        end_two1, two0, two1, end_three0, wide1, wide2, far = together(
+            end_two1, two0, two1, end_three0, wide1, wide2, far
+        )
+
+        end_three1 = move("outer_in_out1", two1, "tensor", outward)
         wide2 = [wide2, move("turn_b2", wide2, copies, turn_b)]
         other1 = [move(f"turn_c1{i}", part, copies, turn_c) for i, part in enumerate(wide1)]
         acc = folded(acc, [by_one], [wide1 + other1], relative_tile, 0, table=[pair[0] for pair in table], both=both)
-        two = jnp.where(middle, by_two, end_two)
+        two = jnp.where(
+            middle, jnp.concatenate([two0, two1], axis=0), jnp.concatenate([end_two0, end_two1], axis=0)
+        )
         total = keep[:rest].astype(F32) + jnp.concatenate(got[:rest], axis=0).astype(F32) + far.astype(F32)
         grad_down, grad_up = jnp.swapaxes(total[:, :, :width], 1, 2), total[:, :, width:]
-        wide2, acc, end_three, two, grad_down, grad_up = together(
-            wide2, acc, end_three, two, grad_down, grad_up
+        wide2, acc, end_three1, two, grad_down, grad_up = together(
+            wide2, acc, end_three1, two, grad_down, grad_up
         )
+        end_three = jnp.concatenate([end_three0, end_three1], axis=0)
 
         other2 = [move(f"turn_c2{i}", part, copies, turn_c) for i, part in enumerate(wide2)]
         other3 = [move(f"turn_c3{i}", part, copies, turn_c) for i, part in enumerate(wide3)]

time: 159 us -> 153 us (0.962)
  starting transfers between devices: 41.1 us -> 34 us
    ppermute x33 -> x36, starting transfers between devices: 41.1 us -> 34 us  [move(): return lax.ppermute(a, axis, pairs)]
    ppermute x33 -> x36, waiting for transfers between devices: 75.4 us -> 75.1 us  [move(): return lax.ppermute(a, axis, pairs)]
  transfers between devices with their start and end apart: 33 -> 36, of which waited for: 16 -> 13; matrix products, arithmetic and copies ran while one was open for 3% -> 4% of each run, Pallas kernels for 15% -> 16%
where the time goes in v5:
time: 153 us; the launch traced here: 152 us
  waiting for transfers between devices  75.1 us (49%)
  starting transfers between devices  34 us (22%)
  Pallas kernels  28.1 us (18%)
  local copies, waits for them, and re-layouts  10.4 us (7%)
  other arithmetic  3.83 us (3%)
    ppermute x36, waiting for transfers between devices, move(): return lax.ppermute(a, axis, pairs)  75.1 us
    ppermute x36, starting transfers between devices, move(): return lax.ppermute(a, axis, pairs)  34 us
    pallas_call x3, Pallas kernels, fold(): pl.pallas_call(functools.partial(fold_kernel, terms=len(xs), parts=parts,...  17.6 us
    unnamed x14, local copies, waits for them, and re-layouts  5.79 us
    pallas_call x1, Pallas kernels, local_products(): pl.pallas_call(local_kernel, grid_spec=pltpu.PrefetchScalarGridSpec(num_s...  3.8 us
    pallas_call x1, Pallas kernels, member_grads(): pl.pallas_call(functools.partial(grads_kernel, width=width, blocks=blocks...  3.44 us
    pallas_call x1, Pallas kernels, rank_partials(): pl.pallas_call(functools.partial(rank_kernel, blocks=blocks, slot=slot, h...  3.26 us
  transfers between devices with their start and end apart: 36, of which 13 were waited for; matrix products, arithmetic and copies ran while one was open for 4% of the time, Pallas kernels for 16%

profile of v5, /device:TPU:0, one launch (start us, length us, event | category | flops | bytes accessed | tf_op | source)
XLA Modules:
  0.0 152.4 jit_solution(16188670442018431264)
XLA Ops:
  0.7 2.6 %constant_dynamic-slice_fusion = (bf16[256,1024]{1,0:T(8,128)(2,1)S(1)}, bf16[256,1024]{1,0:T(8,128)(2,1)}, bf16[256,1024]{1,0:T(8,128)(2,1)}) fusion(bf16[8192,1024]{1,0:T(8,128)(2,1)} %weight.1, s32[]{:T(128)S(6)} %select_n.40, s32[]{:T(128)S(6)} %select_n.39, s32[]{:T(128)S(6)} %select_n.38), kind=kLoop, calls=%fused_computation.10 | loop fusion | bytes 3145740 | tf_op jit(solution)/shard_map/dynamic_slice | solution.py:343
  3.3 3.0 %collective-permute-start.2 = (bf16[256,1024]{1,0:T(8,128)(2,1)}, bf16[256,1024]{1,0:T(8,128)(2,1)}, u32[]{:S(2)}, u32[]{:S(2)}) collective-permute-start(bf16[256,1024]{1,0:T(8,128)(2,1)} %get-tuple-element.99), channel_id=1, source_target_pairs={{0,1},{1,0},{2,3},{3,2},{4,5},{5,4},{6,7},{7,6},{8,9},{9,8},{10,11... | collective-permute-start | bytes 1572872 | tf_op jit(solution)/shard_map/piece1/ppermute | solution.py:22
  6.3 2.5 %collective-permute-start.3 = (bf16[256,1024]{1,0:T(8,128)(2,1)}, bf16[256,1024]{1,0:T(8,128)(2,1)}, u32[]{:S(2)}, u32[]{:S(2)}) collective-permute-start(bf16[256,1024]{1,0:T(8,128)(2,1)} %get-tuple-element.98), channel_id=1, source_target_pairs={{0,3},{1,2},{2,1},{3,0},{4,7},{5,6},{6,5},{7,4},{8,11},{9,10},{10,... | collective-permute-start | bytes 1572872 | tf_op jit(solution)/shard_map/piece3/ppermute | solution.py:22
  8.8 1.5 collective-permute-start.4
  10.9 5.8 %copy-done = bf16[8192,1024]{1,0:T(8,128)(2,1)S(1)} copy-done((bf16[8192,1024]{1,0:T(8,128)(2,1)S(1)}, bf16[8192,1024]{1,0:T(8,128)(2,1)}, u32[]{:S(2)}) %copy-start) | copy-done | bytes 16777240
  16.7 3.8 %local_products.1.acc = f32[512,2048]{1,0:T(8,128)S(1)} custom-call(s32[4]{0:T(128)S(1)} %pad_add_fusion.ids, bf16[512,1024]{1,0:T(8,128)(2,1)S(1)} %copy-done.1, bf16[8192,1024]{1,0:T(8,128)(2,1)S(1)} %copy-done), custom_call_target="tpu_custom_call" | custom-call | flops 1 | bytes 1 | tf_op jit(solution)/shard_map/local_products/pallas_call | solution.py:195
  20.5 7.0 %collective-permute-done.5.refs_3_ = bf16[2,64,1024]{2,1,0:T(8,128)(2,1)S(1)} collective-permute-done((bf16[2,64,1024]{2,1,0:T(8,128)(2,1)S(1)}, bf16[2,64,1024]{2,1,0:T(8,128)(2,1)S(1)}, u32[]{:S(2)}, u32[]{:S(2)}) %collective-permute-start.5) | collective-permute-done | bytes 262176 | tf_op jit(solution)/shard_map/up1_0/ppermute | solution.py:22
  27.5 4.6 %collective-permute-done.3 = bf16[256,1024]{1,0:T(8,128)(2,1)} collective-permute-done((bf16[256,1024]{1,0:T(8,128)(2,1)}, bf16[256,1024]{1,0:T(8,128)(2,1)}, u32[]{:S(2)}, u32[]{:S(2)}) %collective-permute-start.3) | collective-permute-done | bytes 524320 | tf_op jit(solution)/shard_map/piece3/ppermute | solution.py:22
  34.7 1.5 collective-permute-start.7
  36.8 3.3 %rank_partials.1 = bf16[512,128]{1,0:T(8,128)(2,1)S(1)} custom-call(s32[4]{0:T(128)S(1)} %pad_add_fusion.ids, s32[16]{0:T(128)S(1)} %copy-done.5, s32[8]{0:T(128)S(1)} %copy-done.6, bf16[512,2048]{1,0:T(8,128)(2,1)S(1)} %copy-done.2, bf16[512,1024]{1,0:T(8,128)(2,1)S(1)} %copy-done.1, bf16[2,64,2048]{2,1,0:T(8,128)(2,1)S(1)} %bitcast.9, ...), custom_call_target="tpu_custom_call" | custom-call | flops 1 | bytes 1 | tf_op jit(solution)/shard_map/rank_partials/pallas_call | solution.py:89
  40.1 3.5 %collective-permute-start.12 = (bf16[512,128]{1,0:T(8,128)(2,1)S(1)}, bf16[512,128]{1,0:T(8,128)(2,1)S(1)}, u32[]{:S(2)}, u32[]{:S(2)}) collective-permute-start(bf16[512,128]{1,0:T(8,128)(2,1)S(1)} %rank_partials.1), channel_id=1, source_target_pairs={{0,2},{1,3},{2,0},{3,1},{4,6},{5,7},{6,4},{7,5},{8,10},{9,11},{10,... | collective-permute-start | bytes 393224 | tf_op jit(solution)/shard_map/rank_sum1/ppermute | solution.py:22
  45.2 4.5 %collective-permute-done.6 = bf16[256,1024]{1,0:T(8,128)(2,1)S(1)} collective-permute-done((bf16[256,1024]{1,0:T(8,128)(2,1)}, bf16[256,1024]{1,0:T(8,128)(2,1)S(1)}, u32[]{:S(2)}, u32[]{:S(2)}) %collective-permute-start.6) | collective-permute-done | bytes 524320 | tf_op jit(solution)/shard_map/turn_a1/ppermute | solution.py:22
  50.9 16.0 %collective-permute-done.12 = bf16[512,128]{1,0:T(8,128)(2,1)S(1)} collective-permute-done((bf16[512,128]{1,0:T(8,128)(2,1)S(1)}, bf16[512,128]{1,0:T(8,128)(2,1)S(1)}, u32[]{:S(2)}, u32[]{:S(2)}) %collective-permute-start.12) | collective-permute-done | bytes 131104 | tf_op jit(solution)/shard_map/rank_sum1/ppermute | solution.py:22
  66.9 1.6 %collective-permute-start.15 = (bf16[512,1024]{1,0:T(8,128)(2,1)S(1)}, bf16[512,1024]{1,0:T(8,128)(2,1)S(1)}, u32[]{:S(2)}, u32[]{:S(2)}) collective-permute-start(bf16[512,1024]{1,0:T(8,128)(2,1)S(1)} %pad_maximum_fusion.refs_1_), channel_id=1, source_target_pairs={{0,8},{4,20},{8,0},{12,28},{16,24},{20,4},{24,16},{28,12},{1,9},{5... | collective-permute-start | bytes 3145736 | tf_op jit(solution)/shard_map/turn_b1/ppermute | solution.py:22
  69.1 1.3 collective-permute-start.13
  70.4 2.7 %collective-permute-start.14 = (bf16[256,1024]{1,0:T(8,128)(2,1)S(1)}, bf16[256,1024]{1,0:T(8,128)(2,1)S(1)}, u32[]{:S(2)}, u32[]{:S(2)}) collective-permute-start(bf16[256,1024]{1,0:T(8,128)(2,1)S(1)} %get-tuple-element.59), channel_id=1, source_target_pairs={{0,2},{1,3},{2,0},{3,1},{4,6},{5,7},{6,4},{7,5},{8,10},{9,11},{10,... | collective-permute-start | bytes 1572872 | tf_op jit(solution)/shard_map/piece2/ppermute | solution.py:22
  73.1 4.1 %collective-permute-done.17 = bf16[512,128]{1,0:T(8,128)(2,1)S(1)} collective-permute-done((bf16[512,128]{1,0:T(8,128)(2,1)S(1)}, bf16[512,128]{1,0:T(8,128)(2,1)S(1)}, u32[]{:S(2)}, u32[]{:S(2)}) %collective-permute-start.17) | collective-permute-done | bytes 131104 | tf_op jit(solution)/shard_map/rank_sum0/ppermute | solution.py:22
  77.4 3.4 %member_grads.1 = (bf16[1,64,3072]{2,1,0:T(8,128)(2,1)S(1)}, bf16[1,64,3072]{2,1,0:T(8,128)(2,1)S(1)}, bf16[1,64,3072]{2,1,0:T(8,128)(2,1)S(1)}, bf16[1,64,3072]...) custom-call(s32[4]{0:T(128)S(1)} %pad_add_fusion.ids, s32[16]{0:T(128)S(1)} %copy-done.5, bf16[512,2048]{1,0:T(8,128)(2,1)S(1)} %copy-done.2, ...), custom_call_target="tpu_custom_call" | custom-call | flops 1 | bytes 1 | tf_op jit(solution)/shard_map/member_grads/pallas_call | solution.py:141
  80.8 15.5 %collective-permute-done.13 = bf16[256,1024]{1,0:T(8,128)(2,1)S(1)} collective-permute-done((bf16[256,1024]{1,0:T(8,128)(2,1)S(1)}, bf16[256,1024]{1,0:T(8,128)(2,1)S(1)}, u32[]{:S(2)}, u32[]{:S(2)}) %collective-permute-start.13) | collective-permute-done | bytes 524320 | tf_op jit(solution)/shard_map/inner_out0/ppermute | solution.py:22
  96.9 1.5 collective-permute-start.22
  99.1 1.3 collective-permute-start.18
  100.6 1.6 %collective-permute-start.25 = (bf16[2,64,3072]{2,1,0:T(8,128)(2,1)S(1)}, bf16[2,64,3072]{2,1,0:T(8,128)(2,1)S(1)}, u32[]{:S(2)}, u32[]{:S(2)}) collective-permute-start(bf16[2,64,3072]{2,1,0:T(8,128)(2,1)S(1)} %add_convert_fusion), channel_id=1, source_target_pairs={{0,8},{4,12},{8,0},{12,4},{1,9},{5,13},{9,1},{13,5},{2,10},{6,14},... | collective-permute-start | bytes 2359304 | tf_op jit(solution)/shard_map/grads1/ppermute | solution.py:22
  102.9 1.3 collective-permute-start.21
  104.2 1.9 %collective-permute-done.22 = bf16[256,1024]{1,0:T(8,128)(2,1)S(1)} collective-permute-done((bf16[256,1024]{1,0:T(8,128)(2,1)S(1)}, bf16[256,1024]{1,0:T(8,128)(2,1)S(1)}, u32[]{:S(2)}, u32[]{:S(2)}) %collective-permute-start.22) | collective-permute-done | bytes 524320 | tf_op jit(solution)/shard_map/turn_a2/ppermute | solution.py:22
  106.2 8.5 %collective-permute-done.18 = bf16[256,1024]{1,0:T(8,128)(2,1)S(1)} collective-permute-done((bf16[256,1024]{1,0:T(8,128)(2,1)S(1)}, bf16[256,1024]{1,0:T(8,128)(2,1)S(1)}, u32[]{:S(2)}, u32[]{:S(2)}) %collective-permute-start.18) | collective-permute-done | bytes 524320 | tf_op jit(solution)/shard_map/inner_out1/ppermute | solution.py:22
  115.3 10.6 %collective-permute-done.21 = bf16[256,1024]{1,0:T(8,128)(2,1)S(1)} collective-permute-done((bf16[256,1024]{1,0:T(8,128)(2,1)S(1)}, bf16[256,1024]{1,0:T(8,128)(2,1)S(1)}, u32[]{:S(2)}, u32[]{:S(2)}) %collective-permute-start.21) | collective-permute-done | bytes 524320 | tf_op jit(solution)/shard_map/outer_in_out0/ppermute | solution.py:22
  126.9 1.5 collective-permute-start.29
  131.0 1.6 %collective-permute-start.35 = (bf16[512,1024]{1,0:T(8,128)(2,1)S(1)}, bf16[512,1024]{1,0:T(8,128)(2,1)S(1)}, u32[]{:S(2)}, u32[]{:S(2)}) collective-permute-start(bf16[512,1024]{1,0:T(8,128)(2,1)S(1)} %collective-permute-done.16.refs_5_), channel_id=1, source_target_pairs={{0,4},{4,0},{8,12},{12,8},{16,20},{20,16},{24,28},{28,24},{1,5},{5... | collective-permute-start | bytes 3145736 | tf_op jit(solution)/shard_map/turn_c31/ppermute | solution.py:22
  132.6 9.2 %fold.1.acc = f32[512,2048]{1,0:T(8,128)S(1)} custom-call(s32[4]{0:T(128)S(1)} %pad_add_fusion.ids, s32[16]{0:T(128)S(1)} %copy-done.5, s32[8]{0:T(128)S(1)} %copy-done.6, f32[512,2048]{1,0:T(8,128)S(1)} %local_products.1.acc, bf16[512,1024]{1,0:T(8,128)(2,1)S(1)} %collective-permute-done.refs_0_, ...), custom_call_target="tpu_custom_call", output_to_operand_aliasing={{}: (3, {})} | custom-call | flops 1 | bytes 1 | tf_op jit(solution)/shard_map/fold/pallas_call | solution.py:280
  141.8 1.2 collective-permute-done.29
  143.9 4.2 %finish.2.refs_6_ = bf16[512,2048]{1,0:T(8,128)(2,1)} custom-call(s32[4]{0:T(128)S(1)} %pad_add_fusion.ids, s32[16]{0:T(128)S(1)} %copy-done.5, s32[8]{0:T(128)S(1)} %copy-done.6, f32[512,2048]{1,0:T(8,128)S(1)} %fold.1.acc, bf16[512,1024]{1,0:T(8,128)(2,1)S(1)} %maximum_select_fusion.refs_0_, bf16[512,1024]{1,0:T(8,128)(2,1)S(1)} %maximum_select_fusion.1.refs_1_, ...), custom_call_target="tpu_custom_call" | custom-call | flops 1 | bytes 1 | tf_op jit(solution)/shard_map/finish/pallas_call | solution.py:280
  148.2 4.2 %finish.3 = bf16[512,2048]{1,0:T(8,128)(2,1)} custom-call(s32[4]{0:T(128)S(1)} %pad_add_fusion.ids, s32[16]{0:T(128)S(1)} %copy-done.5, s32[8]{0:T(128)S(1)} %copy-done.6, f32[512,2048]{1,0:T(8,128)S(1)} %fold.1.acc, bf16[512,1024]{1,0:T(8,128)(2,1)S(1)} %maximum_select_fusion.refs_0_, ...), custom_call_target="tpu_custom_call", output_to_operand_aliasing={{}: (10, {})} | custom-call | flops 1 | bytes 1 | tf_op jit(solution)/shard_map/finish/pallas_call | solution.py:280
  (75 shorter events, 14.9 us)
Async XLA Ops:
  3.3 24.2 %collective-permute-start.2 = (bf16[256,1024]{1,0:T(8,128)(2,1)}, bf16[256,1024]{1,0:T(8,128)(2,1)}, u32[]{:S(2)}, u32[]{:S(2)}) collective-permute-start(bf16[256,1024]{1,0:T(8,128)(2,1)} %get-tuple-element.99), channel_id=1, source_target_pairs={{0,1},{1,0},{2,3},{3,2},{4,5},{5,4},{6,7},{7,6},{8,9},{9,8},{10,11... | collective-permute-start | bytes 1572872 | tf_op jit(solution)/shard_map/piece1/ppermute | solution.py:22
  6.3 25.8 %collective-permute-start.3 = (bf16[256,1024]{1,0:T(8,128)(2,1)}, bf16[256,1024]{1,0:T(8,128)(2,1)}, u32[]{:S(2)}, u32[]{:S(2)}) collective-permute-start(bf16[256,1024]{1,0:T(8,128)(2,1)} %get-tuple-element.98), channel_id=1, source_target_pairs={{0,3},{1,2},{2,1},{3,0},{4,7},{5,6},{6,5},{7,4},{8,11},{9,10},{10,... | collective-permute-start | bytes 1572872 | tf_op jit(solution)/shard_map/piece3/ppermute | solution.py:22
  8.8 23.3 %collective-permute-start.4 = (bf16[2,64,2048]{2,1,0:T(8,128)(2,1)S(1)}, bf16[2,64,2048]{2,1,0:T(8,128)(2,1)S(1)}, u32[]{:S(2)}, u32[]{:S(2)}) collective-permute-start(bf16[2,64,2048]{2,1,0:T(8,128)(2,1)S(1)} %bitcast.7), channel_id=1, source_target_pairs={{0,8},{4,12},{8,0},{12,4},{1,9},{5,13},{9,1},{13,5},{2,10},{6,14},... | collective-permute-start | bytes 1572872 | tf_op jit(solution)/shard_map/down1_0/ppermute | solution.py:22
  10.3 17.2 %collective-permute-start.5 = (bf16[2,64,1024]{2,1,0:T(8,128)(2,1)S(1)}, bf16[2,64,1024]{2,1,0:T(8,128)(2,1)S(1)}, u32[]{:S(2)}, u32[]{:S(2)}) collective-permute-start(bf16[2,64,1024]{2,1,0:T(8,128)(2,1)S(1)} %copy-done.4), channel_id=1, source_target_pairs={{0,8},{4,12},{8,0},{12,4},{1,9},{5,13},{9,1},{13,5},{2,10},{6,14},... | collective-permute-start | bytes 786440 | tf_op jit(solution)/shard_map/up1_0/ppermute | solution.py:22
  32.1 4.2 %collective-permute-start.10 = (bf16[2,64,2048]{2,1,0:T(8,128)(2,1)S(1)}, bf16[2,64,2048]{2,1,0:T(8,128)(2,1)S(1)}, u32[]{:S(2)}, u32[]{:S(2)}) collective-permute-start(bf16[2,64,2048]{2,1,0:T(8,128)(2,1)S(1)} %collective-permute-done.4.refs_2_.refs_6_), channel_id=1, source_target_pairs={{0,4},{4,0},{8,12},{12,8},{1,5},{5,1},{9,13},{13,9},{2,6},{6,2},{1... | collective-permute-start | bytes 1572872 | tf_op jit(solution)/shard_map/down0_1/ppermute | solution.py:22
  32.6 34.3 %collective-permute-start = (bf16[512,1024]{1,0:T(8,128)(2,1)S(1)}, bf16[512,1024]{1,0:T(8,128)(2,1)S(1)}, u32[]{:S(2)}, u32[]{:S(2)}) collective-permute-start(bf16[512,1024]{1,0:T(8,128)(2,1)S(1)} %copy-done.1), channel_id=1, source_target_pairs={{0,1},{1,0},{2,3},{3,2},{4,5},{5,4},{6,7},{7,6},{8,9},{9,8},{10,11... | collective-permute-start | bytes 3145736 | tf_op jit(solution)/shard_map/outer/ppermute | solution.py:22
  33.2 33.7 %collective-permute-start.1 = (bf16[512,1024]{1,0:T(8,128)(2,1)S(1)}, bf16[512,1024]{1,0:T(8,128)(2,1)S(1)}, u32[]{:S(2)}, u32[]{:S(2)}) collective-permute-start(bf16[512,1024]{1,0:T(8,128)(2,1)S(1)} %copy-done.1), channel_id=1, source_target_pairs={{1,2},{2,1},{5,6},{6,5},{9,10},{10,9},{13,14},{14,13},{17,18},{18,... | collective-permute-start | bytes 3145736 | tf_op jit(solution)/shard_map/inner/ppermute | solution.py:22
  34.7 9.4 %collective-permute-start.7 = (bf16[256,1024]{1,0:T(8,128)(2,1)}, bf16[256,1024]{1,0:T(8,128)(2,1)S(1)}, u32[]{:S(2)}, u32[]{:S(2)}) collective-permute-start(bf16[256,1024]{1,0:T(8,128)(2,1)} %collective-permute-done.3), channel_id=1, source_target_pairs={{0,16},{4,12},{8,24},{12,4},{16,0},{20,28},{24,8},{28,20},{1,17},{... | collective-permute-start | bytes 1572872 | tf_op jit(solution)/shard_map/turn_a3/ppermute | solution.py:22
  36.2 13.5 %collective-permute-start.6 = (bf16[256,1024]{1,0:T(8,128)(2,1)}, bf16[256,1024]{1,0:T(8,128)(2,1)S(1)}, u32[]{:S(2)}, u32[]{:S(2)}) collective-permute-start(bf16[256,1024]{1,0:T(8,128)(2,1)} %collective-permute-done.2), channel_id=1, source_target_pairs={{0,16},{4,12},{8,24},{12,4},{16,0},{20,28},{24,8},{28,20},{1,17},{... | collective-permute-start | bytes 1572872 | tf_op jit(solution)/shard_map/turn_a1/ppermute | solution.py:22
  40.1 26.8 %collective-permute-start.12 = (bf16[512,128]{1,0:T(8,128)(2,1)S(1)}, bf16[512,128]{1,0:T(8,128)(2,1)S(1)}, u32[]{:S(2)}, u32[]{:S(2)}) collective-permute-start(bf16[512,128]{1,0:T(8,128)(2,1)S(1)} %rank_partials.1), channel_id=1, source_target_pairs={{0,2},{1,3},{2,0},{3,1},{4,6},{5,7},{6,4},{7,5},{8,10},{9,11},{10,... | collective-permute-start | bytes 393224 | tf_op jit(solution)/shard_map/rank_sum1/ppermute | solution.py:22
  66.9 29.4 %collective-permute-start.15 = (bf16[512,1024]{1,0:T(8,128)(2,1)S(1)}, bf16[512,1024]{1,0:T(8,128)(2,1)S(1)}, u32[]{:S(2)}, u32[]{:S(2)}) collective-permute-start(bf16[512,1024]{1,0:T(8,128)(2,1)S(1)} %pad_maximum_fusion.refs_1_), channel_id=1, source_target_pairs={{0,8},{4,20},{8,0},{12,28},{16,24},{20,4},{24,16},{28,12},{1,9},{5... | collective-permute-start | bytes 3145736 | tf_op jit(solution)/shard_map/turn_b1/ppermute | solution.py:22
  68.5 27.8 %collective-permute-start.16 = (bf16[512,1024]{1,0:T(8,128)(2,1)S(1)}, bf16[512,1024]{1,0:T(8,128)(2,1)S(1)}, u32[]{:S(2)}, u32[]{:S(2)}) collective-permute-start(bf16[512,1024]{1,0:T(8,128)(2,1)S(1)} %pad_maximum_fusion.1.refs_4_), channel_id=1, source_target_pairs={{0,8},{4,20},{8,0},{12,28},{16,24},{20,4},{24,16},{28,12},{1,9},{5... | collective-permute-start | bytes 3145736 | tf_op jit(solution)/shard_map/turn_b3/ppermute | solution.py:22
  69.0 8.2 %collective-permute-start.17 = (bf16[512,128]{1,0:T(8,128)(2,1)S(1)}, bf16[512,128]{1,0:T(8,128)(2,1)S(1)}, u32[]{:S(2)}, u32[]{:S(2)}) collective-permute-start(bf16[512,128]{1,0:T(8,128)(2,1)S(1)} %add_convert_fusion.2), channel_id=1, source_target_pairs={{0,1},{1,0},{2,3},{3,2},{4,5},{5,4},{6,7},{7,6},{8,9},{9,8},{10,11... | collective-permute-start | bytes 393224 | tf_op jit(solution)/shard_map/rank_sum0/ppermute | solution.py:22
  69.1 27.2 %collective-permute-start.13 = (bf16[256,1024]{1,0:T(8,128)(2,1)S(1)}, bf16[256,1024]{1,0:T(8,128)(2,1)S(1)}, u32[]{:S(2)}, u32[]{:S(2)}) collective-permute-start(bf16[256,1024]{1,0:T(8,128)(2,1)S(1)} %get-tuple-element.100), channel_id=1, source_target_pairs={{1,0},{2,3},{5,4},{6,7},{9,8},{10,11},{13,12},{14,15},{17,16},{18,... | collective-permute-start | bytes 1572872 | tf_op jit(solution)/shard_map/inner_out0/ppermute | solution.py:22
  70.4 25.9 %collective-permute-start.14 = (bf16[256,1024]{1,0:T(8,128)(2,1)S(1)}, bf16[256,1024]{1,0:T(8,128)(2,1)S(1)}, u32[]{:S(2)}, u32[]{:S(2)}) collective-permute-start(bf16[256,1024]{1,0:T(8,128)(2,1)S(1)} %get-tuple-element.59), channel_id=1, source_target_pairs={{0,2},{1,3},{2,0},{3,1},{4,6},{5,7},{6,4},{7,5},{8,10},{9,11},{10,... | collective-permute-start | bytes 1572872 | tf_op jit(solution)/shard_map/piece2/ppermute | solution.py:22
  96.3 4.1 %collective-permute-start.23 = (bf16[1,64,3072]{2,1,0:T(8,128)(2,1)S(1)}, bf16[1,64,3072]{2,1,0:T(8,128)(2,1)S(1)}, u32[]{:S(2)}, u32[]{:S(2)}) collective-permute-start(bf16[1,64,3072]{2,1,0:T(8,128)(2,1)S(1)} %get-tuple-element.74), channel_id=1, source_target_pairs={{0,4},{4,0},{8,12},{12,8},{1,5},{5,1},{9,13},{13,9},{2,6},{6,2},{1... | collective-permute-start | bytes 1179656 | tf_op jit(solution)/shard_map/grads0_2/ppermute | solution.py:22
  96.9 9.2 %collective-permute-start.22 = (bf16[256,1024]{1,0:T(8,128)(2,1)S(1)}, bf16[256,1024]{1,0:T(8,128)(2,1)S(1)}, u32[]{:S(2)}, u32[]{:S(2)}) collective-permute-start(bf16[256,1024]{1,0:T(8,128)(2,1)S(1)} %collective-permute-done.14), channel_id=1, source_target_pairs={{0,16},{4,12},{8,24},{12,4},{16,0},{20,28},{24,8},{28,20},{1,17},{... | collective-permute-start | bytes 1572872 | tf_op jit(solution)/shard_map/turn_a2/ppermute | solution.py:22
  98.4 4.5 %collective-permute-start.19 = (bf16[256,1024]{1,0:T(8,128)(2,1)S(1)}, bf16[256,1024]{1,0:T(8,128)(2,1)S(1)}, u32[]{:S(2)}, u32[]{:S(2)}) collective-permute-start(bf16[256,1024]{1,0:T(8,128)(2,1)S(1)} %get-tuple-element.68), channel_id=1, source_target_pairs={{1,2},{2,1},{5,6},{6,5},{9,10},{10,9},{13,14},{14,13},{17,18},{18,... | collective-permute-start | bytes 1572872 | tf_op jit(solution)/shard_map/outer_in0/ppermute | solution.py:22
  99.1 15.6 %collective-permute-start.18 = (bf16[256,1024]{1,0:T(8,128)(2,1)S(1)}, bf16[256,1024]{1,0:T(8,128)(2,1)S(1)}, u32[]{:S(2)}, u32[]{:S(2)}) collective-permute-start(bf16[256,1024]{1,0:T(8,128)(2,1)S(1)} %get-tuple-element.67), channel_id=1, source_target_pairs={{1,0},{2,3},{5,4},{6,7},{9,8},{10,11},{13,12},{14,15},{17,16},{18,... | collective-permute-start | bytes 1572872 | tf_op jit(solution)/shard_map/inner_out1/ppermute | solution.py:22
  100.6 25.3 %collective-permute-start.25 = (bf16[2,64,3072]{2,1,0:T(8,128)(2,1)S(1)}, bf16[2,64,3072]{2,1,0:T(8,128)(2,1)S(1)}, u32[]{:S(2)}, u32[]{:S(2)}) collective-permute-start(bf16[2,64,3072]{2,1,0:T(8,128)(2,1)S(1)} %add_convert_fusion), channel_id=1, source_target_pairs={{0,8},{4,12},{8,0},{12,4},{1,9},{5,13},{9,1},{13,5},{2,10},{6,14},... | collective-permute-start | bytes 2359304 | tf_op jit(solution)/shard_map/grads1/ppermute | solution.py:22
  102.2 12.5 %collective-permute-start.20 = (bf16[256,1024]{1,0:T(8,128)(2,1)S(1)}, bf16[256,1024]{1,0:T(8,128)(2,1)S(1)}, u32[]{:S(2)}, u32[]{:S(2)}) collective-permute-start(bf16[256,1024]{1,0:T(8,128)(2,1)S(1)} %get-tuple-element.69), channel_id=1, source_target_pairs={{1,2},{2,1},{5,6},{6,5},{9,10},{10,9},{13,14},{14,13},{17,18},{18,... | collective-permute-start | bytes 1572872 | tf_op jit(solution)/shard_map/outer_in1/ppermute | solution.py:22
  102.9 23.0 %collective-permute-start.21 = (bf16[256,1024]{1,0:T(8,128)(2,1)S(1)}, bf16[256,1024]{1,0:T(8,128)(2,1)S(1)}, u32[]{:S(2)}, u32[]{:S(2)}) collective-permute-start(bf16[256,1024]{1,0:T(8,128)(2,1)S(1)} %collective-permute-done.19), channel_id=1, source_target_pairs={{1,0},{2,3},{5,4},{6,7},{9,8},{10,11},{13,12},{14,15},{17,16},{18,... | collective-permute-start | bytes 1572872 | tf_op jit(solution)/shard_map/outer_in_out0/ppermute | solution.py:22
  106.1 20.3 %collective-permute-start.30 = (bf16[1,64,3072]{2,1,0:T(8,128)(2,1)S(1)}, bf16[1,64,3072]{2,1,0:T(8,128)(2,1)S(1)}, u32[]{:S(2)}, u32[]{:S(2)}) collective-permute-start(bf16[1,64,3072]{2,1,0:T(8,128)(2,1)S(1)} %get-tuple-element.84), channel_id=1, source_target_pairs={{0,4},{4,0},{8,12},{12,8},{1,5},{5,1},{9,13},{13,9},{2,6},{6,2},{1... | collective-permute-start | bytes 1179656 | tf_op jit(solution)/shard_map/grads0_0/ppermute | solution.py:22
  114.6 12.2 %collective-permute-start.31 = (bf16[1,64,3072]{2,1,0:T(8,128)(2,1)S(1)}, bf16[1,64,3072]{2,1,0:T(8,128)(2,1)S(1)}, u32[]{:S(2)}, u32[]{:S(2)}) collective-permute-start(bf16[1,64,3072]{2,1,0:T(8,128)(2,1)S(1)} %get-tuple-element.85), channel_id=1, source_target_pairs={{0,4},{4,0},{8,12},{12,8},{1,5},{5,1},{9,13},{13,9},{2,6},{6,2},{1... | collective-permute-start | bytes 1179656 | tf_op jit(solution)/shard_map/grads0_1/ppermute | solution.py:22
  114.7 33.4 %collective-permute-start.34 = (bf16[512,1024]{1,0:T(8,128)(2,1)S(1)}, bf16[512,1024]{1,0:T(8,128)(2,1)S(1)}, u32[]{:S(2)}, u32[]{:S(2)}) collective-permute-start(bf16[512,1024]{1,0:T(8,128)(2,1)S(1)} %pad_maximum_fusion.1.refs_4_), channel_id=1, source_target_pairs={{0,4},{4,0},{8,12},{12,8},{16,20},{20,16},{24,28},{28,24},{1,5},{5... | collective-permute-start | bytes 3145736 | tf_op jit(solution)/shard_map/turn_c30/ppermute | solution.py:22
  125.8 5.2 %collective-permute-start.27 = (bf16[512,1024]{1,0:T(8,128)(2,1)S(1)}, bf16[512,1024]{1,0:T(8,128)(2,1)S(1)}, u32[]{:S(2)}, u32[]{:S(2)}) collective-permute-start(bf16[512,1024]{1,0:T(8,128)(2,1)S(1)} %pad_maximum_fusion.refs_1_), channel_id=1, source_target_pairs={{0,4},{4,0},{8,12},{12,8},{16,20},{20,16},{24,28},{28,24},{1,5},{5... | collective-permute-start | bytes 3145736 | tf_op jit(solution)/shard_map/turn_c10/ppermute | solution.py:22
  125.8 6.7 %collective-permute-start.28 = (bf16[512,1024]{1,0:T(8,128)(2,1)S(1)}, bf16[512,1024]{1,0:T(8,128)(2,1)S(1)}, u32[]{:S(2)}, u32[]{:S(2)}) collective-permute-start(bf16[512,1024]{1,0:T(8,128)(2,1)S(1)} %collective-permute-done.15.refs_2_), channel_id=1, source_target_pairs={{0,4},{4,0},{8,12},{12,8},{16,20},{20,16},{24,28},{28,24},{1,5},{5... | collective-permute-start | bytes 3145736 | tf_op jit(solution)/shard_map/turn_c11/ppermute | solution.py:22
  126.4 16.6 %collective-permute-start.26 = (bf16[512,1024]{1,0:T(8,128)(2,1)S(1)}, bf16[512,1024]{1,0:T(8,128)(2,1)S(1)}, u32[]{:S(2)}, u32[]{:S(2)}) collective-permute-start(bf16[512,1024]{1,0:T(8,128)(2,1)S(1)} %pad_maximum_fusion.2.refs_2_), channel_id=1, source_target_pairs={{0,8},{4,20},{8,0},{12,28},{16,24},{20,4},{24,16},{28,12},{1,9},{5... | collective-permute-start | bytes 3145736 | tf_op jit(solution)/shard_map/turn_b2/ppermute | solution.py:22
  126.9 16.1 %collective-permute-start.29 = (bf16[256,1024]{1,0:T(8,128)(2,1)S(1)}, bf16[256,1024]{1,0:T(8,128)(2,1)S(1)}, u32[]{:S(2)}, u32[]{:S(2)}) collective-permute-start(bf16[256,1024]{1,0:T(8,128)(2,1)S(1)} %collective-permute-done.20), channel_id=1, source_target_pairs={{1,0},{2,3},{5,4},{6,7},{9,8},{10,11},{13,12},{14,15},{17,16},{18,... | collective-permute-start | bytes 1572872 | tf_op jit(solution)/shard_map/outer_in_out1/ppermute | solution.py:22
  131.0 17.2 %collective-permute-start.35 = (bf16[512,1024]{1,0:T(8,128)(2,1)S(1)}, bf16[512,1024]{1,0:T(8,128)(2,1)S(1)}, u32[]{:S(2)}, u32[]{:S(2)}) collective-permute-start(bf16[512,1024]{1,0:T(8,128)(2,1)S(1)} %collective-permute-done.16.refs_5_), channel_id=1, source_target_pairs={{0,4},{4,0},{8,12},{12,8},{16,20},{20,16},{24,28},{28,24},{1,5},{5... | collective-permute-start | bytes 3145736 | tf_op jit(solution)/shard_map/turn_c31/ppermute | solution.py:22
  143.0 5.2 %collective-permute-start.32 = (bf16[512,1024]{1,0:T(8,128)(2,1)S(1)}, bf16[512,1024]{1,0:T(8,128)(2,1)S(1)}, u32[]{:S(2)}, u32[]{:S(2)}) collective-permute-start(bf16[512,1024]{1,0:T(8,128)(2,1)S(1)} %pad_maximum_fusion.2.refs_2_), channel_id=1, source_target_pairs={{0,4},{4,0},{8,12},{12,8},{16,20},{20,16},{24,28},{28,24},{1,5},{5... | collective-permute-start | bytes 3145736 | tf_op jit(solution)/shard_map/turn_c20/ppermute | solution.py:22
  143.4 4.8 %collective-permute-start.33 = (bf16[512,1024]{1,0:T(8,128)(2,1)S(1)}, bf16[512,1024]{1,0:T(8,128)(2,1)S(1)}, u32[]{:S(2)}, u32[]{:S(2)}) collective-permute-start(bf16[512,1024]{1,0:T(8,128)(2,1)S(1)} %collective-permute-done.26.refs_3_), channel_id=1, source_target_pairs={{0,4},{4,0},{8,12},{12,8},{16,20},{20,16},{24,28},{28,24},{1,5},{5... | collective-permute-start | bytes 3145736 | tf_op jit(solution)/shard_map/turn_c21/ppermute | solution.py:22
  (11 other events, 105.0 us)

commit v6 on v5

--- a/solution.py
+++ b/solution.py
@@ -388,12 +388,14 @@
 
         by_one = move("outer", query_gradient, "tensor", outer)
         across = move("inner", query_gradient, "tensor", inner)
-        wide1 = turned("turn_a1", piece1, turn_a)
-        wide3 = turned("turn_a3", piece3, turn_a)
+        near1 = move("turn_a1", piece1, copies, turn_a)
+        near3 = move("turn_a3", piece3, copies, turn_a)
         table = more(bits[1], table)
         both = ranks(table)
         both = rank_sum(1, both)
-        by_one, across, wide1, wide3, both, cut2 = together(by_one, across, wide1, wide3, both, cut2)
+        by_one, across, near1, near3, both, cut2 = together(by_one, across, near1, near3, both, cut2)
+        wide1 = jnp.concatenate([piece1, near1], axis=0)
+        wide3 = jnp.concatenate([piece3, near3], axis=0)
 
         half = tokens // 2
         one0, one1, over0, over1 = by_one[:half], by_one[half:], across[:half], across[half:]

time: 153 us -> 152 us (level)
  other arithmetic: 3.83 us -> 1.61 us
  local copies, waits for them, and re-layouts: 10.4 us -> 12.6 us
  waiting for transfers between devices: 75.1 us -> 73 us
    concatenate x3 -> x1, other arithmetic: 2.29 us -> 0.07 us  [turned(): return jnp.concatenate([own, move(name, own, copies, pairs)], axis=0)]
    ppermute x36, waiting for transfers between devices: 75.1 us -> 73 us  [move(): return lax.ppermute(a, axis, pairs)]
    unnamed x14 -> x16, local copies, waits for them, and re-layouts: 5.79 us -> 7.95 us
  transfers between devices with their start and end apart: 36 -> 36, of which waited for: 13 -> 10; matrix products, arithmetic and copies ran while one was open for 4% -> 4% of each run, Pallas kernels for 16% -> 16%
where the time goes in v6:
time: 152 us; the launch traced here: 151 us
  waiting for transfers between devices  73 us (48%)
  starting transfers between devices  35.2 us (23%)
  Pallas kernels  28.1 us (18%)
  local copies, waits for them, and re-layouts  12.6 us (8%)
  other arithmetic  1.61 us (1%)
    ppermute x36, waiting for transfers between devices, move(): return lax.ppermute(a, axis, pairs)  73 us
    ppermute x36, starting transfers between devices, move(): return lax.ppermute(a, axis, pairs)  35.2 us
    pallas_call x3, Pallas kernels, fold(): pl.pallas_call(functools.partial(fold_kernel, terms=len(xs), parts=parts,...  17.6 us
    unnamed x16, local copies, waits for them, and re-layouts  7.95 us
    pallas_call x1, Pallas kernels, local_products(): pl.pallas_call(local_kernel, grid_spec=pltpu.PrefetchScalarGridSpec(num_s...  3.8 us
    pallas_call x1, Pallas kernels, member_grads(): pl.pallas_call(functools.partial(grads_kernel, width=width, blocks=blocks...  3.44 us
    pallas_call x1, Pallas kernels, rank_partials(): pl.pallas_call(functools.partial(rank_kernel, blocks=blocks, slot=slot, h...  3.23 us
  transfers between devices with their start and end apart: 36, of which 10 were waited for; matrix products, arithmetic and copies ran while one was open for 4% of the time, Pallas kernels for 16%

profile of v6, /device:TPU:0, one launch (start us, length us, event | category | flops | bytes accessed | tf_op | source)
XLA Modules:
  0.0 151.5 jit_solution(12494035504606794685)
XLA Ops:
  0.7 2.6 %constant_dynamic-slice_fusion = (bf16[256,1024]{1,0:T(8,128)(2,1)S(1)}, bf16[256,1024]{1,0:T(8,128)(2,1)}, bf16[256,1024]{1,0:T(8,128)(2,1)}) fusion(bf16[8192,1024]{1,0:T(8,128)(2,1)} %weight.1, s32[]{:T(128)S(6)} %select_n.40, s32[]{:T(128)S(6)} %select_n.39, s32[]{:T(128)S(6)} %select_n.38), kind=kLoop, calls=%fused_computation.12 | loop fusion | bytes 3145740 | tf_op jit(solution)/shard_map/dynamic_slice | solution.py:343
  3.3 3.0 %collective-permute-start.2 = (bf16[256,1024]{1,0:T(8,128)(2,1)}, bf16[256,1024]{1,0:T(8,128)(2,1)}, u32[]{:S(2)}, u32[]{:S(2)}) collective-permute-start(bf16[256,1024]{1,0:T(8,128)(2,1)} %get-tuple-element.99), channel_id=1, source_target_pairs={{0,1},{1,0},{2,3},{3,2},{4,5},{5,4},{6,7},{7,6},{8,9},{9,8},{10,11... | collective-permute-start | bytes 1572872 | tf_op jit(solution)/shard_map/piece1/ppermute | solution.py:22
  6.3 2.5 %collective-permute-start.3 = (bf16[256,1024]{1,0:T(8,128)(2,1)}, bf16[256,1024]{1,0:T(8,128)(2,1)}, u32[]{:S(2)}, u32[]{:S(2)}) collective-permute-start(bf16[256,1024]{1,0:T(8,128)(2,1)} %get-tuple-element.98), channel_id=1, source_target_pairs={{0,3},{1,2},{2,1},{3,0},{4,7},{5,6},{6,5},{7,4},{8,11},{9,10},{10,... | collective-permute-start | bytes 1572872 | tf_op jit(solution)/shard_map/piece3/ppermute | solution.py:22
  8.8 1.5 %collective-permute-start.4 = (bf16[2,64,2048]{2,1,0:T(8,128)(2,1)S(1)}, bf16[2,64,2048]{2,1,0:T(8,128)(2,1)S(1)}, u32[]{:S(2)}, u32[]{:S(2)}) collective-permute-start(bf16[2,64,2048]{2,1,0:T(8,128)(2,1)S(1)} %bitcast.7), channel_id=1, source_target_pairs={{0,8},{4,12},{8,0},{12,4},{1,9},{5,13},{9,1},{13,5},{2,10},{6,14},... | collective-permute-start | bytes 1572872 | tf_op jit(solution)/shard_map/down1_0/ppermute | solution.py:22
  10.9 5.8 %copy-done = bf16[8192,1024]{1,0:T(8,128)(2,1)S(1)} copy-done((bf16[8192,1024]{1,0:T(8,128)(2,1)S(1)}, bf16[8192,1024]{1,0:T(8,128)(2,1)}, u32[]{:S(2)}) %copy-start) | copy-done | bytes 16777240
  16.7 3.8 %local_products.1.acc = f32[512,2048]{1,0:T(8,128)S(1)} custom-call(s32[4]{0:T(128)S(1)} %pad_add_fusion.ids, bf16[512,1024]{1,0:T(8,128)(2,1)S(1)} %copy-done.1, bf16[8192,1024]{1,0:T(8,128)(2,1)S(1)} %copy-done), custom_call_target="tpu_custom_call" | custom-call | flops 1 | bytes 1 | tf_op jit(solution)/shard_map/local_products/pallas_call | solution.py:195
  20.5 7.0 %collective-permute-done.5.refs_3_ = bf16[2,64,1024]{2,1,0:T(8,128)(2,1)S(1)} collective-permute-done((bf16[2,64,1024]{2,1,0:T(8,128)(2,1)S(1)}, bf16[2,64,1024]{2,1,0:T(8,128)(2,1)S(1)}, u32[]{:S(2)}, u32[]{:S(2)}) %collective-permute-start.5) | collective-permute-done | bytes 262176 | tf_op jit(solution)/shard_map/up1_0/ppermute | solution.py:22
  27.5 4.6 %collective-permute-done.3 = bf16[256,1024]{1,0:T(8,128)(2,1)} collective-permute-done((bf16[256,1024]{1,0:T(8,128)(2,1)}, bf16[256,1024]{1,0:T(8,128)(2,1)}, u32[]{:S(2)}, u32[]{:S(2)}) %collective-permute-start.3) | collective-permute-done | bytes 524320 | tf_op jit(solution)/shard_map/piece3/ppermute | solution.py:22
  34.5 1.8 %collective-permute-done.9.refs_5_ = bf16[2,64,1024]{2,1,0:T(8,128)(2,1)S(1)} collective-permute-done((bf16[2,64,1024]{2,1,0:T(8,128)(2,1)S(1)}, bf16[2,64,1024]{2,1,0:T(8,128)(2,1)S(1)}, u32[]{:S(2)}, u32[]{:S(2)}) %collective-permute-start.9) | collective-permute-done | bytes 262176 | tf_op jit(solution)/shard_map/up0_0/ppermute | solution.py:22
  36.2 1.5 collective-permute-start.6
  38.3 3.2 %rank_partials.1 = bf16[512,128]{1,0:T(8,128)(2,1)S(1)} custom-call(s32[4]{0:T(128)S(1)} %pad_add_fusion.ids, s32[16]{0:T(128)S(1)} %copy-done.5, s32[8]{0:T(128)S(1)} %copy-done.6, bf16[512,2048]{1,0:T(8,128)(2,1)S(1)} %copy-done.2, bf16[512,1024]{1,0:T(8,128)(2,1)S(1)} %copy-done.1, bf16[2,64,2048]{2,1,0:T(8,128)(2,1)S(1)} %bitcast.9, ...), custom_call_target="tpu_custom_call" | custom-call | flops 1 | bytes 1 | tf_op jit(solution)/shard_map/rank_partials/pallas_call | solution.py:89
  41.5 4.2 %collective-permute-start.12 = (bf16[512,128]{1,0:T(8,128)(2,1)S(1)}, bf16[512,128]{1,0:T(8,128)(2,1)S(1)}, u32[]{:S(2)}, u32[]{:S(2)}) collective-permute-start(bf16[512,128]{1,0:T(8,128)(2,1)S(1)} %rank_partials.1), channel_id=1, source_target_pairs={{0,2},{1,3},{2,0},{3,1},{4,6},{5,7},{6,4},{7,5},{8,10},{9,11},{10,... | collective-permute-start | bytes 393224 | tf_op jit(solution)/shard_map/rank_sum1/ppermute | solution.py:22
  47.9 18.5 %collective-permute-done.12 = bf16[512,128]{1,0:T(8,128)(2,1)S(1)} collective-permute-done((bf16[512,128]{1,0:T(8,128)(2,1)S(1)}, bf16[512,128]{1,0:T(8,128)(2,1)S(1)}, u32[]{:S(2)}, u32[]{:S(2)}) %collective-permute-start.12) | collective-permute-done | bytes 131104 | tf_op jit(solution)/shard_map/rank_sum1/ppermute | solution.py:22
  66.5 1.6 %collective-permute-start.16 = (bf16[512,1024]{1,0:T(8,128)(2,1)S(1)}, bf16[512,1024]{1,0:T(8,128)(2,1)S(1)}, u32[]{:S(2)}, u32[]{:S(2)}) collective-permute-start(bf16[512,1024]{1,0:T(8,128)(2,1)S(1)} %constant_dynamic-update-slice_fusion.2.refs_4_), channel_id=1, source_target_pairs={{0,8},{4,20},{8,0},{12,28},{16,24},{20,4},{24,16},{28,12},{1,9},{5... | collective-permute-start | bytes 3145736 | tf_op jit(solution)/shard_map/turn_b3/ppermute | solution.py:22
  68.7 1.3 collective-permute-start.13
  70.0 2.8 %collective-permute-start.14 = (bf16[256,1024]{1,0:T(8,128)(2,1)S(1)}, bf16[256,1024]{1,0:T(8,128)(2,1)S(1)}, u32[]{:S(2)}, u32[]{:S(2)}) collective-permute-start(bf16[256,1024]{1,0:T(8,128)(2,1)S(1)} %get-tuple-element.59), channel_id=1, source_target_pairs={{0,2},{1,3},{2,0},{3,1},{4,6},{5,7},{6,4},{7,5},{8,10},{9,11},{10,... | collective-permute-start | bytes 1572872 | tf_op jit(solution)/shard_map/piece2/ppermute | solution.py:22
  72.9 3.8 %collective-permute-done.17 = bf16[512,128]{1,0:T(8,128)(2,1)S(1)} collective-permute-done((bf16[512,128]{1,0:T(8,128)(2,1)S(1)}, bf16[512,128]{1,0:T(8,128)(2,1)S(1)}, u32[]{:S(2)}, u32[]{:S(2)}) %collective-permute-start.17) | collective-permute-done | bytes 131104 | tf_op jit(solution)/shard_map/rank_sum0/ppermute | solution.py:22
  76.7 3.4 %member_grads.1 = (bf16[1,64,3072]{2,1,0:T(8,128)(2,1)S(1)}, bf16[1,64,3072]{2,1,0:T(8,128)(2,1)S(1)}, bf16[1,64,3072]{2,1,0:T(8,128)(2,1)S(1)}, bf16[1,64,3072]...) custom-call(s32[4]{0:T(128)S(1)} %pad_add_fusion.ids, s32[16]{0:T(128)S(1)} %copy-done.5, bf16[512,2048]{1,0:T(8,128)(2,1)S(1)} %copy-done.2, ...), custom_call_target="tpu_custom_call" | custom-call | flops 1 | bytes 1 | tf_op jit(solution)/shard_map/member_grads/pallas_call | solution.py:141
  80.2 15.2 %collective-permute-done.13 = bf16[256,1024]{1,0:T(8,128)(2,1)S(1)} collective-permute-done((bf16[256,1024]{1,0:T(8,128)(2,1)S(1)}, bf16[256,1024]{1,0:T(8,128)(2,1)S(1)}, u32[]{:S(2)}, u32[]{:S(2)}) %collective-permute-start.13) | collective-permute-done | bytes 524320 | tf_op jit(solution)/shard_map/inner_out0/ppermute | solution.py:22
  96.0 1.5 collective-permute-start.22
  98.1 1.3 collective-permute-start.18
  99.7 1.6 %collective-permute-start.25 = (bf16[2,64,3072]{2,1,0:T(8,128)(2,1)S(1)}, bf16[2,64,3072]{2,1,0:T(8,128)(2,1)S(1)}, u32[]{:S(2)}, u32[]{:S(2)}) collective-permute-start(bf16[2,64,3072]{2,1,0:T(8,128)(2,1)S(1)} %add_convert_fusion), channel_id=1, source_target_pairs={{0,8},{4,12},{8,0},{12,4},{1,9},{5,13},{9,1},{13,5},{2,10},{6,14},... | collective-permute-start | bytes 2359304 | tf_op jit(solution)/shard_map/grads1/ppermute | solution.py:22
  101.9 1.3 collective-permute-start.21
  103.2 1.9 %collective-permute-done.22 = bf16[256,1024]{1,0:T(8,128)(2,1)S(1)} collective-permute-done((bf16[256,1024]{1,0:T(8,128)(2,1)S(1)}, bf16[256,1024]{1,0:T(8,128)(2,1)S(1)}, u32[]{:S(2)}, u32[]{:S(2)}) %collective-permute-start.22) | collective-permute-done | bytes 524320 | tf_op jit(solution)/shard_map/turn_a2/ppermute | solution.py:22
  105.3 8.5 %collective-permute-done.18 = bf16[256,1024]{1,0:T(8,128)(2,1)S(1)} collective-permute-done((bf16[256,1024]{1,0:T(8,128)(2,1)S(1)}, bf16[256,1024]{1,0:T(8,128)(2,1)S(1)}, u32[]{:S(2)}, u32[]{:S(2)}) %collective-permute-start.18) | collective-permute-done | bytes 524320 | tf_op jit(solution)/shard_map/inner_out1/ppermute | solution.py:22
  114.4 10.6 %collective-permute-done.21 = bf16[256,1024]{1,0:T(8,128)(2,1)S(1)} collective-permute-done((bf16[256,1024]{1,0:T(8,128)(2,1)S(1)}, bf16[256,1024]{1,0:T(8,128)(2,1)S(1)}, u32[]{:S(2)}, u32[]{:S(2)}) %collective-permute-start.21) | collective-permute-done | bytes 524320 | tf_op jit(solution)/shard_map/outer_in_out0/ppermute | solution.py:22
  126.0 1.5 collective-permute-start.29
  130.1 1.6 %collective-permute-start.35 = (bf16[512,1024]{1,0:T(8,128)(2,1)S(1)}, bf16[512,1024]{1,0:T(8,128)(2,1)S(1)}, u32[]{:S(2)}, u32[]{:S(2)}) collective-permute-start(bf16[512,1024]{1,0:T(8,128)(2,1)S(1)} %collective-permute-done.16.refs_5_), channel_id=1, source_target_pairs={{0,4},{4,0},{8,12},{12,8},{16,20},{20,16},{24,28},{28,24},{1,5},{5... | collective-permute-start | bytes 3145736 | tf_op jit(solution)/shard_map/turn_c31/ppermute | solution.py:22
  131.7 9.2 %fold.1.acc = f32[512,2048]{1,0:T(8,128)S(1)} custom-call(s32[4]{0:T(128)S(1)} %pad_add_fusion.ids, s32[16]{0:T(128)S(1)} %copy-done.5, s32[8]{0:T(128)S(1)} %copy-done.6, f32[512,2048]{1,0:T(8,128)S(1)} %local_products.1.acc, bf16[512,1024]{1,0:T(8,128)(2,1)S(1)} %collective-permute-done.refs_0_, ...), custom_call_target="tpu_custom_call", output_to_operand_aliasing={{}: (3, {})} | custom-call | flops 1 | bytes 1 | tf_op jit(solution)/shard_map/fold/pallas_call | solution.py:280
  140.9 1.2 collective-permute-done.29
  143.0 4.2 %finish.2.refs_6_ = bf16[512,2048]{1,0:T(8,128)(2,1)} custom-call(s32[4]{0:T(128)S(1)} %pad_add_fusion.ids, s32[16]{0:T(128)S(1)} %copy-done.5, s32[8]{0:T(128)S(1)} %copy-done.6, f32[512,2048]{1,0:T(8,128)S(1)} %fold.1.acc, bf16[512,1024]{1,0:T(8,128)(2,1)S(1)} %maximum_select_fusion.refs_0_, bf16[512,1024]{1,0:T(8,128)(2,1)S(1)} %maximum_select_fusion.1.refs_1_, ...), custom_call_target="tpu_custom_call" | custom-call | flops 1 | bytes 1 | tf_op jit(solution)/shard_map/finish/pallas_call | solution.py:280
  147.3 4.2 %finish.3 = bf16[512,2048]{1,0:T(8,128)(2,1)} custom-call(s32[4]{0:T(128)S(1)} %pad_add_fusion.ids, s32[16]{0:T(128)S(1)} %copy-done.5, s32[8]{0:T(128)S(1)} %copy-done.6, f32[512,2048]{1,0:T(8,128)S(1)} %fold.1.acc, bf16[512,1024]{1,0:T(8,128)(2,1)S(1)} %maximum_select_fusion.refs_0_, ...), custom_call_target="tpu_custom_call", output_to_operand_aliasing={{}: (10, {})} | custom-call | flops 1 | bytes 1 | tf_op jit(solution)/shard_map/finish/pallas_call | solution.py:280
  (77 shorter events, 14.1 us)
Async XLA Ops:
  3.3 24.2 %collective-permute-start.2 = (bf16[256,1024]{1,0:T(8,128)(2,1)}, bf16[256,1024]{1,0:T(8,128)(2,1)}, u32[]{:S(2)}, u32[]{:S(2)}) collective-permute-start(bf16[256,1024]{1,0:T(8,128)(2,1)} %get-tuple-element.99), channel_id=1, source_target_pairs={{0,1},{1,0},{2,3},{3,2},{4,5},{5,4},{6,7},{7,6},{8,9},{9,8},{10,11... | collective-permute-start | bytes 1572872 | tf_op jit(solution)/shard_map/piece1/ppermute | solution.py:22
  6.3 25.8 %collective-permute-start.3 = (bf16[256,1024]{1,0:T(8,128)(2,1)}, bf16[256,1024]{1,0:T(8,128)(2,1)}, u32[]{:S(2)}, u32[]{:S(2)}) collective-permute-start(bf16[256,1024]{1,0:T(8,128)(2,1)} %get-tuple-element.98), channel_id=1, source_target_pairs={{0,3},{1,2},{2,1},{3,0},{4,7},{5,6},{6,5},{7,4},{8,11},{9,10},{10,... | collective-permute-start | bytes 1572872 | tf_op jit(solution)/shard_map/piece3/ppermute | solution.py:22
  8.8 23.3 %collective-permute-start.4 = (bf16[2,64,2048]{2,1,0:T(8,128)(2,1)S(1)}, bf16[2,64,2048]{2,1,0:T(8,128)(2,1)S(1)}, u32[]{:S(2)}, u32[]{:S(2)}) collective-permute-start(bf16[2,64,2048]{2,1,0:T(8,128)(2,1)S(1)} %bitcast.7), channel_id=1, source_target_pairs={{0,8},{4,12},{8,0},{12,4},{1,9},{5,13},{9,1},{13,5},{2,10},{6,14},... | collective-permute-start | bytes 1572872 | tf_op jit(solution)/shard_map/down1_0/ppermute | solution.py:22
  10.3 17.2 %collective-permute-start.5 = (bf16[2,64,1024]{2,1,0:T(8,128)(2,1)S(1)}, bf16[2,64,1024]{2,1,0:T(8,128)(2,1)S(1)}, u32[]{:S(2)}, u32[]{:S(2)}) collective-permute-start(bf16[2,64,1024]{2,1,0:T(8,128)(2,1)S(1)} %copy-done.4), channel_id=1, source_target_pairs={{0,8},{4,12},{8,0},{12,4},{1,9},{5,13},{9,1},{13,5},{2,10},{6,14},... | collective-permute-start | bytes 786440 | tf_op jit(solution)/shard_map/up1_0/ppermute | solution.py:22
  32.1 5.7 %collective-permute-start.10 = (bf16[2,64,2048]{2,1,0:T(8,128)(2,1)S(1)}, bf16[2,64,2048]{2,1,0:T(8,128)(2,1)S(1)}, u32[]{:S(2)}, u32[]{:S(2)}) collective-permute-start(bf16[2,64,2048]{2,1,0:T(8,128)(2,1)S(1)} %collective-permute-done.4.refs_2_.refs_6_), channel_id=1, source_target_pairs={{0,4},{4,0},{8,12},{12,8},{1,5},{5,1},{9,13},{13,9},{2,6},{6,2},{1... | collective-permute-start | bytes 1572872 | tf_op jit(solution)/shard_map/down0_1/ppermute | solution.py:22
  32.6 33.8 %collective-permute-start = (bf16[512,1024]{1,0:T(8,128)(2,1)S(1)}, bf16[512,1024]{1,0:T(8,128)(2,1)S(1)}, u32[]{:S(2)}, u32[]{:S(2)}) collective-permute-start(bf16[512,1024]{1,0:T(8,128)(2,1)S(1)} %copy-done.1), channel_id=1, source_target_pairs={{0,1},{1,0},{2,3},{3,2},{4,5},{5,4},{6,7},{7,6},{8,9},{9,8},{10,11... | collective-permute-start | bytes 3145736 | tf_op jit(solution)/shard_map/outer/ppermute | solution.py:22
  33.2 33.3 %collective-permute-start.1 = (bf16[512,1024]{1,0:T(8,128)(2,1)S(1)}, bf16[512,1024]{1,0:T(8,128)(2,1)S(1)}, u32[]{:S(2)}, u32[]{:S(2)}) collective-permute-start(bf16[512,1024]{1,0:T(8,128)(2,1)S(1)} %copy-done.1), channel_id=1, source_target_pairs={{1,2},{2,1},{5,6},{6,5},{9,10},{10,9},{13,14},{14,13},{17,18},{18,... | collective-permute-start | bytes 3145736 | tf_op jit(solution)/shard_map/inner/ppermute | solution.py:22
  33.9 4.4 %collective-permute-start.8 = (bf16[2,64,2048]{2,1,0:T(8,128)(2,1)S(1)}, bf16[2,64,2048]{2,1,0:T(8,128)(2,1)S(1)}, u32[]{:S(2)}, u32[]{:S(2)}) collective-permute-start(bf16[2,64,2048]{2,1,0:T(8,128)(2,1)S(1)} %bitcast.8), channel_id=1, source_target_pairs={{0,4},{4,0},{8,12},{12,8},{1,5},{5,1},{9,13},{13,9},{2,6},{6,2},{1... | collective-permute-start | bytes 1572872 | tf_op jit(solution)/shard_map/down0_0/ppermute | solution.py:22
  36.2 30.1 %collective-permute-start.6 = (bf16[256,1024]{1,0:T(8,128)(2,1)}, bf16[256,1024]{1,0:T(8,128)(2,1)S(1)}, u32[]{:S(2)}, u32[]{:S(2)}) collective-permute-start(bf16[256,1024]{1,0:T(8,128)(2,1)} %collective-permute-done.2), channel_id=1, source_target_pairs={{0,16},{4,12},{8,24},{12,4},{16,0},{20,28},{24,8},{28,20},{1,17},{... | collective-permute-start | bytes 1572872 | tf_op jit(solution)/shard_map/turn_a1/ppermute | solution.py:22
  37.7 28.7 %collective-permute-start.7 = (bf16[256,1024]{1,0:T(8,128)(2,1)}, bf16[256,1024]{1,0:T(8,128)(2,1)S(1)}, u32[]{:S(2)}, u32[]{:S(2)}) collective-permute-start(bf16[256,1024]{1,0:T(8,128)(2,1)} %collective-permute-done.3), channel_id=1, source_target_pairs={{0,16},{4,12},{8,24},{12,4},{16,0},{20,28},{24,8},{28,20},{1,17},{... | collective-permute-start | bytes 1572872 | tf_op jit(solution)/shard_map/turn_a3/ppermute | solution.py:22
  41.5 24.8 %collective-permute-start.12 = (bf16[512,128]{1,0:T(8,128)(2,1)S(1)}, bf16[512,128]{1,0:T(8,128)(2,1)S(1)}, u32[]{:S(2)}, u32[]{:S(2)}) collective-permute-start(bf16[512,128]{1,0:T(8,128)(2,1)S(1)} %rank_partials.1), channel_id=1, source_target_pairs={{0,2},{1,3},{2,0},{3,1},{4,6},{5,7},{6,4},{7,5},{8,10},{9,11},{10,... | collective-permute-start | bytes 393224 | tf_op jit(solution)/shard_map/rank_sum1/ppermute | solution.py:22
  66.5 28.9 %collective-permute-start.16 = (bf16[512,1024]{1,0:T(8,128)(2,1)S(1)}, bf16[512,1024]{1,0:T(8,128)(2,1)S(1)}, u32[]{:S(2)}, u32[]{:S(2)}) collective-permute-start(bf16[512,1024]{1,0:T(8,128)(2,1)S(1)} %constant_dynamic-update-slice_fusion.2.refs_4_), channel_id=1, source_target_pairs={{0,8},{4,20},{8,0},{12,28},{16,24},{20,4},{24,16},{28,12},{1,9},{5... | collective-permute-start | bytes 3145736 | tf_op jit(solution)/shard_map/turn_b3/ppermute | solution.py:22
  68.1 27.3 %collective-permute-start.15 = (bf16[512,1024]{1,0:T(8,128)(2,1)S(1)}, bf16[512,1024]{1,0:T(8,128)(2,1)S(1)}, u32[]{:S(2)}, u32[]{:S(2)}) collective-permute-start(bf16[512,1024]{1,0:T(8,128)(2,1)S(1)} %constant_dynamic-update-slice_fusion.refs_1_), channel_id=1, source_target_pairs={{0,8},{4,20},{8,0},{12,28},{16,24},{20,4},{24,16},{28,12},{1,9},{5... | collective-permute-start | bytes 3145736 | tf_op jit(solution)/shard_map/turn_b1/ppermute | solution.py:22
  68.7 8.0 %collective-permute-start.17 = (bf16[512,128]{1,0:T(8,128)(2,1)S(1)}, bf16[512,128]{1,0:T(8,128)(2,1)S(1)}, u32[]{:S(2)}, u32[]{:S(2)}) collective-permute-start(bf16[512,128]{1,0:T(8,128)(2,1)S(1)} %add_convert_fusion.2), channel_id=1, source_target_pairs={{0,1},{1,0},{2,3},{3,2},{4,5},{5,4},{6,7},{7,6},{8,9},{9,8},{10,11... | collective-permute-start | bytes 393224 | tf_op jit(solution)/shard_map/rank_sum0/ppermute | solution.py:22
  68.7 26.6 %collective-permute-start.13 = (bf16[256,1024]{1,0:T(8,128)(2,1)S(1)}, bf16[256,1024]{1,0:T(8,128)(2,1)S(1)}, u32[]{:S(2)}, u32[]{:S(2)}) collective-permute-start(bf16[256,1024]{1,0:T(8,128)(2,1)S(1)} %get-tuple-element.100), channel_id=1, source_target_pairs={{1,0},{2,3},{5,4},{6,7},{9,8},{10,11},{13,12},{14,15},{17,16},{18,... | collective-permute-start | bytes 1572872 | tf_op jit(solution)/shard_map/inner_out0/ppermute | solution.py:22
  70.0 25.3 %collective-permute-start.14 = (bf16[256,1024]{1,0:T(8,128)(2,1)S(1)}, bf16[256,1024]{1,0:T(8,128)(2,1)S(1)}, u32[]{:S(2)}, u32[]{:S(2)}) collective-permute-start(bf16[256,1024]{1,0:T(8,128)(2,1)S(1)} %get-tuple-element.59), channel_id=1, source_target_pairs={{0,2},{1,3},{2,0},{3,1},{4,6},{5,7},{6,4},{7,5},{8,10},{9,11},{10,... | collective-permute-start | bytes 1572872 | tf_op jit(solution)/shard_map/piece2/ppermute | solution.py:22
  96.0 9.2 %collective-permute-start.22 = (bf16[256,1024]{1,0:T(8,128)(2,1)S(1)}, bf16[256,1024]{1,0:T(8,128)(2,1)S(1)}, u32[]{:S(2)}, u32[]{:S(2)}) collective-permute-start(bf16[256,1024]{1,0:T(8,128)(2,1)S(1)} %collective-permute-done.14), channel_id=1, source_target_pairs={{0,16},{4,12},{8,24},{12,4},{16,0},{20,28},{24,8},{28,20},{1,17},{... | collective-permute-start | bytes 1572872 | tf_op jit(solution)/shard_map/turn_a2/ppermute | solution.py:22
  97.5 4.5 %collective-permute-start.19 = (bf16[256,1024]{1,0:T(8,128)(2,1)S(1)}, bf16[256,1024]{1,0:T(8,128)(2,1)S(1)}, u32[]{:S(2)}, u32[]{:S(2)}) collective-permute-start(bf16[256,1024]{1,0:T(8,128)(2,1)S(1)} %get-tuple-element.68), channel_id=1, source_target_pairs={{1,2},{2,1},{5,6},{6,5},{9,10},{10,9},{13,14},{14,13},{17,18},{18,... | collective-permute-start | bytes 1572872 | tf_op jit(solution)/shard_map/outer_in0/ppermute | solution.py:22
  98.1 15.6 %collective-permute-start.18 = (bf16[256,1024]{1,0:T(8,128)(2,1)S(1)}, bf16[256,1024]{1,0:T(8,128)(2,1)S(1)}, u32[]{:S(2)}, u32[]{:S(2)}) collective-permute-start(bf16[256,1024]{1,0:T(8,128)(2,1)S(1)} %get-tuple-element.67), channel_id=1, source_target_pairs={{1,0},{2,3},{5,4},{6,7},{9,8},{10,11},{13,12},{14,15},{17,16},{18,... | collective-permute-start | bytes 1572872 | tf_op jit(solution)/shard_map/inner_out1/ppermute | solution.py:22
  99.7 25.3 %collective-permute-start.25 = (bf16[2,64,3072]{2,1,0:T(8,128)(2,1)S(1)}, bf16[2,64,3072]{2,1,0:T(8,128)(2,1)S(1)}, u32[]{:S(2)}, u32[]{:S(2)}) collective-permute-start(bf16[2,64,3072]{2,1,0:T(8,128)(2,1)S(1)} %add_convert_fusion), channel_id=1, source_target_pairs={{0,8},{4,12},{8,0},{12,4},{1,9},{5,13},{9,1},{13,5},{2,10},{6,14},... | collective-permute-start | bytes 2359304 | tf_op jit(solution)/shard_map/grads1/ppermute | solution.py:22
  101.2 12.5 %collective-permute-start.20 = (bf16[256,1024]{1,0:T(8,128)(2,1)S(1)}, bf16[256,1024]{1,0:T(8,128)(2,1)S(1)}, u32[]{:S(2)}, u32[]{:S(2)}) collective-permute-start(bf16[256,1024]{1,0:T(8,128)(2,1)S(1)} %get-tuple-element.69), channel_id=1, source_target_pairs={{1,2},{2,1},{5,6},{6,5},{9,10},{10,9},{13,14},{14,13},{17,18},{18,... | collective-permute-start | bytes 1572872 | tf_op jit(solution)/shard_map/outer_in1/ppermute | solution.py:22
  101.9 23.0 %collective-permute-start.21 = (bf16[256,1024]{1,0:T(8,128)(2,1)S(1)}, bf16[256,1024]{1,0:T(8,128)(2,1)S(1)}, u32[]{:S(2)}, u32[]{:S(2)}) collective-permute-start(bf16[256,1024]{1,0:T(8,128)(2,1)S(1)} %collective-permute-done.19), channel_id=1, source_target_pairs={{1,0},{2,3},{5,4},{6,7},{9,8},{10,11},{13,12},{14,15},{17,16},{18,... | collective-permute-start | bytes 1572872 | tf_op jit(solution)/shard_map/outer_in_out0/ppermute | solution.py:22
  105.1 20.3 %collective-permute-start.30 = (bf16[1,64,3072]{2,1,0:T(8,128)(2,1)S(1)}, bf16[1,64,3072]{2,1,0:T(8,128)(2,1)S(1)}, u32[]{:S(2)}, u32[]{:S(2)}) collective-permute-start(bf16[1,64,3072]{2,1,0:T(8,128)(2,1)S(1)} %get-tuple-element.84), channel_id=1, source_target_pairs={{0,4},{4,0},{8,12},{12,8},{1,5},{5,1},{9,13},{13,9},{2,6},{6,2},{1... | collective-permute-start | bytes 1179656 | tf_op jit(solution)/shard_map/grads0_0/ppermute | solution.py:22
  113.7 12.2 %collective-permute-start.31 = (bf16[1,64,3072]{2,1,0:T(8,128)(2,1)S(1)}, bf16[1,64,3072]{2,1,0:T(8,128)(2,1)S(1)}, u32[]{:S(2)}, u32[]{:S(2)}) collective-permute-start(bf16[1,64,3072]{2,1,0:T(8,128)(2,1)S(1)} %get-tuple-element.85), channel_id=1, source_target_pairs={{0,4},{4,0},{8,12},{12,8},{1,5},{5,1},{9,13},{13,9},{2,6},{6,2},{1... | collective-permute-start | bytes 1179656 | tf_op jit(solution)/shard_map/grads0_1/ppermute | solution.py:22
  113.8 33.4 %collective-permute-start.34 = (bf16[512,1024]{1,0:T(8,128)(2,1)S(1)}, bf16[512,1024]{1,0:T(8,128)(2,1)S(1)}, u32[]{:S(2)}, u32[]{:S(2)}) collective-permute-start(bf16[512,1024]{1,0:T(8,128)(2,1)S(1)} %constant_dynamic-update-slice_fusion.2.refs_4_), channel_id=1, source_target_pairs={{0,4},{4,0},{8,12},{12,8},{16,20},{20,16},{24,28},{28,24},{1,5},{5... | collective-permute-start | bytes 3145736 | tf_op jit(solution)/shard_map/turn_c30/ppermute | solution.py:22
  124.9 5.2 %collective-permute-start.27 = (bf16[512,1024]{1,0:T(8,128)(2,1)S(1)}, bf16[512,1024]{1,0:T(8,128)(2,1)S(1)}, u32[]{:S(2)}, u32[]{:S(2)}) collective-permute-start(bf16[512,1024]{1,0:T(8,128)(2,1)S(1)} %constant_dynamic-update-slice_fusion.refs_1_), channel_id=1, source_target_pairs={{0,4},{4,0},{8,12},{12,8},{16,20},{20,16},{24,28},{28,24},{1,5},{5... | collective-permute-start | bytes 3145736 | tf_op jit(solution)/shard_map/turn_c10/ppermute | solution.py:22
  124.9 6.7 %collective-permute-start.28 = (bf16[512,1024]{1,0:T(8,128)(2,1)S(1)}, bf16[512,1024]{1,0:T(8,128)(2,1)S(1)}, u32[]{:S(2)}, u32[]{:S(2)}) collective-permute-start(bf16[512,1024]{1,0:T(8,128)(2,1)S(1)} %collective-permute-done.15.refs_2_), channel_id=1, source_target_pairs={{0,4},{4,0},{8,12},{12,8},{16,20},{20,16},{24,28},{28,24},{1,5},{5... | collective-permute-start | bytes 3145736 | tf_op jit(solution)/shard_map/turn_c11/ppermute | solution.py:22
  125.4 16.6 %collective-permute-start.26 = (bf16[512,1024]{1,0:T(8,128)(2,1)S(1)}, bf16[512,1024]{1,0:T(8,128)(2,1)S(1)}, u32[]{:S(2)}, u32[]{:S(2)}) collective-permute-start(bf16[512,1024]{1,0:T(8,128)(2,1)S(1)} %pad_maximum_fusion.refs_2_), channel_id=1, source_target_pairs={{0,8},{4,20},{8,0},{12,28},{16,24},{20,4},{24,16},{28,12},{1,9},{5... | collective-permute-start | bytes 3145736 | tf_op jit(solution)/shard_map/turn_b2/ppermute | solution.py:22
  126.0 16.1 %collective-permute-start.29 = (bf16[256,1024]{1,0:T(8,128)(2,1)S(1)}, bf16[256,1024]{1,0:T(8,128)(2,1)S(1)}, u32[]{:S(2)}, u32[]{:S(2)}) collective-permute-start(bf16[256,1024]{1,0:T(8,128)(2,1)S(1)} %collective-permute-done.20), channel_id=1, source_target_pairs={{1,0},{2,3},{5,4},{6,7},{9,8},{10,11},{13,12},{14,15},{17,16},{18,... | collective-permute-start | bytes 1572872 | tf_op jit(solution)/shard_map/outer_in_out1/ppermute | solution.py:22
  130.1 17.2 %collective-permute-start.35 = (bf16[512,1024]{1,0:T(8,128)(2,1)S(1)}, bf16[512,1024]{1,0:T(8,128)(2,1)S(1)}, u32[]{:S(2)}, u32[]{:S(2)}) collective-permute-start(bf16[512,1024]{1,0:T(8,128)(2,1)S(1)} %collective-permute-done.16.refs_5_), channel_id=1, source_target_pairs={{0,4},{4,0},{8,12},{12,8},{16,20},{20,16},{24,28},{28,24},{1,5},{5... | collective-permute-start | bytes 3145736 | tf_op jit(solution)/shard_map/turn_c31/ppermute | solution.py:22
  142.1 5.2 %collective-permute-start.32 = (bf16[512,1024]{1,0:T(8,128)(2,1)S(1)}, bf16[512,1024]{1,0:T(8,128)(2,1)S(1)}, u32[]{:S(2)}, u32[]{:S(2)}) collective-permute-start(bf16[512,1024]{1,0:T(8,128)(2,1)S(1)} %pad_maximum_fusion.refs_2_), channel_id=1, source_target_pairs={{0,4},{4,0},{8,12},{12,8},{16,20},{20,16},{24,28},{28,24},{1,5},{5... | collective-permute-start | bytes 3145736 | tf_op jit(solution)/shard_map/turn_c20/ppermute | solution.py:22
  142.5 4.8 %collective-permute-start.33 = (bf16[512,1024]{1,0:T(8,128)(2,1)S(1)}, bf16[512,1024]{1,0:T(8,128)(2,1)S(1)}, u32[]{:S(2)}, u32[]{:S(2)}) collective-permute-start(bf16[512,1024]{1,0:T(8,128)(2,1)S(1)} %collective-permute-done.26.refs_3_), channel_id=1, source_target_pairs={{0,4},{4,0},{8,12},{12,8},{16,20},{20,16},{24,28},{28,24},{1,5},{5... | collective-permute-start | bytes 3145736 | tf_op jit(solution)/shard_map/turn_c21/ppermute | solution.py:22
  (11 other events, 110.9 us)

commit v7 on v6

--- a/solution.py
+++ b/solution.py
@@ -423,6 +423,7 @@
         )
 
         end_three1 = move("outer_in_out1", two1, "tensor", outward)
+        core2 = move("turn_c20", wide2, copies, turn_c)
         wide2 = [wide2, move("turn_b2", wide2, copies, turn_b)]
         other1 = [move(f"turn_c1{i}", part, copies, turn_c) for i, part in enumerate(wide1)]
         acc = folded(acc, [by_one], [wide1 + other1], relative_tile, 0, table=[pair[0] for pair in table], both=both)
@@ -431,12 +432,12 @@
         )
         total = keep[:rest].astype(F32) + jnp.concatenate(got[:rest], axis=0).astype(F32) + far.astype(F32)
         grad_down, grad_up = jnp.swapaxes(total[:, :, :width], 1, 2), total[:, :, width:]
-        wide2, acc, end_three1, two, grad_down, grad_up = together(
-            wide2, acc, end_three1, two, grad_down, grad_up
+        wide2, core2, acc, end_three1, two, grad_down, grad_up = together(
+            wide2, core2, acc, end_three1, two, grad_down, grad_up
         )
         end_three = jnp.concatenate([end_three0, end_three1], axis=0)
 
-        other2 = [move(f"turn_c2{i}", part, copies, turn_c) for i, part in enumerate(wide2)]
+        other2 = [core2, move("turn_c21", wide2[1], copies, turn_c)]
         other3 = [move(f"turn_c3{i}", part, copies, turn_c) for i, part in enumerate(wide3)]
         three = jnp.where(middle, across, end_three)
         result = folded(acc, [two, three], [wide2, wide3], relative_tile, 0, final=True)

time: 152 us -> 155 us (1.020)
  waiting for transfers between devices: 73 us -> 80.1 us
  starting transfers between devices: 35.2 us -> 31.8 us
    ppermute x36, waiting for transfers between devices: 73 us -> 80.1 us  [move(): return lax.ppermute(a, axis, pairs)]
    ppermute x36, starting transfers between devices: 35.2 us -> 31.8 us  [move(): return lax.ppermute(a, axis, pairs)]
  transfers between devices with their start and end apart: 36 -> 36, of which waited for: 10 -> 12; matrix products, arithmetic and copies ran while one was open for 4% -> 5% of each run, Pallas kernels for 16% -> 15%
where the time goes in v7:
time: 155 us
  waiting for transfers between devices  80.1 us (52%)
  starting transfers between devices  31.8 us (21%)
  Pallas kernels  28.1 us (18%)
  local copies, waits for them, and re-layouts  12.3 us (8%)
  other arithmetic  1.6 us (1%)
    ppermute x36, waiting for transfers between devices, move(): return lax.ppermute(a, axis, pairs)  80.1 us
    ppermute x36, starting transfers between devices, move(): return lax.ppermute(a, axis, pairs)  31.8 us
    pallas_call x3, Pallas kernels, fold(): pl.pallas_call(functools.partial(fold_kernel, terms=len(xs), parts=parts,...  17.6 us
    unnamed x16, local copies, waits for them, and re-layouts  7.95 us
    pallas_call x1, Pallas kernels, local_products(): pl.pallas_call(local_kernel, grid_spec=pltpu.PrefetchScalarGridSpec(num_s...  3.8 us
    pallas_call x1, Pallas kernels, member_grads(): pl.pallas_call(functools.partial(grads_kernel, width=width, blocks=blocks...  3.44 us
    pallas_call x1, Pallas kernels, rank_partials(): pl.pallas_call(functools.partial(rank_kernel, blocks=blocks, slot=slot, h...  3.24 us
  transfers between devices with their start and end apart: 36, of which 12 were waited for; matrix products, arithmetic and copies ran while one was open for 5% of the time, Pallas kernels for 15%

profile of v7, /device:TPU:0, one launch (start us, length us, event | category | flops | bytes accessed | tf_op | source)
XLA Modules:
  0.0 154.8 jit_solution(13806628971891571483)
XLA Ops:
  0.7 3.0 %collective-permute-start.4 = (bf16[2,64,2048]{2,1,0:T(8,128)(2,1)}, bf16[2,64,2048]{2,1,0:T(8,128)(2,1)S(1)}, u32[]{:S(2)}, u32[]{:S(2)}) collective-permute-start(bf16[2,64,2048]{2,1,0:T(8,128)(2,1)} %bitcast.7), channel_id=1, source_target_pairs={{0,8},{4,12},{8,0},{12,4},{1,9},{5,13},{9,1},{13,5},{2,10},{6,14},... | collective-permute-start | bytes 1572872 | tf_op jit(solution)/shard_map/down1_0/ppermute | solution.py:22
  3.7 2.3 %constant_dynamic-slice_fusion = (bf16[256,1024]{1,0:T(8,128)(2,1)S(1)}, bf16[256,1024]{1,0:T(8,128)(2,1)}, bf16[256,1024]{1,0:T(8,128)(2,1)S(1)}) fusion(bf16[8192,1024]{1,0:T(8,128)(2,1)} %weight.1, s32[]{:T(128)S(6)} %select_n.40, s32[]{:T(128)S(6)} %select_n.39, s32[]{:T(128)S(6)} %select_n.38), kind=kLoop, calls=%fused_computation.12 | loop fusion | bytes 3145740 | tf_op jit(solution)/shard_map/dynamic_slice | solution.py:343
  6.0 3.6 %collective-permute-start.3 = (bf16[256,1024]{1,0:T(8,128)(2,1)}, bf16[256,1024]{1,0:T(8,128)(2,1)}, u32[]{:S(2)}, u32[]{:S(2)}) collective-permute-start(bf16[256,1024]{1,0:T(8,128)(2,1)} %get-tuple-element.100), channel_id=1, source_target_pairs={{0,3},{1,2},{2,1},{3,0},{4,7},{5,6},{6,5},{7,4},{8,11},{9,10},{10,... | collective-permute-start | bytes 1572872 | tf_op jit(solution)/shard_map/piece3/ppermute | solution.py:22
  10.2 5.8 %copy-done = bf16[8192,1024]{1,0:T(8,128)(2,1)S(1)} copy-done((bf16[8192,1024]{1,0:T(8,128)(2,1)S(1)}, bf16[8192,1024]{1,0:T(8,128)(2,1)}, u32[]{:S(2)}) %copy-start) | copy-done | bytes 16777240
  16.0 3.8 %local_products.1.acc = f32[512,2048]{1,0:T(8,128)S(1)} custom-call(s32[4]{0:T(128)S(1)} %pad_add_fusion.ids, bf16[512,1024]{1,0:T(8,128)(2,1)S(1)} %copy-done.1, bf16[8192,1024]{1,0:T(8,128)(2,1)S(1)} %copy-done), custom_call_target="tpu_custom_call" | custom-call | flops 1 | bytes 1 | tf_op jit(solution)/shard_map/local_products/pallas_call | solution.py:195
  19.8 1.7 %collective-permute-done.5.refs_3_ = bf16[2,64,1024]{2,1,0:T(8,128)(2,1)S(1)} collective-permute-done((bf16[2,64,1024]{2,1,0:T(8,128)(2,1)S(1)}, bf16[2,64,1024]{2,1,0:T(8,128)(2,1)S(1)}, u32[]{:S(2)}, u32[]{:S(2)}) %collective-permute-start.5) | collective-permute-done | bytes 262176 | tf_op jit(solution)/shard_map/up1_0/ppermute | solution.py:22
  21.4 1.6 %collective-permute-done.3 = bf16[256,1024]{1,0:T(8,128)(2,1)} collective-permute-done((bf16[256,1024]{1,0:T(8,128)(2,1)}, bf16[256,1024]{1,0:T(8,128)(2,1)}, u32[]{:S(2)}, u32[]{:S(2)}) %collective-permute-start.3) | collective-permute-done | bytes 524320 | tf_op jit(solution)/shard_map/piece3/ppermute | solution.py:22
  23.0 9.9 %collective-permute-done.2 = bf16[256,1024]{1,0:T(8,128)(2,1)} collective-permute-done((bf16[256,1024]{1,0:T(8,128)(2,1)S(1)}, bf16[256,1024]{1,0:T(8,128)(2,1)}, u32[]{:S(2)}, u32[]{:S(2)}) %collective-permute-start.2) | collective-permute-done | bytes 524320 | tf_op jit(solution)/shard_map/piece1/ppermute | solution.py:22
  33.6 2.9 %collective-permute-start = (bf16[512,1024]{1,0:T(8,128)(2,1)S(1)}, bf16[512,1024]{1,0:T(8,128)(2,1)S(1)}, u32[]{:S(2)}, u32[]{:S(2)}) collective-permute-start(bf16[512,1024]{1,0:T(8,128)(2,1)S(1)} %copy-done.1), channel_id=1, source_target_pairs={{0,1},{1,0},{2,3},{3,2},{4,5},{5,4},{6,7},{7,6},{8,9},{9,8},{10,11... | collective-permute-start | bytes 3145736 | tf_op jit(solution)/shard_map/outer/ppermute | solution.py:22
  37.3 2.3 %collective-permute-done.11.refs_7_ = bf16[2,64,1024]{2,1,0:T(8,128)(2,1)S(1)} collective-permute-done((bf16[2,64,1024]{2,1,0:T(8,128)(2,1)S(1)}, bf16[2,64,1024]{2,1,0:T(8,128)(2,1)S(1)}, u32[]{:S(2)}, u32[]{:S(2)}) %collective-permute-start.11) | collective-permute-done | bytes 262176 | tf_op jit(solution)/shard_map/up0_1/ppermute | solution.py:22
  39.6 1.5 collective-permute-start.6
  41.7 3.2 %rank_partials.1 = bf16[512,128]{1,0:T(8,128)(2,1)S(1)} custom-call(s32[4]{0:T(128)S(1)} %pad_add_fusion.ids, s32[16]{0:T(128)S(1)} %copy-done.5, s32[8]{0:T(128)S(1)} %copy-done.6, bf16[512,2048]{1,0:T(8,128)(2,1)S(1)} %copy-done.2, bf16[512,1024]{1,0:T(8,128)(2,1)S(1)} %copy-done.1, bf16[2,64,2048]{2,1,0:T(8,128)(2,1)S(1)} %bitcast.9, ...), custom_call_target="tpu_custom_call" | custom-call | flops 1 | bytes 1 | tf_op jit(solution)/shard_map/rank_partials/pallas_call | solution.py:89
  44.9 1.6 %collective-permute-start.12 = (bf16[512,128]{1,0:T(8,128)(2,1)S(1)}, bf16[512,128]{1,0:T(8,128)(2,1)S(1)}, u32[]{:S(2)}, u32[]{:S(2)}) collective-permute-start(bf16[512,128]{1,0:T(8,128)(2,1)S(1)} %rank_partials.1), channel_id=1, source_target_pairs={{0,2},{1,3},{2,0},{3,1},{4,6},{5,7},{6,4},{7,5},{8,10},{9,11},{10,... | collective-permute-start | bytes 393224 | tf_op jit(solution)/shard_map/rank_sum1/ppermute | solution.py:22
  47.6 1.1 constant_dynamic-update-slice_fusion.3
  48.7 18.4 %collective-permute-done.12 = bf16[512,128]{1,0:T(8,128)(2,1)S(1)} collective-permute-done((bf16[512,128]{1,0:T(8,128)(2,1)S(1)}, bf16[512,128]{1,0:T(8,128)(2,1)S(1)}, u32[]{:S(2)}, u32[]{:S(2)}) %collective-permute-start.12) | collective-permute-done | bytes 131104 | tf_op jit(solution)/shard_map/rank_sum1/ppermute | solution.py:22
  67.9 1.5 collective-permute-start.15
  69.4 1.8 %collective-permute-start.14 = (bf16[256,1024]{1,0:T(8,128)(2,1)S(1)}, bf16[256,1024]{1,0:T(8,128)(2,1)S(1)}, u32[]{:S(2)}, u32[]{:S(2)}) collective-permute-start(bf16[256,1024]{1,0:T(8,128)(2,1)S(1)} %get-tuple-element.60), channel_id=1, source_target_pairs={{0,2},{1,3},{2,0},{3,1},{4,6},{5,7},{6,4},{7,5},{8,10},{9,11},{10,... | collective-permute-start | bytes 1572872 | tf_op jit(solution)/shard_map/piece2/ppermute | solution.py:22
  71.2 1.3 collective-permute-start.13
  72.5 4.0 %collective-permute-done.17 = bf16[512,128]{1,0:T(8,128)(2,1)S(1)} collective-permute-done((bf16[512,128]{1,0:T(8,128)(2,1)S(1)}, bf16[512,128]{1,0:T(8,128)(2,1)S(1)}, u32[]{:S(2)}, u32[]{:S(2)}) %collective-permute-start.17) | collective-permute-done | bytes 131104 | tf_op jit(solution)/shard_map/rank_sum0/ppermute | solution.py:22
  76.7 3.4 %member_grads.1 = (bf16[1,64,3072]{2,1,0:T(8,128)(2,1)S(1)}, bf16[1,64,3072]{2,1,0:T(8,128)(2,1)S(1)}, bf16[1,64,3072]{2,1,0:T(8,128)(2,1)S(1)}, bf16[1,64,3072]...) custom-call(s32[4]{0:T(128)S(1)} %pad_add_fusion.ids, s32[16]{0:T(128)S(1)} %copy-done.5, bf16[512,2048]{1,0:T(8,128)(2,1)S(1)} %copy-done.2, ...), custom_call_target="tpu_custom_call" | custom-call | flops 1 | bytes 1 | tf_op jit(solution)/shard_map/member_grads/pallas_call | solution.py:141
  80.1 14.6 %collective-permute-done.14 = bf16[256,1024]{1,0:T(8,128)(2,1)S(1)} collective-permute-done((bf16[256,1024]{1,0:T(8,128)(2,1)S(1)}, bf16[256,1024]{1,0:T(8,128)(2,1)S(1)}, u32[]{:S(2)}, u32[]{:S(2)}) %collective-permute-start.14) | collective-permute-done | bytes 524320 | tf_op jit(solution)/shard_map/piece2/ppermute | solution.py:22
  94.7 1.8 %collective-permute-done.13 = bf16[256,1024]{1,0:T(8,128)(2,1)S(1)} collective-permute-done((bf16[256,1024]{1,0:T(8,128)(2,1)S(1)}, bf16[256,1024]{1,0:T(8,128)(2,1)S(1)}, u32[]{:S(2)}, u32[]{:S(2)}) %collective-permute-start.13) | collective-permute-done | bytes 524320 | tf_op jit(solution)/shard_map/inner_out0/ppermute | solution.py:22
  97.0 1.3 collective-permute-start.18
  99.0 1.6 %collective-permute-start.22 = (bf16[256,1024]{1,0:T(8,128)(2,1)S(1)}, bf16[256,1024]{1,0:T(8,128)(2,1)S(1)}, u32[]{:S(2)}, u32[]{:S(2)}) collective-permute-start(bf16[256,1024]{1,0:T(8,128)(2,1)S(1)} %collective-permute-done.14), channel_id=1, source_target_pairs={{0,16},{4,12},{8,24},{12,4},{16,0},{20,28},{24,8},{28,20},{1,17},{... | collective-permute-start | bytes 1572872 | tf_op jit(solution)/shard_map/turn_a2/ppermute | solution.py:22
  102.1 1.3 collective-permute-start.21
  103.4 9.4 %collective-permute-done.18 = bf16[256,1024]{1,0:T(8,128)(2,1)S(1)} collective-permute-done((bf16[256,1024]{1,0:T(8,128)(2,1)S(1)}, bf16[256,1024]{1,0:T(8,128)(2,1)S(1)}, u32[]{:S(2)}, u32[]{:S(2)}) %collective-permute-start.18) | collective-permute-done | bytes 524320 | tf_op jit(solution)/shard_map/inner_out1/ppermute | solution.py:22
  113.4 15.4 %collective-permute-done.21 = bf16[256,1024]{1,0:T(8,128)(2,1)S(1)} collective-permute-done((bf16[256,1024]{1,0:T(8,128)(2,1)S(1)}, bf16[256,1024]{1,0:T(8,128)(2,1)S(1)}, u32[]{:S(2)}, u32[]{:S(2)}) %collective-permute-start.21) | collective-permute-done | bytes 524320 | tf_op jit(solution)/shard_map/outer_in_out0/ppermute | solution.py:22
  129.3 1.5 collective-permute-start.30
  130.8 1.2 collective-permute-start.28
  136.1 9.2 %fold.1.acc = f32[512,2048]{1,0:T(8,128)S(1)} custom-call(s32[4]{0:T(128)S(1)} %pad_add_fusion.ids, s32[16]{0:T(128)S(1)} %copy-done.5, s32[8]{0:T(128)S(1)} %copy-done.6, f32[512,2048]{1,0:T(8,128)S(1)} %local_products.1.acc, bf16[512,1024]{1,0:T(8,128)(2,1)S(1)} %collective-permute-done.refs_0_, ...), custom_call_target="tpu_custom_call", output_to_operand_aliasing={{}: (3, {})} | custom-call | flops 1 | bytes 1 | tf_op jit(solution)/shard_map/fold/pallas_call | solution.py:280
  146.4 4.2 %finish.2.refs_6_ = bf16[512,2048]{1,0:T(8,128)(2,1)} custom-call(s32[4]{0:T(128)S(1)} %pad_add_fusion.ids, s32[16]{0:T(128)S(1)} %copy-done.5, s32[8]{0:T(128)S(1)} %copy-done.6, f32[512,2048]{1,0:T(8,128)S(1)} %fold.1.acc, bf16[512,1024]{1,0:T(8,128)(2,1)S(1)} %maximum_select_fusion.refs_0_, bf16[512,1024]{1,0:T(8,128)(2,1)S(1)} %maximum_select_fusion.1.refs_1_, ...), custom_call_target="tpu_custom_call" | custom-call | flops 1 | bytes 1 | tf_op jit(solution)/shard_map/finish/pallas_call | solution.py:280
  150.6 4.2 %finish.3 = bf16[512,2048]{1,0:T(8,128)(2,1)} custom-call(s32[4]{0:T(128)S(1)} %pad_add_fusion.ids, s32[16]{0:T(128)S(1)} %copy-done.5, s32[8]{0:T(128)S(1)} %copy-done.6, f32[512,2048]{1,0:T(8,128)S(1)} %fold.1.acc, bf16[512,1024]{1,0:T(8,128)(2,1)S(1)} %maximum_select_fusion.refs_0_, ...), custom_call_target="tpu_custom_call", output_to_operand_aliasing={{}: (10, {})} | custom-call | flops 1 | bytes 1 | tf_op jit(solution)/shard_map/finish/pallas_call | solution.py:280
  (77 shorter events, 13.7 us)
Async XLA Ops:
  0.7 20.8 %collective-permute-start.4 = (bf16[2,64,2048]{2,1,0:T(8,128)(2,1)}, bf16[2,64,2048]{2,1,0:T(8,128)(2,1)S(1)}, u32[]{:S(2)}, u32[]{:S(2)}) collective-permute-start(bf16[2,64,2048]{2,1,0:T(8,128)(2,1)} %bitcast.7), channel_id=1, source_target_pairs={{0,8},{4,12},{8,0},{12,4},{1,9},{5,13},{9,1},{13,5},{2,10},{6,14},... | collective-permute-start | bytes 1572872 | tf_op jit(solution)/shard_map/down1_0/ppermute | solution.py:22
  6.0 17.0 %collective-permute-start.3 = (bf16[256,1024]{1,0:T(8,128)(2,1)}, bf16[256,1024]{1,0:T(8,128)(2,1)}, u32[]{:S(2)}, u32[]{:S(2)}) collective-permute-start(bf16[256,1024]{1,0:T(8,128)(2,1)} %get-tuple-element.100), channel_id=1, source_target_pairs={{0,3},{1,2},{2,1},{3,0},{4,7},{5,6},{6,5},{7,4},{8,11},{9,10},{10,... | collective-permute-start | bytes 1572872 | tf_op jit(solution)/shard_map/piece3/ppermute | solution.py:22
  9.6 23.3 %collective-permute-start.2 = (bf16[256,1024]{1,0:T(8,128)(2,1)S(1)}, bf16[256,1024]{1,0:T(8,128)(2,1)}, u32[]{:S(2)}, u32[]{:S(2)}) collective-permute-start(bf16[256,1024]{1,0:T(8,128)(2,1)S(1)} %get-tuple-element.101), channel_id=1, source_target_pairs={{0,1},{1,0},{2,3},{3,2},{4,5},{5,4},{6,7},{7,6},{8,9},{9,8},{10,11... | collective-permute-start | bytes 1572872 | tf_op jit(solution)/shard_map/piece1/ppermute | solution.py:22
  9.6 11.8 %collective-permute-start.5 = (bf16[2,64,1024]{2,1,0:T(8,128)(2,1)S(1)}, bf16[2,64,1024]{2,1,0:T(8,128)(2,1)S(1)}, u32[]{:S(2)}, u32[]{:S(2)}) collective-permute-start(bf16[2,64,1024]{2,1,0:T(8,128)(2,1)S(1)} %copy-done.4), channel_id=1, source_target_pairs={{0,8},{4,12},{8,0},{12,4},{1,9},{5,13},{9,1},{13,5},{2,10},{6,14},... | collective-permute-start | bytes 786440 | tf_op jit(solution)/shard_map/up1_0/ppermute | solution.py:22
  32.9 4.2 %collective-permute-start.9 = (bf16[2,64,1024]{2,1,0:T(8,128)(2,1)S(1)}, bf16[2,64,1024]{2,1,0:T(8,128)(2,1)S(1)}, u32[]{:S(2)}, u32[]{:S(2)}) collective-permute-start(bf16[2,64,1024]{2,1,0:T(8,128)(2,1)S(1)} %copy-done.4), channel_id=1, source_target_pairs={{0,4},{4,0},{8,12},{12,8},{1,5},{5,1},{9,13},{13,9},{2,6},{6,2},{1... | collective-permute-start | bytes 786440 | tf_op jit(solution)/shard_map/up0_0/ppermute | solution.py:22
  32.9 34.2 %collective-permute-start.1 = (bf16[512,1024]{1,0:T(8,128)(2,1)S(1)}, bf16[512,1024]{1,0:T(8,128)(2,1)S(1)}, u32[]{:S(2)}, u32[]{:S(2)}) collective-permute-start(bf16[512,1024]{1,0:T(8,128)(2,1)S(1)} %copy-done.1), channel_id=1, source_target_pairs={{1,2},{2,1},{5,6},{6,5},{9,10},{10,9},{13,14},{14,13},{17,18},{18,... | collective-permute-start | bytes 3145736 | tf_op jit(solution)/shard_map/inner/ppermute | solution.py:22
  33.6 33.5 %collective-permute-start = (bf16[512,1024]{1,0:T(8,128)(2,1)S(1)}, bf16[512,1024]{1,0:T(8,128)(2,1)S(1)}, u32[]{:S(2)}, u32[]{:S(2)}) collective-permute-start(bf16[512,1024]{1,0:T(8,128)(2,1)S(1)} %copy-done.1), channel_id=1, source_target_pairs={{0,1},{1,0},{2,3},{3,2},{4,5},{5,4},{6,7},{7,6},{8,9},{9,8},{10,11... | collective-permute-start | bytes 3145736 | tf_op jit(solution)/shard_map/outer/ppermute | solution.py:22
  36.6 4.5 %collective-permute-start.8 = (bf16[2,64,2048]{2,1,0:T(8,128)(2,1)S(1)}, bf16[2,64,2048]{2,1,0:T(8,128)(2,1)S(1)}, u32[]{:S(2)}, u32[]{:S(2)}) collective-permute-start(bf16[2,64,2048]{2,1,0:T(8,128)(2,1)S(1)} %bitcast.8), channel_id=1, source_target_pairs={{0,4},{4,0},{8,12},{12,8},{1,5},{5,1},{9,13},{13,9},{2,6},{6,2},{1... | collective-permute-start | bytes 1572872 | tf_op jit(solution)/shard_map/down0_0/ppermute | solution.py:22
  36.8 4.8 %collective-permute-start.10 = (bf16[2,64,2048]{2,1,0:T(8,128)(2,1)S(1)}, bf16[2,64,2048]{2,1,0:T(8,128)(2,1)S(1)}, u32[]{:S(2)}, u32[]{:S(2)}) collective-permute-start(bf16[2,64,2048]{2,1,0:T(8,128)(2,1)S(1)} %collective-permute-done.4.refs_2_.refs_6_), channel_id=1, source_target_pairs={{0,4},{4,0},{8,12},{12,8},{1,5},{5,1},{9,13},{13,9},{2,6},{6,2},{1... | collective-permute-start | bytes 1572872 | tf_op jit(solution)/shard_map/down0_1/ppermute | solution.py:22
  39.6 27.6 %collective-permute-start.6 = (bf16[256,1024]{1,0:T(8,128)(2,1)}, bf16[256,1024]{1,0:T(8,128)(2,1)S(1)}, u32[]{:S(2)}, u32[]{:S(2)}) collective-permute-start(bf16[256,1024]{1,0:T(8,128)(2,1)} %collective-permute-done.2), channel_id=1, source_target_pairs={{0,16},{4,12},{8,24},{12,4},{16,0},{20,28},{24,8},{28,20},{1,17},{... | collective-permute-start | bytes 1572872 | tf_op jit(solution)/shard_map/turn_a1/ppermute | solution.py:22
  41.1 26.1 %collective-permute-start.7 = (bf16[256,1024]{1,0:T(8,128)(2,1)}, bf16[256,1024]{1,0:T(8,128)(2,1)S(1)}, u32[]{:S(2)}, u32[]{:S(2)}) collective-permute-start(bf16[256,1024]{1,0:T(8,128)(2,1)} %collective-permute-done.3), channel_id=1, source_target_pairs={{0,16},{4,12},{8,24},{12,4},{16,0},{20,28},{24,8},{28,20},{1,17},{... | collective-permute-start | bytes 1572872 | tf_op jit(solution)/shard_map/turn_a3/ppermute | solution.py:22
  44.9 22.2 %collective-permute-start.12 = (bf16[512,128]{1,0:T(8,128)(2,1)S(1)}, bf16[512,128]{1,0:T(8,128)(2,1)S(1)}, u32[]{:S(2)}, u32[]{:S(2)}) collective-permute-start(bf16[512,128]{1,0:T(8,128)(2,1)S(1)} %rank_partials.1), channel_id=1, source_target_pairs={{0,2},{1,3},{2,0},{3,1},{4,6},{5,7},{6,4},{7,5},{8,10},{9,11},{10,... | collective-permute-start | bytes 393224 | tf_op jit(solution)/shard_map/rank_sum1/ppermute | solution.py:22
  67.2 29.2 %collective-permute-start.16 = (bf16[512,1024]{1,0:T(8,128)(2,1)S(1)}, bf16[512,1024]{1,0:T(8,128)(2,1)S(1)}, u32[]{:S(2)}, u32[]{:S(2)}) collective-permute-start(bf16[512,1024]{1,0:T(8,128)(2,1)S(1)} %constant_dynamic-update-slice_fusion.2.refs_4_), channel_id=1, source_target_pairs={{0,8},{4,20},{8,0},{12,28},{16,24},{20,4},{24,16},{28,12},{1,9},{5... | collective-permute-start | bytes 3145736 | tf_op jit(solution)/shard_map/turn_b3/ppermute | solution.py:22
  67.9 28.5 %collective-permute-start.15 = (bf16[512,1024]{1,0:T(8,128)(2,1)S(1)}, bf16[512,1024]{1,0:T(8,128)(2,1)S(1)}, u32[]{:S(2)}, u32[]{:S(2)}) collective-permute-start(bf16[512,1024]{1,0:T(8,128)(2,1)S(1)} %constant_dynamic-update-slice_fusion.refs_1_), channel_id=1, source_target_pairs={{0,8},{4,20},{8,0},{12,28},{16,24},{20,4},{24,16},{28,12},{1,9},{5... | collective-permute-start | bytes 3145736 | tf_op jit(solution)/shard_map/turn_b1/ppermute | solution.py:22
  69.4 7.2 %collective-permute-start.17 = (bf16[512,128]{1,0:T(8,128)(2,1)S(1)}, bf16[512,128]{1,0:T(8,128)(2,1)S(1)}, u32[]{:S(2)}, u32[]{:S(2)}) collective-permute-start(bf16[512,128]{1,0:T(8,128)(2,1)S(1)} %add_convert_fusion.2), channel_id=1, source_target_pairs={{0,1},{1,0},{2,3},{3,2},{4,5},{5,4},{6,7},{7,6},{8,9},{9,8},{10,11... | collective-permute-start | bytes 393224 | tf_op jit(solution)/shard_map/rank_sum0/ppermute | solution.py:22
  69.4 25.3 %collective-permute-start.14 = (bf16[256,1024]{1,0:T(8,128)(2,1)S(1)}, bf16[256,1024]{1,0:T(8,128)(2,1)S(1)}, u32[]{:S(2)}, u32[]{:S(2)}) collective-permute-start(bf16[256,1024]{1,0:T(8,128)(2,1)S(1)} %get-tuple-element.60), channel_id=1, source_target_pairs={{0,2},{1,3},{2,0},{3,1},{4,6},{5,7},{6,4},{7,5},{8,10},{9,11},{10,... | collective-permute-start | bytes 1572872 | tf_op jit(solution)/shard_map/piece2/ppermute | solution.py:22
  71.2 25.2 %collective-permute-start.13 = (bf16[256,1024]{1,0:T(8,128)(2,1)S(1)}, bf16[256,1024]{1,0:T(8,128)(2,1)S(1)}, u32[]{:S(2)}, u32[]{:S(2)}) collective-permute-start(bf16[256,1024]{1,0:T(8,128)(2,1)S(1)} %get-tuple-element.102), channel_id=1, source_target_pairs={{1,0},{2,3},{5,4},{6,7},{9,8},{10,11},{13,12},{14,15},{17,16},{18,... | collective-permute-start | bytes 1572872 | tf_op jit(solution)/shard_map/inner_out0/ppermute | solution.py:22
  96.5 4.1 %collective-permute-start.23 = (bf16[1,64,3072]{2,1,0:T(8,128)(2,1)S(1)}, bf16[1,64,3072]{2,1,0:T(8,128)(2,1)S(1)}, u32[]{:S(2)}, u32[]{:S(2)}) collective-permute-start(bf16[1,64,3072]{2,1,0:T(8,128)(2,1)S(1)} %get-tuple-element.75), channel_id=1, source_target_pairs={{0,4},{4,0},{8,12},{12,8},{1,5},{5,1},{9,13},{13,9},{2,6},{6,2},{1... | collective-permute-start | bytes 1179656 | tf_op jit(solution)/shard_map/grads0_2/ppermute | solution.py:22
  96.5 4.1 %collective-permute-start.24 = (bf16[1,64,3072]{2,1,0:T(8,128)(2,1)S(1)}, bf16[1,64,3072]{2,1,0:T(8,128)(2,1)S(1)}, u32[]{:S(2)}, u32[]{:S(2)}) collective-permute-start(bf16[1,64,3072]{2,1,0:T(8,128)(2,1)S(1)} %get-tuple-element.76), channel_id=1, source_target_pairs={{0,4},{4,0},{8,12},{12,8},{1,5},{5,1},{9,13},{13,9},{2,6},{6,2},{1... | collective-permute-start | bytes 1179656 | tf_op jit(solution)/shard_map/grads0_3/ppermute | solution.py:22
  97.0 15.8 %collective-permute-start.18 = (bf16[256,1024]{1,0:T(8,128)(2,1)S(1)}, bf16[256,1024]{1,0:T(8,128)(2,1)S(1)}, u32[]{:S(2)}, u32[]{:S(2)}) collective-permute-start(bf16[256,1024]{1,0:T(8,128)(2,1)S(1)} %get-tuple-element.68), channel_id=1, source_target_pairs={{1,0},{2,3},{5,4},{6,7},{9,8},{10,11},{13,12},{14,15},{17,16},{18,... | collective-permute-start | bytes 1572872 | tf_op jit(solution)/shard_map/inner_out1/ppermute | solution.py:22
  99.0 13.8 %collective-permute-start.22 = (bf16[256,1024]{1,0:T(8,128)(2,1)S(1)}, bf16[256,1024]{1,0:T(8,128)(2,1)S(1)}, u32[]{:S(2)}, u32[]{:S(2)}) collective-permute-start(bf16[256,1024]{1,0:T(8,128)(2,1)S(1)} %collective-permute-done.14), channel_id=1, source_target_pairs={{0,16},{4,12},{8,24},{12,4},{16,0},{20,28},{24,8},{28,20},{1,17},{... | collective-permute-start | bytes 1572872 | tf_op jit(solution)/shard_map/turn_a2/ppermute | solution.py:22
  100.7 28.0 %collective-permute-start.25 = (bf16[2,64,3072]{2,1,0:T(8,128)(2,1)S(1)}, bf16[2,64,3072]{2,1,0:T(8,128)(2,1)S(1)}, u32[]{:S(2)}, u32[]{:S(2)}) collective-permute-start(bf16[2,64,3072]{2,1,0:T(8,128)(2,1)S(1)} %add_convert_fusion), channel_id=1, source_target_pairs={{0,8},{4,12},{8,0},{12,4},{1,9},{5,13},{9,1},{13,5},{2,10},{6,14},... | collective-permute-start | bytes 2359304 | tf_op jit(solution)/shard_map/grads1/ppermute | solution.py:22
  101.4 12.0 %collective-permute-start.20 = (bf16[256,1024]{1,0:T(8,128)(2,1)S(1)}, bf16[256,1024]{1,0:T(8,128)(2,1)S(1)}, u32[]{:S(2)}, u32[]{:S(2)}) collective-permute-start(bf16[256,1024]{1,0:T(8,128)(2,1)S(1)} %get-tuple-element.70), channel_id=1, source_target_pairs={{1,2},{2,1},{5,6},{6,5},{9,10},{10,9},{13,14},{14,13},{17,18},{18,... | collective-permute-start | bytes 1572872 | tf_op jit(solution)/shard_map/outer_in1/ppermute | solution.py:22
  102.1 26.6 %collective-permute-start.21 = (bf16[256,1024]{1,0:T(8,128)(2,1)S(1)}, bf16[256,1024]{1,0:T(8,128)(2,1)S(1)}, u32[]{:S(2)}, u32[]{:S(2)}) collective-permute-start(bf16[256,1024]{1,0:T(8,128)(2,1)S(1)} %collective-permute-done.19), channel_id=1, source_target_pairs={{1,0},{2,3},{5,4},{6,7},{9,8},{10,11},{13,12},{14,15},{17,16},{18,... | collective-permute-start | bytes 1572872 | tf_op jit(solution)/shard_map/outer_in_out0/ppermute | solution.py:22
  112.8 18.0 %collective-permute-start.31 = (bf16[1,64,3072]{2,1,0:T(8,128)(2,1)S(1)}, bf16[1,64,3072]{2,1,0:T(8,128)(2,1)S(1)}, u32[]{:S(2)}, u32[]{:S(2)}) collective-permute-start(bf16[1,64,3072]{2,1,0:T(8,128)(2,1)S(1)} %get-tuple-element.85), channel_id=1, source_target_pairs={{0,4},{4,0},{8,12},{12,8},{1,5},{5,1},{9,13},{13,9},{2,6},{6,2},{1... | collective-permute-start | bytes 1179656 | tf_op jit(solution)/shard_map/grads0_0/ppermute | solution.py:22
  112.8 19.2 %collective-permute-start.32 = (bf16[1,64,3072]{2,1,0:T(8,128)(2,1)S(1)}, bf16[1,64,3072]{2,1,0:T(8,128)(2,1)S(1)}, u32[]{:S(2)}, u32[]{:S(2)}) collective-permute-start(bf16[1,64,3072]{2,1,0:T(8,128)(2,1)S(1)} %get-tuple-element.86), channel_id=1, source_target_pairs={{0,4},{4,0},{8,12},{12,8},{1,5},{5,1},{9,13},{13,9},{2,6},{6,2},{1... | collective-permute-start | bytes 1179656 | tf_op jit(solution)/shard_map/grads0_1/ppermute | solution.py:22
  128.7 17.1 %collective-permute-start.27 = (bf16[512,1024]{1,0:T(8,128)(2,1)S(1)}, bf16[512,1024]{1,0:T(8,128)(2,1)S(1)}, u32[]{:S(2)}, u32[]{:S(2)}) collective-permute-start(bf16[512,1024]{1,0:T(8,128)(2,1)S(1)} %pad_maximum_fusion.refs_2_), channel_id=1, source_target_pairs={{0,4},{4,0},{8,12},{12,8},{16,20},{20,16},{24,28},{28,24},{1,5},{5... | collective-permute-start | bytes 3145736 | tf_op jit(solution)/shard_map/turn_c20/ppermute | solution.py:22
  128.7 17.1 %collective-permute-start.26 = (bf16[512,1024]{1,0:T(8,128)(2,1)S(1)}, bf16[512,1024]{1,0:T(8,128)(2,1)S(1)}, u32[]{:S(2)}, u32[]{:S(2)}) collective-permute-start(bf16[512,1024]{1,0:T(8,128)(2,1)S(1)} %pad_maximum_fusion.refs_2_), channel_id=1, source_target_pairs={{0,8},{4,20},{8,0},{12,28},{16,24},{20,4},{24,16},{28,12},{1,9},{5... | collective-permute-start | bytes 3145736 | tf_op jit(solution)/shard_map/turn_b2/ppermute | solution.py:22
  129.3 16.5 %collective-permute-start.30 = (bf16[256,1024]{1,0:T(8,128)(2,1)S(1)}, bf16[256,1024]{1,0:T(8,128)(2,1)S(1)}, u32[]{:S(2)}, u32[]{:S(2)}) collective-permute-start(bf16[256,1024]{1,0:T(8,128)(2,1)S(1)} %collective-permute-done.20), channel_id=1, source_target_pairs={{1,0},{2,3},{5,4},{6,7},{9,8},{10,11},{13,12},{14,15},{17,16},{18,... | collective-permute-start | bytes 1572872 | tf_op jit(solution)/shard_map/outer_in_out1/ppermute | solution.py:22
  134.7 15.9 %collective-permute-start.34 = (bf16[512,1024]{1,0:T(8,128)(2,1)S(1)}, bf16[512,1024]{1,0:T(8,128)(2,1)S(1)}, u32[]{:S(2)}, u32[]{:S(2)}) collective-permute-start(bf16[512,1024]{1,0:T(8,128)(2,1)S(1)} %constant_dynamic-update-slice_fusion.2.refs_4_), channel_id=1, source_target_pairs={{0,4},{4,0},{8,12},{12,8},{16,20},{20,16},{24,28},{28,24},{1,5},{5... | collective-permute-start | bytes 3145736 | tf_op jit(solution)/shard_map/turn_c30/ppermute | solution.py:22
  135.8 14.8 %collective-permute-start.35 = (bf16[512,1024]{1,0:T(8,128)(2,1)S(1)}, bf16[512,1024]{1,0:T(8,128)(2,1)S(1)}, u32[]{:S(2)}, u32[]{:S(2)}) collective-permute-start(bf16[512,1024]{1,0:T(8,128)(2,1)S(1)} %collective-permute-done.16.refs_5_), channel_id=1, source_target_pairs={{0,4},{4,0},{8,12},{12,8},{16,20},{20,16},{24,28},{28,24},{1,5},{5... | collective-permute-start | bytes 3145736 | tf_op jit(solution)/shard_map/turn_c31/ppermute | solution.py:22
  145.8 4.8 %collective-permute-start.33 = (bf16[512,1024]{1,0:T(8,128)(2,1)S(1)}, bf16[512,1024]{1,0:T(8,128)(2,1)S(1)}, u32[]{:S(2)}, u32[]{:S(2)}) collective-permute-start(bf16[512,1024]{1,0:T(8,128)(2,1)S(1)} %collective-permute-done.26.refs_3_), channel_id=1, source_target_pairs={{0,4},{4,0},{8,12},{12,8},{16,20},{20,16},{24,28},{28,24},{1,5},{5... | collective-permute-start | bytes 3145736 | tf_op jit(solution)/shard_map/turn_c21/ppermute | solution.py:22
  (11 other events, 136.0 us)
